TPU v7x, 32 devices: a whole 2x2x4 slice. The times are simulated.
32 devices in a mesh: dp: 4 (over y, x), seq: 8 (over z, core).
Axes of the slice: x: 2, y: 2, z: 4, core: 2. Of those that a mesh axis runs over, the one named last changes fastest.
Arguments:
- byte_ids: int32 [4, 4096], P('dp', 'seq'), may hold values from 0 to 255
- embedding: bfloat16 [256, 1024], replicated, may hold values from -6 to 6
- cotangent: bfloat16 [4, 4096, 1024], P('dp', 'seq'), may hold values from -6 to 6
- norm_gain: float32 [1024], replicated, may hold values from 0.5 to 1.5
- input_projection_weight: bfloat16 [1024, 4096], replicated, may hold values from -0.1875 to 0.1875
- conv_weight: float32 [4, 2048], replicated, may hold values from -3 to 3
- conv_bias: float32 [2048], replicated, may hold values from -3 to 3
- select_weight: bfloat16 [2048, 96], replicated, may hold values from -0.125 to 0.125
- step_weight: bfloat16 [64, 2048], replicated, may hold values from -0.75 to 0.75
- step_bias: float32 [2048], replicated, may hold values from -7 to -3
- decay_log: float32 [16, 2048], replicated, may hold values from -5 to 1
- skip_gain: float32 [2048], replicated, may hold values from 0.5 to 1.5
- output_projection_weight: bfloat16 [2048, 1024], replicated, may hold values from -0.5 to 0.5
Outputs:
- output: bfloat16 [4, 4096, 1024], P('dp', 'seq')
- d_inputs: float32 [4, 4096, 1024], P('dp', 'seq')
- d_embedding: float32 [256, 1024], replicated
- d_norm_gain: float32 [1024], replicated
- d_input_weight: float32 [1024, 4096], replicated
- d_conv_weight: float32 [4, 2048], replicated
- d_conv_bias: float32 [2048], replicated
- d_select_weight: float32 [2048, 96], replicated
- d_step_weight: float32 [64, 2048], replicated
- d_step_bias: float32 [2048], replicated
- d_decay_log: float32 [16, 2048], replicated
- d_skip_gain: float32 [2048], replicated
- d_output_weight: float32 [2048, 1024], replicated
All inputs are finite; a program needn't handle non-finite values.
Results may differ from a plain program's by a relative error of at most 0.0087.
The roundings to bfloat16 on the way count: a program that leaves them out, or rounds other values in their place, can miss the bound.
Values may be sent and summed in bfloat16 or wider, within the bound.
A program may use at most 192 MiB of HBM per device.

v0:
```python
import functools
import math

import jax
import jax.numpy as jnp
from jax import lax
from jax.experimental import pallas as pl
from jax.experimental.pallas import tpu as pltpu
from jax.sharding import PartitionSpec as P

EPS = 1e-05
LANES = 128
SUB = 8
LOG2E = math.log2(math.e)
LN2 = math.log(2.0)
F32 = jnp.float32
BF16 = jnp.bfloat16
MESH = pl.DeviceIdType.MESH


def passed_along(value, axis, by):
    peers = lax.axis_size(axis)
    pairs = [(i, i + by) for i in range(peers) if 0 <= i + by < peers]
    return lax.ppermute(value, axis, pairs)


def silu_slope(value):
    sigma = jax.nn.sigmoid(value)
    return sigma * (1.0 + value * (1.0 - sigma))


def contract_rows(left, right):
    return lax.dot_general(
        left, right, (((0,), (0,)), ((), ())), preferred_element_type=F32
    )


def contract_cols(left, right):
    return lax.dot_general(
        left, right, (((1,), (1,)), ((), ())), preferred_element_type=F32
    )


def to_spans(array):
    rows = array.shape[0]
    return array.reshape(SUB, rows // SUB, -1).swapaxes(0, 1).reshape(rows, -1)


def from_spans(array):
    rows = array.shape[0]
    return array.reshape(rows // SUB, SUB, -1).swapaxes(0, 1).reshape(rows, -1)


def sublane(shape):
    return lax.broadcasted_iota(jnp.int32, shape, len(shape) - 2)


def shift_up(value, by, fill, reverse):
    place = sublane(value.shape)
    if reverse:
        moved = pltpu.roll(value, SUB - by, value.ndim - 2)
        return jnp.where(place < SUB - by, moved, fill)
    moved = pltpu.roll(value, by, value.ndim - 2)
    return jnp.where(place >= by, moved, fill)


def expand_columns(select, first, states):
    width = select.shape[1]
    shape = (width, states * LANES)
    source = lax.broadcasted_iota(jnp.int32, shape, 0)
    target = lax.broadcasted_iota(jnp.int32, shape, 1) // LANES + first
    spread = (source == target).astype(F32).astype(BF16)
    return jnp.dot(select, spread, preferred_element_type=F32)


def tree_sum(value):
    while value.shape[0] > 1:
        half = value.shape[0] // 2
        value = value[:half] + value[half:]
    return value[0]


def early_chunks(inner, phases):
    slots = 2 * (inner // LANES)
    return min((slots - 4 - phases) // 2 + 1, inner // LANES) // 2 * 2


class Prefix:
    states = 16

    def __init__(self, totals, landing, start, incoming, gaps, rates, send_sem, recv_sem, rounds):
        self.totals, self.landing, self.start, self.incoming, self.gaps = totals, landing, start, incoming, gaps
        self.rates, self.send_sem, self.recv_sem, self.rounds = rates, send_sem, recv_sem, rounds

    def copy(self, e, r):
        return pltpu.make_async_remote_copy(
            src_ref=self.totals.at[e], dst_ref=self.landing.at[e, r],
            send_sem=self.send_sem.at[e, r], recv_sem=self.recv_sem.at[e, r],
            device_id=other("seq", 1 << r), device_id_type=MESH,
        )

    def advance(self, e, r):
        if r > 0:
            self.copy(e, r - 1).wait()
            self.merge(e, r - 1)
        if r < self.rounds:
            self.copy(e, r).start()

    def merge(self, e, r):
        n = self.rates.shape[1]
        rates = self.rates[e]
        later = bit_of(lax.axis_index("seq"), 1 << r) == 1
        end, message, total = self.totals[e, :n], self.totals[e, n : 2 * n], self.totals[e, 2 * n : 2 * n + 1]
        end2, message2 = self.landing[e, r, :n], self.landing[e, r, n : 2 * n]
        total2 = self.landing[e, r, 2 * n : 2 * n + 1]

        @pl.when(later)
        def _():
            gap = self.gaps[e, 0:1]
            self.start[e] = self.start[e] + jnp.exp2(gap * rates) * end2
            self.gaps[e, 0:1] = gap + total2

        @pl.when(jnp.logical_not(later))
        def _():
            gap = self.gaps[e, 1:2]
            self.incoming[e] = self.incoming[e] + jnp.exp2(gap * rates) * message2
            self.gaps[e, 1:2] = gap + total2

        if r < self.rounds - 1:
            reach, reach2 = jnp.exp2(total * rates), jnp.exp2(total2 * rates)
            self.totals[e, :n] = jnp.where(later, end + reach * end2, end2 + reach2 * end)
            self.totals[e, n : 2 * n] = jnp.where(later, message2 + reach2 * message, message + reach * message2)
            self.totals[e, 2 * n : 2 * n + 1] = total + total2


def scan_kernel(
    rank, states, chunk, rounds, seq,
    pre_ref, active_ref, gate_ref, graded_ref, select_ref, decay_ref, skip_ref, normed_ref, upstream_ref,
    gated_ref, dgate_ref, dprelow_ref, dactive_ref, drate_ref, dbias_ref, dskip_ref, dselect_ref,
    gate_sum, out_sum, gate_part, out_part,
    inject_scr, readout_scr, dread_scr, dinject_scr, state_scr, factor_scr,
    rates_scr, rate_scr, delta_scr, drive_scr, grad_scr, scan_scr, weight_scr,
    ahead_scr, behind_scr, sums_scr, gated_scr, dgated_scr,
    totals, totals_in, start_scr, incoming_scr, gaps_scr, prefix_send, prefix_recv,
    acc, out, landing, extra, send_sem, recv_sem, store_sem,
):
    rows = pre_ref.shape[0]
    steps = rows // SUB
    step = pl.program_id(0)
    tiles = pl.num_programs(0) // 2
    count = 2 * rates_scr.shape[0] // 2
    width = upstream_ref.shape[1]
    tile = lax.rem(step, tiles)
    prefix = Prefix(
        totals, totals_in, start_scr, incoming_scr, gaps_scr, rates_scr, prefix_send, prefix_recv, rounds
    )
    ex = Exchange(acc, out, landing, extra, send_sem, recv_sem, chunk, landing.shape[0], seq)
    early = early_chunks(count * LANES, ex.phases)
    half, unroll = states // 2, 8
    halves = [pl.ds(0, half), pl.ds(half, half)]

    def stores(k, kind):
        pair, final = k // 2, kind < 2
        at = pair - (0 if final else early // 2)
        source = (out if final else acc).at[k]
        copies = []
        if kind % 2 == 0:
            target = gate_sum if final else gate_part
            for side in range(2):
                lanes = pl.ds(pl.multiple_of(at * 2 * LANES + side * LANES, LANES), LANES)
                copies.append((source.at[pl.ds(side * width, width), :], target.at[:, lanes]))
        else:
            target = out_sum if final else out_part
            tall = pl.ds(pl.multiple_of(at * 2 * LANES, 2 * LANES), 2 * LANES)
            for b in range(width // LANES):
                copies.append((
                    source.at[pl.ds(b * 2 * LANES, 2 * LANES), :], target.at[tall, pl.ds(b * LANES, LANES)]
                ))
        for source, target in copies:
            pltpu.make_async_copy(source, target, store_sem.at[k]).start()

    def store(k):
        for kind in range(4):
            fits = (lax.rem(k, 2) == kind % 2) & ((k < early) if kind < 2 else (k >= early))

            @pl.when(fits)
            def _():
                stores(k, kind)

    @pl.when(step == 0)
    def _():
        for first, scr in ((rank, inject_scr), (rank + states, readout_scr)):
            wide = expand_columns(select_ref[...], first, states)
            for n in range(states):
                scr[:, n] = wide[:, n * LANES : (n + 1) * LANES].reshape(steps, SUB, LANES)
        dread_scr[...] = jnp.zeros_like(dread_scr)
        dinject_scr[...] = jnp.zeros_like(dinject_scr)
        start_scr[...] = jnp.zeros_like(start_scr)
        incoming_scr[...] = jnp.zeros_like(incoming_scr)
        gaps_scr[...] = jnp.zeros_like(gaps_scr)
        for e in range(count):
            rates_scr[e] = -jnp.exp(decay_ref[:, e * LANES : (e + 1) * LANES]) * LOG2E
        ex.greet()

    rates = rates_scr[tile]
    for n in range(states):
        rate_scr[n] = jnp.broadcast_to(rates[n : n + 1], (SUB, LANES))
    flat = lambda value: value.reshape(steps, SUB, LANES)
    active = active_ref[...].astype(F32)
    delta = jax.nn.softplus(pre_ref[...])
    delta_scr[...] = flat(delta)
    drive_scr[...] = flat(delta * active)
    gate = gate_ref[...].astype(F32)
    sigma = jax.nn.sigmoid(gate)
    grad_scr[...] = flat(graded_ref[...] * (gate * sigma))
    zero = jnp.zeros((half, SUB, LANES), F32)

    @pl.when(step < tiles)
    def _():
        total = jnp.sum(delta_scr[...], axis=0)
        sums_scr[tile] = total
        whole = jnp.sum(total, axis=0, keepdims=True)
        totals[tile, 2 * states :] = jnp.broadcast_to(whole, (SUB, LANES))
        for h, part in enumerate(halves):

            def ends(i, carry):
                state, message, decay = carry
                for u in range(unroll):
                    j = i * unroll + u
                    factor = jnp.exp2(delta_scr[j][None] * rate_scr[part])
                    state = factor * state + drive_scr[j][None] * inject_scr[j, part]
                    decay = decay * factor
                    message = message + decay * (grad_scr[j][None] * readout_scr[j, part])
                return state, message, decay

            state, message, decay = lax.fori_loop(0, steps // unroll, ends, (zero, zero, zero + 1.0))
            for value, kept, at, reverse in (
                (state, ahead_scr, h * half, False), (message, behind_scr, states + h * half, True)
            ):
                factor = decay
                for by in (1, 2, 4):
                    value = value + factor * shift_up(value, by, 0.0, reverse)
                    factor = factor * shift_up(factor, by, 1.0, reverse)
                kept[tile, part] = shift_up(value, 1, 0.0, reverse)
                last = 0 if reverse else SUB - 1
                for n in range(half):
                    totals[tile, at + n : at + n + 1] = value[n, last : last + 1]

    def spread(table):
        return jnp.concatenate(
            [jnp.broadcast_to(table[n : n + 1], (1, SUB, LANES)) for n in range(states)], axis=0
        )

    @pl.when(step >= tiles)
    def _():
        c = step - tiles
        total = sums_scr[tile]
        before, after = total, total
        for by in (1, 2, 4):
            before = before + shift_up(before, by, 0.0, False)
            after = after + shift_up(after, by, 0.0, True)
        before, after = before - total, after - total
        state_scr[0] = ahead_scr[tile] + jnp.exp2(before[None] * rate_scr[...]) * spread(start_scr[tile])

        def forward(i, state):
            for u in range(unroll // 2):
                j = i * (unroll // 2) + u
                factor = jnp.exp2(delta_scr[j][None] * rate_scr[...])
                factor_scr[j] = factor
                state = factor * state + drive_scr[j][None] * inject_scr[j]
                state_scr[j + 1] = state
                dread_scr[j] += grad_scr[j][None] * state
                scan_scr[j] = tree_sum(readout_scr[j] * state)
            return state

        lax.fori_loop(0, steps // (unroll // 2), forward, state_scr[0])
        for p in range(ex.phases - 1 + ex.phases % 2, 0, -2):
            k = c - (3 + p) // 2

            @pl.when((k >= 0) & (k < early))
            def _():
                ex.advance(k, p)
                if p == ex.phases:
                    store(k)

        active = active_ref[...].astype(F32)
        skip = skip_ref[...]
        gate = gate_ref[...].astype(F32)
        sigma = jax.nn.sigmoid(gate)
        graded = graded_ref[...]
        scanned = scan_scr[...].reshape(rows, LANES) + skip * active
        gated = (scanned * (gate * sigma)).astype(BF16)
        gated_ref[...] = gated
        dgate = (graded * scanned * (sigma * (1.0 + gate * (1.0 - sigma)))).astype(BF16)
        dgate_ref[...] = dgate
        dskip_ref[...] = jnp.sum(graded * (gate * sigma) * active, axis=0, keepdims=True)
        odd = lax.rem(c, 2)

        @pl.when(odd == 0)
        def _():
            gated_scr[:, :LANES] = gated
            dgated_scr[:, :LANES] = dgate

        @pl.when(odd == 1)
        def _():
            gated_scr[:, LANES:] = gated
            dgated_scr[:, LANES:] = dgate

        adjoint0 = behind_scr[tile] + jnp.exp2(after[None] * rate_scr[...]) * spread(incoming_scr[tile])
        state_scr[steps] = adjoint0
        for h, part in enumerate(halves):

            def backward(i, carry):
                adjoint, total = carry
                for u in range(unroll):
                    j = steps - 1 - (i * unroll + u)
                    d, g = delta_scr[j], grad_scr[j]
                    whole = adjoint + g[None] * readout_scr[j, part]
                    adjoint = factor_scr[j, part] * whole
                    through = adjoint * state_scr[j, part]
                    total = total + through * d[None]
                    dinject_scr[j, part] += whole * drive_scr[j][None]
                    one = tree_sum(through * rate_scr[part])
                    two = tree_sum(whole * inject_scr[j, part])
                    scan_scr[j] = scan_scr[j] + one if h else one
                    weight_scr[j] = weight_scr[j] + two if h else two
                return adjoint, total

            unused, total = lax.fori_loop(0, steps // unroll, backward, (state_scr[steps, part], zero))
            for n in range(half):
                at = h * half + n
                drate_ref[at : at + 1, :] = (
                    jnp.sum(total[n], axis=0, keepdims=True) * rate_scr[at, 0:1] * LN2
                )
        weight = weight_scr[...].reshape(rows, LANES)
        delta = delta_scr[...].reshape(rows, LANES)
        active = active_ref[...].astype(F32)
        dactive_ref[...] = delta * weight + skip_ref[...] * grad_scr[...].reshape(rows, LANES)
        dpre = (scan_scr[...].reshape(rows, LANES) * LN2 + active * weight) * jax.nn.sigmoid(pre_ref[...])
        dprelow_ref[...] = dpre.astype(BF16)
        dbias_ref[...] = jnp.sum(dpre, axis=0, keepdims=True)

        @pl.when(odd == 1)
        def _():
            pair = c // 2
            block = chunk // 8

            def gates(i, _):
                here = pl.ds(pl.multiple_of(i * block, block), block)
                part = jnp.dot(normed_ref[here, :], dgated_scr[...], preferred_element_type=F32).astype(BF16)
                acc[2 * pair, here, :] = part[:, :LANES]
                acc[2 * pair, pl.ds(pl.multiple_of(width + i * block, block), block), :] = part[:, LANES:]
                return 0

            lax.fori_loop(0, width // block, gates, 0)
            for b in range(width // (2 * LANES)):
                part = contract_rows(gated_scr[...], upstream_ref[:, b * 2 * LANES : (b + 1) * 2 * LANES]).astype(BF16)
                for side in range(2):
                    at = (2 * b + side) * 2 * LANES
                    acc[2 * pair + 1, at : at + 2 * LANES, :] = part[:, side * LANES : (side + 1) * LANES]

            @pl.when(2 * pair >= early)
            def _():
                store(2 * pair)
                store(2 * pair + 1)

    @pl.when(step >= tiles)
    def _():
        c = step - tiles
        for p in range(ex.phases - ex.phases % 2, -1, -2):
            k = c - 1 - p // 2

            @pl.when((k >= 0) & (k < early))
            def _():
                ex.advance(k, p)
                if p == ex.phases:
                    store(k)

    for r in range(rounds, -1, -1):
        e = step - 2 * r

        @pl.when((e >= 0) & (e < tiles))
        def _():
            prefix.advance(e, r)

    @pl.when(step == 2 * tiles - 1)
    def _():
        ones = jnp.ones((LANES, LANES), BF16)
        for first, scr in ((0, dinject_scr), (states, dread_scr)):
            for n in range(states):
                value = scr[:, n].reshape(rows, LANES)
                high = value.astype(BF16)
                low = (value - high.astype(F32)).astype(BF16)
                part = jnp.dot(high, ones, preferred_element_type=F32) + jnp.dot(
                    low, ones, preferred_element_type=F32
                )
                dselect_ref[:, first + n : first + n + 1] = part[:, first + n : first + n + 1]

        def done(k, _):
            pltpu.make_async_copy(acc.at[k], acc.at[k], store_sem.at[k]).wait()
            return 0

        lax.fori_loop(0, count, done, 0)


def run_scan(pre, active, gate, graded, select, decay_log, skip, normed, upstream, rank, seq):
    rows, inner = pre.shape
    states = decay_log.shape[0]
    width = upstream.shape[1]
    chunk = 2 * width
    tiles, steps = inner // LANES, rows // SUB
    rounds = seq.bit_length() - 1
    phases = 10 + max(rounds - 3, 0)
    early = early_chunks(inner, phases)
    first = early * LANES
    tall = pl.BlockSpec((rows, LANES), lambda i: (0, lax.rem(i, tiles)))
    line = pl.BlockSpec((1, LANES), lambda i: (0, lax.rem(i, tiles)))
    late = lambda shape: pl.BlockSpec(shape, lambda i: (0, lax.max(i - tiles, 0)))
    whole = lambda a: pl.BlockSpec(a.shape, lambda i: (0, 0), pipeline_mode=pl.Buffered(1))
    hbm = pl.BlockSpec(memory_space=pltpu.HBM)
    wide = pltpu.VMEM((steps, states, SUB, LANES), F32)
    thin = pltpu.VMEM((steps, SUB, LANES), F32)
    cube = pltpu.VMEM((tiles, states, SUB, LANES), F32)
    small = pltpu.VMEM((tiles, states, LANES), F32)
    pair = pltpu.VMEM((rows, 2 * LANES), BF16)
    buffers = scratch(tiles, chunk, early, seq)
    buffers[1] = pltpu.VMEM((early, chunk, LANES), BF16)
    return pl.pallas_call(
        functools.partial(scan_kernel, rank, states, chunk, rounds, seq),
        grid=(2 * tiles,),
        in_specs=[
            tall, tall, tall, tall, whole(select), whole(decay_log), line, whole(normed), whole(upstream),
        ],
        out_specs=[
            late((rows, LANES)), late((rows, LANES)), late((rows, LANES)), late((rows, LANES)),
            late((states, LANES)), late((1, LANES)), late((1, LANES)),
            pl.BlockSpec((rows, 2 * states), lambda i: (0, 0)), hbm, hbm, hbm, hbm,
        ],
        out_shape=[
            jax.ShapeDtypeStruct((rows, inner), BF16),
            jax.ShapeDtypeStruct((rows, inner), BF16),
            jax.ShapeDtypeStruct((rows, inner), BF16),
            jax.ShapeDtypeStruct((rows, inner), F32),
            jax.ShapeDtypeStruct((states, inner), F32),
            jax.ShapeDtypeStruct((1, inner), F32),
            jax.ShapeDtypeStruct((1, inner), F32),
            jax.ShapeDtypeStruct((rows, 2 * states), F32),
            jax.ShapeDtypeStruct((width, first), BF16),
            jax.ShapeDtypeStruct((first, width), BF16),
            jax.ShapeDtypeStruct((width, inner - first), BF16),
            jax.ShapeDtypeStruct((inner - first, width), BF16),
        ],
        scratch_shapes=[
            wide, wide, wide, wide,
            pltpu.VMEM((steps + 1, states, SUB, LANES), F32), wide,
            small, pltpu.VMEM((states, SUB, LANES), F32), thin, thin, thin, thin, thin,
            cube, cube, pltpu.VMEM((tiles, SUB, LANES), F32), pair, pair,
            pltpu.VMEM((tiles, 2 * states + SUB, LANES), F32),
            pltpu.VMEM((tiles, rounds, 2 * states + SUB, LANES), F32),
            small, small, pltpu.VMEM((tiles, SUB, LANES), F32),
            pltpu.SemaphoreType.DMA((tiles, rounds)), pltpu.SemaphoreType.DMA((tiles, rounds)),
        ]
        + buffers
        + [pltpu.SemaphoreType.DMA((tiles,))],
        compiler_params=pltpu.CompilerParams(
            collective_id=1, has_side_effects=True, vmem_limit_bytes=62 << 20
        ),
        name="span_scan",
    )(pre, active, gate, graded, select, decay_log, skip, normed, upstream)


def bit_of(index, step):
    return (index // step) % 2

def other(axis, step):
    place = lax.axis_index(axis)
    place = place + step * (1 - 2 * bit_of(place, step))
    if axis == "dp":
        return (place, lax.axis_index("seq"))
    return (lax.axis_index("dp"), place)

CORE, X, Y, Z, ZZ = ("seq", 1), ("dp", 1), ("dp", 2), ("seq", 2), ("seq", 4)

class Exchange:
    def __init__(self, acc, out, landing, extra, send_sem, recv_sem, rows, window, seq):
        self.acc, self.out, self.landing, self.extra = acc, out, landing, extra
        self.send_sem, self.recv_sem = send_sem, recv_sem
        self.rows, self.window = rows, window
        self.more = [("seq", step) for step in (8 << i for i in range(12)) if step < seq]
        self.orders = ((CORE, X, Y, Z, ZZ), (CORE, Y, X, Z, ZZ))
        self.halvings = 5
        self.phases = 2 * self.halvings + len(self.more)
        quarter = rows // 4
        core = bit_of(lax.axis_index("seq"), 1)
        self.core_base = core * (rows // 2)
        self.kept = []
        for s, order in enumerate(self.orders):
            base, size = core * (rows // 2) + s * quarter, quarter
            spans = [(base, size)]
            for axis, step in order[1:]:
                size = size // 2
                base = base + bit_of(lax.axis_index(axis), step) * size
                spans.append((base, size))
            self.kept.append(spans)

    def partners(self):
        return [other(*link) for link in (CORE, X, Y, Z, ZZ)] + [other(*link) for link in self.more]

    def greet(self):
        barrier = pltpu.get_barrier_semaphore()
        partners = self.partners()
        for device in partners:
            pl.semaphore_signal(barrier, inc=1, device_id=device, device_id_type=MESH)
        pl.semaphore_wait(barrier, len(partners))

    def sent(self, s, level):
        base, size = self.kept[s][level]
        axis, step = self.orders[s][level]
        before = self.kept[s][level - 1][0]
        mine = bit_of(lax.axis_index(axis), step)
        return before + (1 - mine) * size, size

    def span(self, ref, k, base, size):
        return ref.at[k, pl.ds(pl.multiple_of(base, 16), size), :]

    def copies(self, k, p):
        w = lax.rem(k, self.window)
        rows, levels, more = self.rows, self.halvings, len(self.more)
        out = []
        def copy(s, src, dst, link):
            return pltpu.make_async_remote_copy(
                src_ref=src, dst_ref=dst, send_sem=self.send_sem.at[w, p, s], recv_sem=self.recv_sem.at[w, p, s],
                device_id=other(*link), device_id_type=MESH)
        if p == 0:
            src = self.span(self.acc, k, rows // 2 - self.core_base, rows // 2)
            return [copy(0, src, self.landing.at[w, pl.ds(0, rows // 2), :], CORE)]
        if p == levels * 2 + more - 1:
            half = self.span(self.out, k, self.core_base, rows // 2)
            return [copy(0, half, half, CORE)]
        for s in range(2):
            if p < levels:
                base, size = self.sent(s, p)
                dst = self.landing.at[w, pl.ds(self.land(p, s), size), :]
                out.append(copy(s, self.span(self.acc, k, base, size), dst, self.orders[s][p]))
            elif p < levels + more:
                base, size = self.kept[s][-1]
                dst = self.extra.at[w, p - levels, pl.ds(s * size, size), :]
                out.append(copy(s, self.span(self.acc, k, base, size), dst, self.more[p - levels]))
            else:
                level = 2 * levels + more - 1 - p
                piece = self.span(self.out, k, *self.kept[s][level])
                out.append(copy(s, piece, piece, self.orders[s][level]))
        return out

    def land(self, p, s):
        size = self.rows // 4 >> p
        start = self.rows // 2 + sum(2 * (self.rows // 4 >> q) for q in range(1, p))
        return start + s * size

    def add(self, k, base, source, first, size, target):
        step = math.gcd(size, 128)
        w = lax.rem(k, self.window)
        def body(i, _):
            here = pl.ds(pl.multiple_of(base + i * step, 16), step)
            there = pl.ds(pl.multiple_of(first + i * step, 16), step)
            target[k, here, :] = (self.acc[k, here, :].astype(F32) + source(w, there).astype(F32)).astype(BF16)
            return 0
        lax.fori_loop(0, size // step, body, 0)

    def finish(self, k, p):
        for copy in self.copies(k, p):
            copy.wait()
        levels, more = self.halvings, len(self.more)
        target = self.out if p == levels + more - 1 else self.acc
        landed = lambda w, there: self.landing[w, there, :]
        if p == 0:
            self.add(k, self.core_base, landed, 0, self.rows // 2, self.acc)
        elif p < levels:
            for s in range(2):
                base, size = self.kept[s][p]
                self.add(k, base, landed, self.land(p, s), size, target)
        elif p < levels + more:
            for s in range(2):
                base, size = self.kept[s][-1]
                self.add(k, base, lambda w, there: self.extra[w, p - levels, there, :], s * size, size, target)

    def advance(self, k, p):
        if p > 0:
            self.finish(k, p - 1)
        if p < self.phases:
            for copy in self.copies(k, p):
                copy.start()

def scratch(chunks, rows, window, seq):
    more = len([1 for i in range(12) if (8 << i) < seq])
    phases = 10 + more
    return [
        pltpu.VMEM((chunks, rows, LANES), BF16),
        pltpu.VMEM((chunks, rows, LANES), BF16),
        pltpu.VMEM((window, rows, LANES), BF16),
        pltpu.VMEM((window, max(more, 1), rows // 32, LANES), BF16),
        pltpu.SemaphoreType.DMA((window, phases, 2)),
        pltpu.SemaphoreType.DMA((window, phases, 2)),
    ]

def blocks(shape, rows):
    height, width = shape
    pieces = []
    at = 0
    for b in range(width // LANES):
        r = 0
        while r < height:
            size = min(height - r, rows - at % rows)
            pieces.append((at // rows, r, b * LANES, at % rows, size))
            at += size
            r += size
    assert at % rows == 0
    return at // rows, pieces


def sum_kernel(rows, window, seq, shapes, gap, *refs):
    n = len(shapes)
    ins, outs = refs[:n], refs[n:2*n]
    acc, out, landing, extra, send_sem, recv_sem, load_sem, store_sem = refs[2 * n :]
    ex = Exchange(acc, out, landing, extra, send_sem, recv_sem, rows, window, seq)
    count = acc.shape[0]
    loads, stores = {}, {}
    first = 0
    for i, shape in enumerate(shapes):
        used, pieces = blocks(shape, rows)
        for j, (c, r, lane, at, size) in enumerate(pieces):
            hbm = lambda ref: ref.at[pl.ds(r, size), pl.ds(lane, LANES)]
            vm = acc.at[first + c, pl.ds(at, size), :]
            done = out.at[first + c, pl.ds(at, size), :]
            loads.setdefault(first + c, []).append(pltpu.make_async_copy(hbm(ins[i]), vm, load_sem.at[first + c]))
            stores.setdefault(first + c, []).append(pltpu.make_async_copy(done, hbm(outs[i]), store_sem.at[first + c]))
        first += used
    for c in range(count):
        for copy in loads[c]:
            copy.start()
    ex.greet()
    whole = lambda c, ref, sem: pltpu.make_async_copy(ref.at[c], ref.at[c], sem)
    def slot(t, _):
        for p in range(ex.phases, -1, -1):
            k = t - p * gap
            @pl.when((k >= 0) & (k < count))
            def _():
                if p == 0:
                    whole(k, acc, load_sem.at[k]).wait()
                ex.advance(k, p)
                if p == ex.phases:
                    for c in range(count):
                        @pl.when(k == c)
                        def _():
                            for copy in stores[c]:
                                copy.start()
        return 0
    lax.fori_loop(0, count + ex.phases * gap, slot, 0)
    def done(c, _):
        whole(c, out, store_sem.at[c]).wait()
        return 0
    lax.fori_loop(0, count, done, 0)

def sum_everywhere(arrays, seq, rows=2048, window=22, collective_id=0, gap=2):
    shapes = [a.shape for a in arrays]
    count = sum(blocks(s, rows)[0] for s in shapes)
    hbm = pl.BlockSpec(memory_space=pltpu.HBM)
    return pl.pallas_call(
        functools.partial(sum_kernel, rows, window, seq, shapes, gap),
        out_shape=[jax.ShapeDtypeStruct(s, BF16) for s in shapes],
        in_specs=[hbm] * len(arrays), out_specs=[hbm] * len(arrays),
        scratch_shapes=scratch(count, rows, window, seq) + [pltpu.SemaphoreType.DMA((count,)), pltpu.SemaphoreType.DMA((count,))],
        compiler_params=pltpu.CompilerParams(collective_id=collective_id, has_side_effects=True, vmem_limit_bytes=60 << 20),
        name="sum_everywhere",
    )(*arrays)


def on_device(
    byte_ids,
    embedding,
    cotangent,
    norm_gain,
    input_projection_weight,
    conv_weight,
    conv_bias,
    select_weight,
    step_weight,
    step_bias,
    decay_log,
    skip_gain,
    output_projection_weight,
):
    count, stretch = byte_ids.shape
    vocab, width = embedding.shape
    kernel, inner = conv_weight.shape
    states = decay_log.shape[0]
    rank = step_weight.shape[0]
    rows = count * stretch
    halo = kernel - 1
    ids = to_spans(byte_ids.reshape(rows, 1))
    one_hot = ids == jnp.arange(vocab, dtype=jnp.int32)[None, :]
    block_inputs = jnp.dot(one_hot.astype(BF16), embedding, preferred_element_type=F32)
    scale = lax.rsqrt(jnp.mean(block_inputs * block_inputs, axis=1, keepdims=True) + EPS)
    normed_input = (block_inputs * scale * norm_gain).astype(BF16)
    front = jnp.dot(
        normed_input, input_projection_weight[:, :inner], preferred_element_type=F32
    ).astype(BF16)
    gate = jnp.dot(
        normed_input, input_projection_weight[:, inner:], preferred_element_type=F32
    ).astype(BF16)
    last = front[rows - halo * SUB :].reshape(halo, SUB, inner)
    tail = passed_along(last[:, SUB - 1], "seq", 1)
    earlier = jnp.concatenate([tail[:, None], last[:, : SUB - 1]], axis=1)
    extended = jnp.concatenate([earlier.reshape(halo * SUB, inner), front], axis=0).astype(F32)
    mixed = conv_bias + conv_weight[0] * extended[:rows]
    for place in range(1, kernel):
        mixed = mixed + conv_weight[place] * extended[place * SUB : place * SUB + rows]
    active = jax.nn.silu(mixed).astype(BF16)
    select = jnp.dot(active, select_weight, preferred_element_type=F32).astype(BF16)
    lowrank = select[:, :rank]
    pre = jnp.dot(lowrank, step_weight, preferred_element_type=F32) + step_bias
    upstream = to_spans(cotangent.reshape(rows, width))
    graded = contract_cols(upstream, output_projection_weight)
    (
        gated, d_gate, d_pre_low, d_active, d_decay_log, d_step_bias, d_skip_gain, d_pair,
        gate_sum, out_sum, gate_part, out_part,
    ) = run_scan(
        pre, active, gate, graded, select, decay_log, skip_gain.reshape(1, inner),
        normed_input.T, upstream, rank, lax.axis_size("seq"),
    )

    result = block_inputs + jnp.dot(gated, output_projection_weight, preferred_element_type=F32)
    output = from_spans(result.astype(BF16)).reshape(count, stretch, width)
    d_step_weight = contract_rows(lowrank, d_pre_low)
    d_lowrank = contract_cols(d_pre_low, step_weight)
    d_select = jnp.concatenate([d_lowrank, d_pair], axis=1).astype(BF16)
    d_select_weight = contract_rows(active, d_select)
    d_mixed = (d_active + contract_cols(d_select, select_weight)) * silu_slope(mixed)
    d_conv_bias = jnp.sum(d_mixed, axis=0)
    d_conv_weight = jnp.stack(
        [
            jnp.sum(d_mixed * extended[place * SUB : place * SUB + rows], axis=0)
            for place in range(kernel)
        ]
    )
    first = d_mixed[: halo * SUB].reshape(halo, SUB, inner)
    after = passed_along(first[:, 0], "seq", -1)
    later = jnp.concatenate([first[:, 1:], after[:, None]], axis=1)
    spread = jnp.concatenate([d_mixed, later.reshape(halo * SUB, inner)], axis=0)
    d_front = conv_weight[halo] * spread[:rows]
    for place in range(1, kernel):
        d_front = d_front + conv_weight[halo - place] * spread[place * SUB : place * SUB + rows]
    d_front = d_front.astype(BF16)
    d_both = jnp.concatenate([d_front, d_gate], axis=1)
    d_front_weight = contract_rows(normed_input, d_front)
    d_normed = contract_cols(d_both, input_projection_weight)
    d_norm_gain = jnp.sum(d_normed * block_inputs * scale, axis=0)
    scaled = norm_gain * d_normed
    cubed = scale * scale * scale
    d_inputs = (
        upstream.astype(F32)
        + scale * scaled
        - block_inputs * cubed * jnp.mean(scaled * block_inputs, axis=1, keepdims=True)
    )
    high = d_inputs.astype(BF16)
    low = (d_inputs - high.astype(F32)).astype(BF16)
    hot = one_hot.astype(BF16)
    d_embedding = contract_rows(hot, high) + contract_rows(hot, low)
    small = (
        d_norm_gain,
        d_conv_weight,
        d_conv_bias,
        d_select_weight,
        d_step_weight,
        d_step_bias,
        d_decay_log,
        d_skip_gain,
    )
    flat = jnp.concatenate([part.astype(BF16).reshape(-1) for part in small])
    unit = 2048 * LANES
    flat = jnp.pad(flat, (0, -flat.size % unit)).reshape(-1, LANES)
    front_sum, gate_rest, out_rest, embedding_sum, flat = sum_everywhere(
        [d_front_weight.astype(BF16), gate_part, out_part, d_embedding.astype(BF16), flat], lax.axis_size("seq")
    )
    d_input_sum = jnp.concatenate([front_sum, gate_sum, gate_rest], axis=1).astype(F32)
    d_output_sum = jnp.concatenate([out_sum, out_rest], axis=0).astype(F32)
    d_embedding_sum = embedding_sum.astype(F32)
    flat = flat.astype(F32)
    flat = flat.reshape(-1)
    sums, at = [], 0
    shapes = [norm_gain, conv_weight, conv_bias, select_weight, step_weight, step_bias, decay_log, skip_gain]
    for like in shapes:
        sums.append(flat[at : at + like.size].reshape(like.shape))
        at += like.size
    return (
        output,
        from_spans(d_inputs).reshape(count, stretch, width),
        d_embedding_sum,
        sums[0],
        d_input_sum,
        sums[1],
        sums[2],
        sums[3],
        sums[4],
        sums[5],
        sums[6],
        sums[7],
        d_output_sum,
    )


def solution(mesh):
    placed = (P("dp", "seq"), P(), P("dp", "seq", None)) + (P(),) * 10
    return jax.shard_map(
        on_device,
        mesh=mesh,
        in_specs=placed,
        out_specs=(P("dp", "seq", None), P("dp", "seq", None)) + (P(),) * 11,
        check_vma=False,
    )
```

profile of v0, /device:TPU:0, one launch (start us, length us, event | category | flops | bytes accessed | tf_op | source)
XLA Modules:
  0.0 376.0 jit_solution(7579223889842449583)
XLA Ops:
  1.2 1.3 reduce.7
  4.0 1.1 multiply_convert_fusion.1
  5.1 5.2 %fusion.17 = bf16[512,2048]{1,0:T(8,128)(2,1)S(1)} fusion(bf16[512,1024]{1,0:T(8,128)(2,1)S(1)} %multiply_convert_fusion.1, bf16[1024,4096]{1,0:T(8,128)(2,1)} %param.17), kind=kOutput, calls=%fused_computation.34 | convolution fusion | flops 2148532224 | bytes 7340032 | tf_op jit(solution)/shard_map/dot_general | solution.py:705
  10.4 1.2 copy-done.14
  11.6 2.6 collective-permute-start
  14.3 3.7 fusion.20.gate_ref
  18.0 4.5 %fusion.38.graded_ref = f32[512,2048]{1,0:T(8,128)} fusion(bf16[2048,1024]{1,0:T(8,128)(2,1)S(1)} %copy-done.40, bf16[8,64,1024]{2,1,0:T(8,128)(2,1)S(1)} %bitcast.81), kind=kOutput, calls=%fused_computation.93 | convolution fusion | flops 2147483648 | bytes 9437184 | tf_op jit(solution)/shard_map/dot_general | solution.py:39
  22.8 1.5 copy.59
  24.3 1.5 copy.40.normed_ref
  25.9 2.1 maximum_convert_fusion.2
  28.1 3.7 multiply_convert_fusion
  31.8 1.3 copy-done.7
  33.1 0.7 convolution_convert_fusion.3.select_ref
  33.9 2.7 convolution_add_fusion.pre_ref
  36.5 158.2 %span_scan.1 = (bf16[512,2048]{1,0:T(8,128)(2,1)}, bf16[512,2048]{1,0:T(8,128)(2,1)}, bf16[512,2048]{1,0:T(8,128)(2,1)}, f32[512,2048]{1,0:T(8,128)}, f32[16,204...) custom-call(f32[512,2048]{1,0:T(8,128)} %convolution_add_fusion.pre_, ...), custom_call_target="tpu_custom_call" | custom-call | tf_op jit(solution)/shard_map/span_scan/pallas_call | solution.py:428
  194.8 2.5 convolution_convert_fusion.4
  197.3 2.2 fusion.25
  199.5 5.6 %fusion.23 = bf16[8,64,1024]{2,0,1:T(8,128)(2,1)} fusion(f32[512,1024]{1,0:T(8,128)S(1)} %copy-done.4, bf16[512,2048]{1,0:T(8,128)(2,1)S(1)} %copy-done.42, bf16[2048,1024]{1,0:T(8,128)(2,1)} %param.25), kind=kOutput, calls=%fused_computation.46 | convolution fusion | flops 2148532224 | bytes 9437184 | tf_op jit(solution)/shard_map/dot_general | solution.py:732
  205.2 2.1 convolution_convert_fusion.1
  207.3 5.2 %multiply_multiply_fusion = f32[512,2048]{1,0:T(8,128)S(1)} fusion(f32[512,2048]{1,0:T(8,128)} %get-tuple-element.81, f32[512,2048]{1,0:T(8,128)} %get-tuple-element.31, bf16[2048,96]{0,1:T(8,128)(2,1)S(1)} %copy-done.43, bf16[512,32]{0,1:T(8,128)(2,1)S(1)} %copy.42, bf16[512,64]{0,1:T(8,128)(2,1)S(1)} %convolution_convert_fusion.4), kind=kOutput, calls=%fused_computation.24 | convolution fusion | flops 210960384 | bytes 13074432 | tf_op jit(solution)/shard_map/dot_general | solution.py:39
  212.6 2.0 copy-done.8
  215.2 1.3 collective-permute-start.1
  217.2 1.5 copy.41
  219.1 0.7 reshape.127
  219.8 0.8 broadcast_in_dim.5
  220.7 14.1 %multiply_reduce_fusion.3 = (bf16[2048]{0:T(1024)(128)(2,1)S(1)}, bf16[2048]{0:T(1024)(128)(2,1)S(1)}, bf16[2048]{0:T(1024)(128)(2,1)S(1)}, bf16[2048]{0:T(1024)...) fusion(f32[512,2048]{1,0:T(8,128)} %copy-done.8, f32[536,2048]{1,0:T(8,128)} %copy-done.2, ...), kind=kLoop, calls=%fused_computation.23 | loop fusion | flops 20961280 | bytes 23318528 | tf_op jit(solution)/shard_map/reduce_sum | solution.py:742
  234.9 4.4 %convolution_convert_fusion.refs_0_ = bf16[1024,2048]{1,0:T(8,128)(2,1)} fusion(bf16[512,1024]{1,0:T(8,128)(2,1)S(1)} %copy-done.20, bf16[512,2048]{1,0:T(8,128)(2,1)S(1)} %get-tuple-element.82), kind=kOutput, calls=%fused_computation.32 | convolution fusion | flops 2149580800 | bytes 7340032 | tf_op jit(solution)/shard_map/dot_general | solution.py:33
  239.3 8.3 %multiply_reduce_fusion.4 = (bf16[1024]{0:T(1024)(128)(2,1)S(1)}, f32[512]{0:T(512)S(1)}, f32[512,1024]{1,0:T(8,128)S(1)}) fusion(f32[512,1024]{1,0:T(8,128)S(1)} %copy-done.4, f32[512]{0:T(512)S(1)} %copy-done.32, f32[1024]{0:T(1024)S(1)} %copy-done.27, bf16[1024,4096]{1,0:T(8,128)(2,1)} %param.17, bf16[512,2048]{1,0:T(8,128)(2,1)S(1)} %copy-done.41, ...), kind=kOutput, calls=%fused_computation.39 | convolution fusion | flops 4306500096 | bytes 16787456 | tf_op jit(solution)/shard_map/dot_general | solution.py:39
  247.9 1.0 pad_bitcast_fusion.refs_4_
  249.0 0.9 multiply_subtract_fusion
  250.5 0.7 copy-done.5
  251.3 1.4 fusion.24.refs_3_
  252.6 91.8 %sum_everywhere.1 = (bf16[1024,2048]{1,0:T(8,128)(2,1)}, bf16[1024,768]{1,0:T(8,128)(2,1)}, bf16[768,1024]{1,0:T(8,128)(2,1)}, bf16[256,1024]{1,0:T(8,128)(2,1)}, bf16[4096,128]{1,0:T(8,128)(2,1)}) custom-call(bf16[1024,2048]{1,0:T(8,128)(2,1)} %convolution_convert_fusion.refs_0_, bf16[1024,768]{1,0:T(8,128)(2,1)} %get-tuple-element.35.refs_1_, ...), custom_call_target="tpu_custom_call" | custom-call | tf_op jit(solution)/shard_map/sum_everywhere/pallas_call | solution.py:668
  344.4 1.3 slice.156
  345.8 0.8 slice.161
  346.6 1.0 slice.159
  347.6 1.0 slice.158
  348.7 1.5 convert_element_type.113
  351.4 1.4 reshape.133
  352.8 0.7 reshape.136
  353.4 2.1 convert_element_type.112
  355.6 0.9 reshape.135
  356.4 1.2 reshape.134
  357.7 2.4 copy.46
  360.1 2.5 copy.44
  362.7 5.4 %maximum_convert_fusion.1 = f32[2048,1024]{1,0:T(8,128)} fusion(bf16[768,1024]{1,0:T(8,128)(2,1)S(1)} %copy-done.16, bf16[1280,1024]{1,0:T(8,128)(2,1)S(1)} %copy-done.13), kind=kLoop, calls=%fused_computation.19 | loop fusion | flops 8388608 | bytes 12582912 | tf_op jit(solution)/shard_map/convert_element_type | solution.py:786
  368.1 1.0 copy-done.15
  369.1 6.4 %maximum_convert_fusion = f32[1024,4096]{1,0:T(8,128)} fusion(bf16[1024,768]{1,0:T(8,128)(2,1)S(1)} %copy-done.15, bf16[1024,1280]{1,0:T(8,128)(2,1)S(1)} %copy-done.12, bf16[1024,2048]{1,0:T(8,128)(2,1)S(1)} %copy-done.11), kind=kLoop, calls=%fused_computation | loop fusion | flops 25165824 | bytes 25165824 | tf_op jit(solution)/shard_map/convert_element_type | solution.py:785
  (133 shorter events, 6.3 us)
Async XLA Ops:
  0.6 2.1 copy-start
  2.8 7.5 %copy-start.29 = (s32[512]{0:T(512)}, s32[512]{0:T(512)S(1)}, u32[]{:S(2)}) copy-start(s32[512]{0:T(512)S(1)} %eq.15) | copy-start | bytes 6148
  3.4 19.2 %copy-start.3 = (f32[512,1024]{1,0:T(8,128)}, f32[512,1024]{1,0:T(8,128)S(1)}, u32[]{:S(2)}) copy-start(f32[512,1024]{1,0:T(8,128)S(1)} %get-tuple-element.93) | copy-start | bytes 6291460
  4.0 18.5 %copy-start.31 = (f32[512]{0:T(512)}, f32[512]{0:T(512)S(1)}, u32[]{:S(2)}) copy-start(f32[512]{0:T(512)S(1)} %get-tuple-element.91) | copy-start | bytes 6148
  4.0 10.3 %slice-start = ((s8[8388608]{0:T(1024)(128)(4,1)}), s8[4194304]{0:T(1024)(128)(4,1)S(1)}, s32[]{:S(2)}) async-start(s8[8388608]{0:T(1024)(128)(4,1)} %bitcast.103), calls=%async_computation | async-start | bytes 8388608
  5.1 9.2 %copy-start.19 = (bf16[512,1024]{1,0:T(8,128)(2,1)}, bf16[512,1024]{1,0:T(8,128)(2,1)S(1)}, u32[]{:S(2)}) copy-start(bf16[512,1024]{1,0:T(8,128)(2,1)S(1)} %multiply_convert_fusion.1) | copy-start | bytes 3145732
  5.1 9.2 %slice-start.1 = ((s8[8388608]{0:T(1024)(128)(4,1)}), s8[4194304]{0:T(1024)(128)(4,1)S(1)}, s32[]{:S(2)}) async-start(s8[8388608]{0:T(1024)(128)(4,1)} %bitcast.103), calls=%async_computation.1 | async-start | bytes 8388608
  10.3 1.3 copy-start.14
  11.6 6.3 %copy-start.28 = (f32[4,2048]{1,0:T(4,128)S(1)}, f32[4,2048]{1,0:T(4,128)}, u32[]{:S(2)}) copy-start(f32[4,2048]{1,0:T(4,128)} %param.18) | copy-start | bytes 98308
  11.6 6.4 %copy-start.9 = (bf16[1,512,1024]{2,1,0:T(8,128)(2,1)S(1)}, bf16[1,512,1024]{2,1,0:T(8,128)(2,1)}, u32[]{:S(2)}) copy-start(bf16[1,512,1024]{2,1,0:T(8,128)(2,1)} %param.15) | copy-start | bytes 3145732
  11.6 6.4 %copy-start.40 = (bf16[2048,1024]{1,0:T(8,128)(2,1)S(1)}, bf16[2048,1024]{1,0:T(8,128)(2,1)}, u32[]{:S(2)}) copy-start(bf16[2048,1024]{1,0:T(8,128)(2,1)} %param.25) | copy-start | bytes 12582916
  11.6 14.2 %collective-permute-start = (bf16[3,2048]{1,0:T(4,128)(2,1)S(1)}, bf16[3,2048]{1,0:T(4,128)(2,1)S(1)}, u32[]{:S(2)}, u32[]{:S(2)}) collective-permute-start(bf16[3,2048]{1,0:T(4,128)(2,1)S(1)} %bitcast.100), channel_id=1, source_target_pairs={{0,1},{1,2},{2,3},{3,4},{4,5},{5,6},{6,7},{8,9},{9,10},{10,11},{11... | collective-permute-start | bytes 36872 | tf_op jit(solution)/shard_map/ppermute | solution.py:24
  18.0 10.1 %copy-start.24 = (f32[1,2048]{1,0:T(1,128)}, f32[1,2048]{1,0:T(1,128)S(1)}, u32[]{:S(2)}) copy-start(f32[1,2048]{1,0:T(1,128)S(1)} %get-tuple-element.88) | copy-start | bytes 24580
  18.0 10.1 %copy-start.25 = (f32[1,2048]{1,0:T(1,128)}, f32[1,2048]{1,0:T(1,128)S(1)}, u32[]{:S(2)}) copy-start(f32[1,2048]{1,0:T(1,128)S(1)} %get-tuple-element.89) | copy-start | bytes 24580
  18.0 4.5 %copy-start.26 = (f32[1024]{0:T(1024)S(1)}, f32[1024]{0:T(1024)}, u32[]{:S(2)}) copy-start(f32[1024]{0:T(1024)} %param.16) | copy-start | bytes 12292
  24.3 3.7 copy-start.35
  28.0 3.8 %copy-start.2 = (f32[536,2048]{1,0:T(8,128)}, f32[536,2048]{1,0:T(8,128)S(1)}, u32[]{:S(2)}) copy-start(f32[536,2048]{1,0:T(8,128)S(1)} %maximum_convert_fusion.2) | copy-start | bytes 13172740
  28.1 5.1 %copy-start.43 = (bf16[2048,96]{0,1:T(8,128)(2,1)S(1)}, bf16[2048,96]{0,1:T(8,128)(2,1)}, u32[]{:S(2)}) copy-start(bf16[2048,96]{0,1:T(8,128)(2,1)} %param.20) | copy-start | bytes 1179652
  28.1 5.8 %copy-start.18 = (bf16[64,2048]{1,0:T(8,128)(2,1)S(1)}, bf16[64,2048]{1,0:T(8,128)(2,1)}, u32[]{:S(2)}) copy-start(bf16[64,2048]{1,0:T(8,128)(2,1)} %param.21) | copy-start | bytes 786436
  28.1 5.8 %copy-start.36 = (f32[2048]{0:T(1024)S(1)}, f32[2048]{0:T(1024)}, u32[]{:S(2)}) copy-start(f32[2048]{0:T(1024)} %param.22) | copy-start | bytes 24580
  31.8 1.3 copy-start.7
  33.9 2.7 copy-start.17
  194.7 4.7 %copy-start.4 = (f32[512,1024]{1,0:T(8,128)S(1)}, f32[512,1024]{1,0:T(8,128)}, u32[]{:S(2)}) copy-start(f32[512,1024]{1,0:T(8,128)} %copy-done.3) | copy-start | bytes 6291460
  194.7 4.7 %copy-start.42 = (bf16[512,2048]{1,0:T(8,128)(2,1)S(1)}, bf16[512,2048]{1,0:T(8,128)(2,1)}, u32[]{:S(2)}) copy-start(bf16[512,2048]{1,0:T(8,128)(2,1)} %get-tuple-element.30) | copy-start | bytes 6291460
  199.5 5.6 %copy-start.23 = (f32[16,2048]{1,0:T(8,128)S(1)}, f32[16,2048]{1,0:T(8,128)}, u32[]{:S(2)}) copy-start(f32[16,2048]{1,0:T(8,128)} %get-tuple-element.38) | copy-start | bytes 393220
  199.5 5.6 %copy-start.22 = (f32[512,32]{1,0:T(8,128)S(1)}, f32[512,32]{1,0:T(8,128)}, u32[]{:S(2)}) copy-start(f32[512,32]{1,0:T(8,128)} %get-tuple-element.33) | copy-start | bytes 196612
  207.3 9.2 %copy-start.38 = (f32[1,2048]{1,0:T(1,128)S(1)}, f32[1,2048]{1,0:T(1,128)}, u32[]{:S(2)}) copy-start(f32[1,2048]{1,0:T(1,128)} %get-tuple-element.37) | copy-start | bytes 24580
  207.3 9.2 %copy-start.39 = (f32[1,2048]{1,0:T(1,128)S(1)}, f32[1,2048]{1,0:T(1,128)}, u32[]{:S(2)}) copy-start(f32[1,2048]{1,0:T(1,128)} %get-tuple-element.39) | copy-start | bytes 24580
  207.3 9.9 %copy-start.21 = (bf16[8,64,1024]{2,0,1:T(8,128)(2,1)S(1)}, bf16[8,64,1024]{2,0,1:T(8,128)(2,1)}, u32[]{:S(2)}) copy-start(bf16[8,64,1024]{2,0,1:T(8,128)(2,1)} %fusion.23) | copy-start | bytes 3145732
  212.5 2.0 copy-start.8
  215.2 4.6 %collective-permute-start.1 = (f32[3,2048]{1,0:T(4,128)}, f32[3,2048]{1,0:T(4,128)}, u32[]{:S(2)}, u32[]{:S(2)}) collective-permute-start(f32[3,2048]{1,0:T(4,128)} %bitcast.77), channel_id=1, source_target_pairs={{1,0},{2,1},{3,2},{4,3},{5,4},{6,5},{7,6},{9,8},{10,9},{11,10},{12... | collective-permute-start | bytes 73736 | tf_op jit(solution)/shard_map/ppermute | solution.py:24
  220.7 14.2 %copy-start.20 = (bf16[512,1024]{1,0:T(8,128)(2,1)S(1)}, bf16[512,1024]{1,0:T(8,128)(2,1)}, u32[]{:S(2)}) copy-start(bf16[512,1024]{1,0:T(8,128)(2,1)} %copy-done.19) | copy-start | bytes 3145732
  234.8 4.5 %copy-start.27 = (f32[1024]{0:T(1024)S(1)}, f32[1024]{0:T(1024)}, u32[]{:S(2)}) copy-start(f32[1024]{0:T(1024)} %param.16) | copy-start | bytes 12292
  234.8 4.5 %copy-start.32 = (f32[512]{0:T(512)S(1)}, f32[512]{0:T(512)}, u32[]{:S(2)}) copy-start(f32[512]{0:T(512)} %copy-done.31) | copy-start | bytes 6148
  234.9 4.4 %copy-start.41 = (bf16[512,2048]{1,0:T(8,128)(2,1)S(1)}, bf16[512,2048]{1,0:T(8,128)(2,1)}, u32[]{:S(2)}) copy-start(bf16[512,2048]{1,0:T(8,128)(2,1)} %get-tuple-element.34) | copy-start | bytes 6291460
  239.3 8.6 %copy-start.34 = (bf16[2048]{0:T(1024)(128)(2,1)S(1)}, bf16[2048]{0:T(1024)(128)(2,1)}, u32[]{:S(2)}) copy-start(bf16[2048]{0:T(1024)(128)(2,1)} %get-tuple-element.96) | copy-start | bytes 12292
  239.3 8.6 %copy-start.33 = (bf16[2048]{0:T(1024)(128)(2,1)S(1)}, bf16[2048]{0:T(1024)(128)(2,1)}, u32[]{:S(2)}) copy-start(bf16[2048]{0:T(1024)(128)(2,1)} %get-tuple-element.95) | copy-start | bytes 12292
  239.3 9.6 %copy-start.10 = (bf16[1,512,1024]{2,1,0:T(8,128)(2,1)S(1)}, bf16[1,512,1024]{2,1,0:T(8,128)(2,1)}, u32[]{:S(2)}) copy-start(bf16[1,512,1024]{2,1,0:T(8,128)(2,1)} %param.15) | copy-start | bytes 3145732
  239.3 9.6 %copy-start.37 = (f32[512]{0:T(512)S(1)}, f32[512]{0:T(512)}, u32[]{:S(2)}) copy-start(f32[512]{0:T(512)} %get-tuple-element.90) | copy-start | bytes 6148
  247.9 2.0 copy-start.30
  249.9 1.3 copy-start.5
  348.7 11.5 %copy-start.6 = (f32[512,1024]{1,0:T(8,128)S(1)}, f32[512,1024]{1,0:T(8,128)}, u32[]{:S(2)}) copy-start(f32[512,1024]{1,0:T(8,128)} %copy-done.5) | copy-start | bytes 6291460
  360.1 2.5 copy-start.13
  360.1 2.5 copy-start.16
  362.7 5.4 %copy-start.11 = (bf16[1024,2048]{1,0:T(8,128)(2,1)S(1)}, bf16[1024,2048]{1,0:T(8,128)(2,1)}, u32[]{:S(2)}) copy-start(bf16[1024,2048]{1,0:T(8,128)(2,1)} %get-tuple-element.42) | copy-start | bytes 12582916
  362.7 5.4 %copy-start.12 = (bf16[1024,1280]{1,0:T(8,128)(2,1)S(1)}, bf16[1024,1280]{1,0:T(8,128)(2,1)}, u32[]{:S(2)}) copy-start(bf16[1024,1280]{1,0:T(8,128)(2,1)} %get-tuple-element.43) | copy-start | bytes 7864324
  362.7 6.4 %copy-start.15 = (bf16[1024,768]{1,0:T(8,128)(2,1)S(1)}, bf16[1024,768]{1,0:T(8,128)(2,1)}, u32[]{:S(2)}) copy-start(bf16[1024,768]{1,0:T(8,128)(2,1)} %get-tuple-element.44) | copy-start | bytes 4718596
  369.1 6.4 %copy-start.1 = (bf16[256,1024]{1,0:T(8,128)(2,1)S(1)}, bf16[256,1024]{1,0:T(8,128)(2,1)}, u32[]{:S(2)}) copy-start(bf16[256,1024]{1,0:T(8,128)(2,1)} %param.14) | copy-start | bytes 1572868
where the time goes:
time: 382 us; the launch traced here: 376 us
  Pallas kernels  250 us (65%)
  matrix products  49.5 us (13%)
  other arithmetic  40.4 us (11%)
  local copies, waits for them, and re-layouts  30.2 us (8%)
  starting transfers between devices  3.89 us (1%)
    pallas_call x1, Pallas kernels, run_scan(): pl.pallas_call(functools.partial(scan_kernel, rank, states, chunk, rounds...  158 us
    pallas_call x1, Pallas kernels, sum_everywhere(): pl.pallas_call(functools.partial(sum_kernel, rows, window, seq, shapes, g...  91.8 us
    dot_general x4, matrix products, contract_cols(): lax.dot_general(left, right, (((1,), (1,)), ((), ())), preferred_element_...  20.5 us
    reduce_sum x1, other arithmetic, on_device(): jnp.sum(d_mixed * extended[place * SUB:place * SUB + rows], axis=0)  14.1 us
    dot_general x5, matrix products, contract_rows(): lax.dot_general(left, right, (((0,), (0,)), ((), ())), preferred_element_...  10.6 us
    unnamed x106, local copies, waits for them, and re-layouts  10.2 us
  transfers between devices with their start and end apart: 2, of which 0 were waited for; matrix products, arithmetic and copies ran while one was open for 4% of the time, Pallas kernels for 0%

commit v1 on v0

--- a/solution.py
+++ b/solution.py
@@ -80,14 +80,23 @@
     return value[0]
 
 
-def early_chunks(inner, phases):
-    slots = 2 * (inner // LANES)
-    return min((slots - 4 - phases) // 2 + 1, inner // LANES) // 2 * 2
+def slot_of(k, p):
+    return 3 * k + 5 + 2 * p
+
+
+def turns(phases, place):
+    return [(p, (place - 5 - 2 * p) // 3) for p in range(phases, -1, -1) if (place - 5 - 2 * p) % 3 == 0]
+
+
+def done_early(tiles, phases):
+    return sum(slot_of(k, phases) < 3 * tiles for k in range(tiles))
+
+
+def next_phase(k, tiles):
+    return next(p for p in range(1000) if slot_of(k, p) >= 3 * tiles)
 
 
 class Prefix:
-    states = 16
-
     def __init__(self, totals, landing, start, incoming, gaps, rates, send_sem, recv_sem, rounds):
         self.totals, self.landing, self.start, self.incoming, self.gaps = totals, landing, start, incoming, gaps
         self.rates, self.send_sem, self.recv_sem, self.rounds = rates, send_sem, recv_sem, rounds
@@ -137,7 +146,7 @@
     rank, states, chunk, rounds, seq,
     pre_ref, active_ref, gate_ref, graded_ref, select_ref, decay_ref, skip_ref, normed_ref, upstream_ref,
     gated_ref, dgate_ref, dprelow_ref, dactive_ref, drate_ref, dbias_ref, dskip_ref, dselect_ref,
-    gate_sum, out_sum, gate_part, out_part,
+    gate_sum, out_sum, handed,
     inject_scr, readout_scr, dread_scr, dinject_scr, state_scr, factor_scr,
     rates_scr, rate_scr, delta_scr, drive_scr, grad_scr, scan_scr, weight_scr,
     ahead_scr, behind_scr, sums_scr, gated_scr, dgated_scr,
@@ -155,37 +164,31 @@
         totals, totals_in, start_scr, incoming_scr, gaps_scr, rates_scr, prefix_send, prefix_recv, rounds
     )
     ex = Exchange(acc, out, landing, extra, send_sem, recv_sem, chunk, landing.shape[0], seq)
-    early = early_chunks(count * LANES, ex.phases)
+    early = done_early(count, ex.phases)
     half, unroll = states // 2, 8
     halves = [pl.ds(0, half), pl.ds(half, half)]
 
-    def stores(k, kind):
-        pair, final = k // 2, kind < 2
-        at = pair - (0 if final else early // 2)
-        source = (out if final else acc).at[k]
-        copies = []
-        if kind % 2 == 0:
-            target = gate_sum if final else gate_part
-            for side in range(2):
-                lanes = pl.ds(pl.multiple_of(at * 2 * LANES + side * LANES, LANES), LANES)
-                copies.append((source.at[pl.ds(side * width, width), :], target.at[:, lanes]))
-        else:
-            target = out_sum if final else out_part
-            tall = pl.ds(pl.multiple_of(at * 2 * LANES, 2 * LANES), 2 * LANES)
-            for b in range(width // LANES):
-                copies.append((
-                    source.at[pl.ds(b * 2 * LANES, 2 * LANES), :], target.at[tall, pl.ds(b * LANES, LANES)]
-                ))
-        for source, target in copies:
-            pltpu.make_async_copy(source, target, store_sem.at[k]).start()
-
     def store(k):
-        for kind in range(4):
-            fits = (lax.rem(k, 2) == kind % 2) & ((k < early) if kind < 2 else (k >= early))
-
-            @pl.when(fits)
+        pair = k // 2
+
+        @pl.when(lax.rem(k, 2) == 0)
+        def _():
+            store_lanes(out.at[k], gate_sum, pair, store_sem.at[k])
+
+        @pl.when(lax.rem(k, 2) == 1)
+        def _():
+            store_rows(out.at[k], out_sum, pair, store_sem.at[k])
+
+    def take_turns(place):
+        c = step - tiles
+        for p, shift in turns(ex.phases, place):
+            k = c + shift
+
+            @pl.when(k >= 0)
             def _():
-                stores(k, kind)
+                ex.advance(k, p)
+                if p == ex.phases:
+                    store(k)
 
     @pl.when(step == 0)
     def _():
@@ -274,15 +277,7 @@
             return state
 
         lax.fori_loop(0, steps // (unroll // 2), forward, state_scr[0])
-        for p in range(ex.phases - 1 + ex.phases % 2, 0, -2):
-            k = c - (3 + p) // 2
-
-            @pl.when((k >= 0) & (k < early))
-            def _():
-                ex.advance(k, p)
-                if p == ex.phases:
-                    store(k)
-
+        take_turns(0)
         active = active_ref[...].astype(F32)
         skip = skip_ref[...]
         gate = gate_ref[...].astype(F32)
@@ -332,6 +327,8 @@
                 drate_ref[at : at + 1, :] = (
                     jnp.sum(total[n], axis=0, keepdims=True) * rate_scr[at, 0:1] * LN2
                 )
+            if h == 0:
+                take_turns(1)
         weight = weight_scr[...].reshape(rows, LANES)
         delta = delta_scr[...].reshape(rows, LANES)
         active = active_ref[...].astype(F32)
@@ -343,38 +340,19 @@
         @pl.when(odd == 1)
         def _():
             pair = c // 2
-            block = chunk // 8
-
-            def gates(i, _):
-                here = pl.ds(pl.multiple_of(i * block, block), block)
-                part = jnp.dot(normed_ref[here, :], dgated_scr[...], preferred_element_type=F32).astype(BF16)
-                acc[2 * pair, here, :] = part[:, :LANES]
-                acc[2 * pair, pl.ds(pl.multiple_of(width + i * block, block), block), :] = part[:, LANES:]
-                return 0
-
-            lax.fori_loop(0, width // block, gates, 0)
+            part = jnp.dot(normed_ref[...], dgated_scr[...], preferred_element_type=F32).astype(BF16)
+            acc[2 * pair, :width, :] = part[:, :LANES]
+            acc[2 * pair, width:, :] = part[:, LANES:]
+            turned = gated_scr[...].T
             for b in range(width // (2 * LANES)):
-                part = contract_rows(gated_scr[...], upstream_ref[:, b * 2 * LANES : (b + 1) * 2 * LANES]).astype(BF16)
+                part = jnp.dot(
+                    turned, upstream_ref[:, b * 2 * LANES : (b + 1) * 2 * LANES], preferred_element_type=F32
+                ).astype(BF16)
                 for side in range(2):
                     at = (2 * b + side) * 2 * LANES
                     acc[2 * pair + 1, at : at + 2 * LANES, :] = part[:, side * LANES : (side + 1) * LANES]
 
-            @pl.when(2 * pair >= early)
-            def _():
-                store(2 * pair)
-                store(2 * pair + 1)
-
-    @pl.when(step >= tiles)
-    def _():
-        c = step - tiles
-        for p in range(ex.phases - ex.phases % 2, -1, -2):
-            k = c - 1 - p // 2
-
-            @pl.when((k >= 0) & (k < early))
-            def _():
-                ex.advance(k, p)
-                if p == ex.phases:
-                    store(k)
+        take_turns(2)
 
     for r in range(rounds, -1, -1):
         e = step - 2 * r
@@ -396,11 +374,22 @@
                 )
                 dselect_ref[:, first + n : first + n + 1] = part[:, first + n : first + n + 1]
 
-        def done(k, _):
-            pltpu.make_async_copy(acc.at[k], acc.at[k], store_sem.at[k]).wait()
-            return 0
-
-        lax.fori_loop(0, count, done, 0)
+        slots = 3 * count
+        for k in range(count):
+            for p in range(ex.phases):
+                if slots - 2 <= slot_of(k, p) < slots:
+                    ex.finish(k, p)
+        sizes = []
+        for k in range(early, count):
+            sizes.append(0)
+            for ref, base, size in ex.state(k, next_phase(k, count)):
+                here = pl.ds(pl.multiple_of(base, 16), size)
+                sizes[-1] += size
+                pltpu.make_async_copy(ref.at[k, here, :], handed.at[k - early, here, :], store_sem.at[k]).start()
+        for k in range(early):
+            wait_rows(out.at[k], store_sem.at[k])
+        for k in range(early, count):
+            wait_rows(acc.at[k, pl.ds(0, sizes[k - early]), :], store_sem.at[k])
 
 
 def run_scan(pre, active, gate, graded, select, decay_log, skip, normed, upstream, rank, seq):
@@ -411,7 +400,7 @@
     tiles, steps = inner // LANES, rows // SUB
     rounds = seq.bit_length() - 1
     phases = 10 + max(rounds - 3, 0)
-    early = early_chunks(inner, phases)
+    early = done_early(tiles, phases)
     first = early * LANES
     tall = pl.BlockSpec((rows, LANES), lambda i: (0, lax.rem(i, tiles)))
     line = pl.BlockSpec((1, LANES), lambda i: (0, lax.rem(i, tiles)))
@@ -423,8 +412,8 @@
     cube = pltpu.VMEM((tiles, states, SUB, LANES), F32)
     small = pltpu.VMEM((tiles, states, LANES), F32)
     pair = pltpu.VMEM((rows, 2 * LANES), BF16)
-    buffers = scratch(tiles, chunk, early, seq)
-    buffers[1] = pltpu.VMEM((early, chunk, LANES), BF16)
+    buffers = scratch(tiles, chunk, 3 * tiles // 4, seq)
+    buffers[1] = pltpu.VMEM((3 * tiles // 4, chunk, LANES), BF16)
     return pl.pallas_call(
         functools.partial(scan_kernel, rank, states, chunk, rounds, seq),
         grid=(2 * tiles,),
@@ -434,7 +423,7 @@
         out_specs=[
             late((rows, LANES)), late((rows, LANES)), late((rows, LANES)), late((rows, LANES)),
             late((states, LANES)), late((1, LANES)), late((1, LANES)),
-            pl.BlockSpec((rows, 2 * states), lambda i: (0, 0)), hbm, hbm, hbm, hbm,
+            pl.BlockSpec((rows, 2 * states), lambda i: (0, 0)), hbm, hbm, hbm,
         ],
         out_shape=[
             jax.ShapeDtypeStruct((rows, inner), BF16),
@@ -447,8 +436,7 @@
             jax.ShapeDtypeStruct((rows, 2 * states), F32),
             jax.ShapeDtypeStruct((width, first), BF16),
             jax.ShapeDtypeStruct((first, width), BF16),
-            jax.ShapeDtypeStruct((width, inner - first), BF16),
-            jax.ShapeDtypeStruct((inner - first, width), BF16),
+            jax.ShapeDtypeStruct((tiles - early, chunk, LANES), BF16),
         ],
         scratch_shapes=[
             wide, wide, wide, wide,
@@ -480,6 +468,26 @@
     return (lax.axis_index("dp"), place)
 
 CORE, X, Y, Z, ZZ = ("seq", 1), ("dp", 1), ("dp", 2), ("seq", 2), ("seq", 4)
+
+def wait_rows(rows, sem):
+    pltpu.make_async_copy(rows, rows, sem).wait()
+
+
+def store_lanes(source, target, pair, sem):
+    width = target.shape[0]
+    for side in range(2):
+        lanes = pl.ds(pl.multiple_of((2 * pair + side) * LANES, LANES), LANES)
+        pltpu.make_async_copy(source.at[pl.ds(side * width, width), :], target.at[:, lanes], sem).start()
+
+
+def store_rows(source, target, pair, sem):
+    tall = 2 * LANES
+    rows = pl.ds(pl.multiple_of(pair * tall, tall), tall)
+    for b in range(target.shape[1] // LANES):
+        pltpu.make_async_copy(
+            source.at[pl.ds(b * tall, tall), :], target.at[rows, pl.ds(b * LANES, LANES)], sem
+        ).start()
+
 
 class Exchange:
     def __init__(self, acc, out, landing, extra, send_sem, recv_sem, rows, window, seq):
@@ -584,12 +592,26 @@
                 base, size = self.kept[s][-1]
                 self.add(k, base, lambda w, there: self.extra[w, p - levels, there, :], s * size, size, target)
 
+    def start(self, k, p):
+        for copy in self.copies(k, p):
+            copy.start()
+
     def advance(self, k, p):
         if p > 0:
             self.finish(k, p - 1)
         if p < self.phases:
-            for copy in self.copies(k, p):
-                copy.start()
+            self.start(k, p)
+
+    def state(self, k, p):
+        levels, more, rows = self.halvings, len(self.more), self.rows
+        if p == 0:
+            return [(self.acc, 0, rows)]
+        if p == self.phases:
+            return [(self.out, 0, rows)]
+        sending = p < levels + more
+        level = min(p - 1, levels - 1) if sending else 2 * levels + more - 1 - p
+        spans = [(self.core_base, rows // 2)] if level == 0 else [self.kept[s][level] for s in range(2)]
+        return [(self.acc if sending else self.out, base, size) for base, size in spans]
 
 def scratch(chunks, rows, window, seq):
     more = len([1 for i in range(12) if (8 << i) < seq])
@@ -603,76 +625,328 @@
         pltpu.SemaphoreType.DMA((window, phases, 2)),
     ]
 
-def blocks(shape, rows):
-    height, width = shape
-    pieces = []
-    at = 0
-    for b in range(width // LANES):
-        r = 0
-        while r < height:
-            size = min(height - r, rows - at % rows)
-            pieces.append((at // rows, r, b * LANES, at % rows, size))
-            at += size
-            r += size
-    assert at % rows == 0
-    return at // rows, pieces
-
-
-def sum_kernel(rows, window, seq, shapes, gap, *refs):
-    n = len(shapes)
-    ins, outs = refs[:n], refs[n:2*n]
-    acc, out, landing, extra, send_sem, recv_sem, load_sem, store_sem = refs[2 * n :]
-    ex = Exchange(acc, out, landing, extra, send_sem, recv_sem, rows, window, seq)
-    count = acc.shape[0]
-    loads, stores = {}, {}
-    first = 0
-    for i, shape in enumerate(shapes):
-        used, pieces = blocks(shape, rows)
-        for j, (c, r, lane, at, size) in enumerate(pieces):
-            hbm = lambda ref: ref.at[pl.ds(r, size), pl.ds(lane, LANES)]
-            vm = acc.at[first + c, pl.ds(at, size), :]
-            done = out.at[first + c, pl.ds(at, size), :]
-            loads.setdefault(first + c, []).append(pltpu.make_async_copy(hbm(ins[i]), vm, load_sem.at[first + c]))
-            stores.setdefault(first + c, []).append(pltpu.make_async_copy(done, hbm(outs[i]), store_sem.at[first + c]))
-        first += used
-    for c in range(count):
-        for copy in loads[c]:
-            copy.start()
-    ex.greet()
-    whole = lambda c, ref, sem: pltpu.make_async_copy(ref.at[c], ref.at[c], sem)
-    def slot(t, _):
+def tail_kernel(
+    rank, states, chunk, seq,
+    dprelow_ref, select_ref, dpair_ref, step_weight_ref, normed_ref, upstream_ref, inputs_ref, scale_ref, ids_ref,
+    gain_ref, dactive_first_ref, mixed_first_ref, select_weight_ref, halo_ref, drate_ref, dbias_ref, dskip_ref,
+    dactive_ref, mixed_ref, front_ref, active_ref, select_tile_ref, conv_ref, front_weight_ref, gate_weight_ref,
+    dgate_ref, gated_ref, out_weight_ref, handed,
+    output_ref, dinputs_ref, front_sum, gate_rest, out_rest, embedding_sum, wide_sum, mixed_sum,
+    dselect_scr, first_scr, after_scr, spread_scr, extended_scr, dnormed_scr, result_scr, misc_scr, gain_scr,
+    acc, out, landing, extra, send_sem, recv_sem, load_sem, store_sem, first_send, first_recv,
+):
+    step = pl.program_id(0)
+    rows, width = upstream_ref.shape
+    across = width // LANES
+    inner = dprelow_ref.shape[1]
+    tiles, pairs = inner // LANES, inner // (2 * LANES)
+    tall = 2 * LANES
+    kernel = conv_ref.shape[0]
+    halo = kernel - 1
+    vocab = embedding_sum.shape[0]
+    ex = Exchange(acc, out, landing, extra, send_sem, recv_sem, chunk, landing.shape[0], seq)
+    early = done_early(tiles, ex.phases)
+    old = tiles - early
+    embedding_at, wide_at, mixed_at = (old + pairs + i for i in range(3))
+    count = old + pairs + 3
+    place = lax.axis_index("seq")
+    here_dp = lax.axis_index("dp")
+
+    def add(scr, value):
+        for b in range(across):
+            scr[b] += value[:, b * LANES : (b + 1) * LANES]
+
+    def put(scr, here, value):
+        for b in range(across):
+            scr[b, here, :] = value[:, b * LANES : (b + 1) * LANES]
+
+    def take(scr, here):
+        return jnp.concatenate([scr[b, here, :] for b in range(across)], axis=1)
+
+    def first_copy():
+        return pltpu.make_async_remote_copy(
+            src_ref=first_scr, dst_ref=after_scr, send_sem=first_send, recv_sem=first_recv,
+            device_id=(here_dp, lax.rem(place + seq - 1, seq)), device_id_type=MESH,
+        )
+
+    def greet():
+        barrier = pltpu.get_barrier_semaphore()
+        partners = ex.partners()
+        for device in partners:
+            pl.semaphore_signal(barrier, inc=1, device_id=device, device_id_type=MESH)
+        for there, by in ((place > 0, -1), (place < seq - 1, 1)):
+
+            @pl.when(there)
+            def _():
+                pl.semaphore_signal(barrier, inc=1, device_id=(here_dp, place + by), device_id_type=MESH)
+
+        neighbours = 2 - (place == 0).astype(jnp.int32) - (place == seq - 1).astype(jnp.int32)
+        pl.semaphore_wait(barrier, len(partners) + neighbours)
+
+    def store(k):
+        pair = (k + early) // 2
+
+        @pl.when((k < old) & (lax.rem(k + early, 2) == 0))
+        def _():
+            store_lanes(out.at[k], gate_rest, pair - early // 2, store_sem.at[k])
+
+        @pl.when((k < old) & (lax.rem(k + early, 2) == 1))
+        def _():
+            store_rows(out.at[k], out_rest, pair - early // 2, store_sem.at[k])
+
+        @pl.when((k >= old) & (k < embedding_at))
+        def _():
+            store_lanes(out.at[k], front_sum, k - old, store_sem.at[k])
+
+        @pl.when(k == embedding_at)
+        def _():
+            for b in range(width // LANES):
+                pltpu.make_async_copy(
+                    out.at[k, pl.ds(b * vocab, vocab), :], embedding_sum.at[:, pl.ds(b * LANES, LANES)], store_sem.at[k]
+                ).start()
+
+        @pl.when(k == wide_at)
+        def _():
+            pltpu.make_async_copy(out.at[k], wide_sum, store_sem.at[k]).start()
+
+        @pl.when(k == mixed_at)
+        def _():
+            pltpu.make_async_copy(out.at[k], mixed_sum, store_sem.at[k]).start()
+
+    def old_turns():
+        for spot in range(3):
+            slot = 3 * (tiles + step) + spot
+            for p, shift in turns(ex.phases, spot):
+                k = tiles + step + shift - early
+
+                @pl.when((k >= 0) & (k < old))
+                def _():
+                    if p > 0:
+
+                        @pl.when(slot >= 3 * tiles + 2)
+                        def _():
+                            ex.finish(k, p - 1)
+
+                    if p < ex.phases:
+                        ex.start(k, p)
+                    else:
+                        store(k)
+
+    def new_turns():
         for p in range(ex.phases, -1, -1):
-            k = t - p * gap
-            @pl.when((k >= 0) & (k < count))
+            k = old + step - 2 * p
+
+            @pl.when((k >= old) & (k < count))
             def _():
-                if p == 0:
-                    whole(k, acc, load_sem.at[k]).wait()
                 ex.advance(k, p)
                 if p == ex.phases:
-                    for c in range(count):
-                        @pl.when(k == c)
-                        def _():
-                            for copy in stores[c]:
-                                copy.start()
-        return 0
-    lax.fori_loop(0, count + ex.phases * gap, slot, 0)
-    def done(c, _):
-        whole(c, out, store_sem.at[c]).wait()
-        return 0
-    lax.fori_loop(0, count, done, 0)
-
-def sum_everywhere(arrays, seq, rows=2048, window=22, collective_id=0, gap=2):
-    shapes = [a.shape for a in arrays]
-    count = sum(blocks(s, rows)[0] for s in shapes)
+                    store(k)
+
+    @pl.when(step == 0)
+    def _():
+        sizes = []
+        for k in range(old):
+            sizes.append(0)
+            for ref, base, size in ex.state(k, next_phase(k + early, tiles)):
+                here = pl.ds(pl.multiple_of(base, 16), size)
+                sizes[-1] += size
+                pltpu.make_async_copy(handed.at[k, here, :], ref.at[k, here, :], load_sem.at[k]).start()
+        greet()
+        dlow = contract_cols(dprelow_ref[...], step_weight_ref[...])
+        dselect_scr[...] = jnp.concatenate([dlow, dpair_ref[...]], axis=1).astype(BF16)
+        some = contract_cols(dselect_scr[: halo * SUB], select_weight_ref[...])
+        some = (dactive_first_ref[...] + some) * silu_slope(mixed_first_ref[...])
+        for i in range(halo):
+            first_scr[i : i + 1, :] = some[i * SUB : i * SUB + 1, :]
+        first_scr[halo:, :] = jnp.zeros((SUB - halo, inner), F32)
+
+        @pl.when(place > 0)
+        def _():
+            first_copy().start()
+
+        dnormed_scr[...] = jnp.zeros_like(dnormed_scr)
+        result_scr[...] = jnp.zeros_like(result_scr)
+        misc_scr[...] = jnp.zeros_like(misc_scr)
+        misc_scr[kernel + 1 : kernel + 2, :] = dbias_ref[...]
+        misc_scr[kernel + 2 : kernel + 3, :] = dskip_ref[...]
+        acc[wide_at] = jnp.zeros_like(acc[wide_at])
+        acc[mixed_at] = jnp.zeros_like(acc[mixed_at])
+        for b in range(tiles):
+            at = rank * tiles + b * states
+            acc[mixed_at, at : at + states, :] = drate_ref[:, b * LANES : (b + 1) * LANES].astype(BF16)
+        for k in range(old):
+            wait_rows(acc.at[k, pl.ds(0, sizes[k]), :], load_sem.at[k])
+
+    old_turns()
+
+    @pl.when(step < pairs)
+    def _():
+        add(result_scr, jnp.dot(gated_ref[...], out_weight_ref[...], preferred_element_type=F32))
+        add(dnormed_scr, contract_cols(dgate_ref[...], gate_weight_ref[...]))
+        lanes = pl.ds(pl.multiple_of(step * tall, tall), tall)
+        mixed = mixed_ref[...]
+        back = contract_cols(dselect_scr[...], select_tile_ref[...])
+        dmixed = (dactive_ref[...] + back) * silu_slope(mixed)
+        spread_scr[:rows] = dmixed
+        extended_scr[: halo * SUB] = halo_ref[...].astype(F32)
+        extended_scr[halo * SUB :] = front_ref[...].astype(F32)
+        misc_scr[kernel : kernel + 1, lanes] = jnp.sum(dmixed, axis=0, keepdims=True)
+        for i in range(kernel):
+            misc_scr[i : i + 1, lanes] = jnp.sum(
+                dmixed * extended_scr[i * SUB : i * SUB + rows], axis=0, keepdims=True
+            )
+        wide = contract_rows(active_ref[...], dselect_scr[...]).astype(BF16)
+        acc[wide_at, pl.ds(pl.multiple_of(step * tall, tall), tall), : wide.shape[1]] = wide
+        part = contract_rows(select_ref[:, :rank], dprelow_ref[:, lanes]).astype(BF16)
+        for side in range(2):
+            at = pl.ds(pl.multiple_of((2 * step + side) * rank, rank), rank)
+            acc[mixed_at, at, :] = part[:, side * LANES : (side + 1) * LANES]
+
+        @pl.when(step == 0)
+        def _():
+            @pl.when(place > 0)
+            def _():
+                first_copy().wait_send()
+
+            @pl.when(place < seq - 1)
+            def _():
+                first_copy().wait_recv()
+
+            @pl.when(place == seq - 1)
+            def _():
+                after_scr[...] = jnp.zeros_like(after_scr)
+
+        sub = lax.broadcasted_iota(jnp.int32, (SUB, tall), 0)
+        for i in range(halo):
+            own = pltpu.roll(spread_scr[i * SUB : (i + 1) * SUB, :], SUB - 1, 0)
+            spread_scr[rows + i * SUB : rows + (i + 1) * SUB] = jnp.where(
+                sub < SUB - 1, own, after_scr[i : i + 1, lanes]
+            )
+        dfront = conv_ref[halo : halo + 1] * spread_scr[:rows]
+        for i in range(1, kernel):
+            dfront = dfront + conv_ref[halo - i : halo - i + 1] * spread_scr[i * SUB : i * SUB + rows]
+        dfront = dfront.astype(BF16)
+        part = jnp.dot(normed_ref[...], dfront, preferred_element_type=F32).astype(BF16)
+        acc[old + step, :width, :] = part[:, :LANES]
+        acc[old + step, width:, :] = part[:, LANES:]
+        add(dnormed_scr, contract_cols(dfront, front_weight_ref[...]))
+
+    @pl.when(step == pairs)
+    def _():
+        part = rows // SUB
+
+        def norms(i, total):
+            here = pl.ds(pl.multiple_of(i * part, part), part)
+            dnormed, inputs, scale = take(dnormed_scr, here), inputs_ref[here, :], scale_ref[here, :]
+            scaled = gain_ref[...] * dnormed
+            mean = jnp.sum(scaled * inputs, axis=1, keepdims=True) * (1.0 / width)
+            put(
+                dnormed_scr, here,
+                upstream_ref[here, :].astype(F32) + scale * scaled - inputs * (scale * scale * scale * mean),
+            )
+            put(result_scr, here, take(result_scr, here) + inputs)
+            return total + jnp.sum((dnormed * inputs * scale).reshape(-1, SUB, width), axis=0)
+
+        total = lax.fori_loop(0, SUB, norms, jnp.zeros((SUB, width), F32))
+        gain_scr[...] = jnp.sum(total, axis=0, keepdims=True)
+        hot = (ids_ref[...] == lax.broadcasted_iota(jnp.int32, (rows, vocab), 1)).astype(F32).astype(BF16)
+        for b in range(width // tall):
+            value = jnp.concatenate([dnormed_scr[2 * b], dnormed_scr[2 * b + 1]], axis=1)
+            high = value.astype(BF16)
+            low = (value - high.astype(F32)).astype(BF16)
+            whole = (contract_rows(hot, high) + contract_rows(hot, low)).astype(BF16)
+            for side in range(2):
+                at = (2 * b + side) * vocab
+                acc[embedding_at, at : at + vocab, :] = whole[:, side * LANES : (side + 1) * LANES]
+        at = (rank + states) * tiles
+        for b in range(tiles):
+            acc[mixed_at, at + b * 16 : at + (b + 1) * 16, :] = misc_scr[:, b * LANES : (b + 1) * LANES].astype(BF16)
+        at = (rank + states + 16) * tiles
+        for b in range(width // LANES):
+            acc[mixed_at, at + b * 16 : at + (b + 1) * 16, :] = jnp.broadcast_to(
+                gain_scr[:, b * LANES : (b + 1) * LANES], (16, LANES)
+            ).astype(BF16)
+
+    @pl.when(step == pairs + 1)
+    def _():
+        span = rows // SUB
+        for i in range(SUB):
+            for b in range(across):
+                lanes, every = slice(b * LANES, (b + 1) * LANES), pl.ds(i, span, stride=SUB)
+                dinputs_ref[i * span : (i + 1) * span, lanes] = dnormed_scr[b, every, :]
+                output_ref[i * span : (i + 1) * span, lanes] = result_scr[b, every, :].astype(BF16)
+
+    new_turns()
+
+    @pl.when(step == pl.num_programs(0) - 1)
+    def _():
+        for k in range(count):
+            wait_rows(out.at[k], store_sem.at[k])
+
+
+def run_tail(
+    d_pre_low, select, d_pair, step_weight, normed, upstream, inputs, scale, ids, gain, d_active, mixed, select_weight,
+    halo, d_rate, d_bias, d_skip, front, active, conv_weight, input_weight, d_gate, gated, output_weight, handed, vocab, seq,
+):
+    rows, inner = front.shape
+    width = inputs.shape[1]
+    rank, states = step_weight.shape[0], d_rate.shape[0]
+    chunk = 2 * width
+    tiles, pairs, tall = inner // LANES, inner // (2 * LANES), 2 * LANES
+    phases = 10 + max(seq.bit_length() - 4, 0)
+    early = done_early(tiles, phases)
+    count = tiles - early + pairs + 3
+    some = halo.shape[0]
+    at = lambda i: lax.min(i, pairs - 1)
+    whole = lambda a: pl.BlockSpec(a.shape, lambda i: (0, 0), pipeline_mode=pl.Buffered(1))
+    first = pl.BlockSpec((some, inner), lambda i: (0, 0), pipeline_mode=pl.Buffered(1))
+    tile = lambda height: pl.BlockSpec((height, tall), lambda i: (0, at(i)))
+    high = lambda wide: pl.BlockSpec((tall, wide), lambda i: (at(i), 0))
     hbm = pl.BlockSpec(memory_space=pltpu.HBM)
+    fixed = pl.BlockSpec((rows, width), lambda i: (0, 0))
+    rest = (tiles - early) * LANES
     return pl.pallas_call(
-        functools.partial(sum_kernel, rows, window, seq, shapes, gap),
-        out_shape=[jax.ShapeDtypeStruct(s, BF16) for s in shapes],
-        in_specs=[hbm] * len(arrays), out_specs=[hbm] * len(arrays),
-        scratch_shapes=scratch(count, rows, window, seq) + [pltpu.SemaphoreType.DMA((count,)), pltpu.SemaphoreType.DMA((count,))],
-        compiler_params=pltpu.CompilerParams(collective_id=collective_id, has_side_effects=True, vmem_limit_bytes=60 << 20),
-        name="sum_everywhere",
-    )(*arrays)
+        functools.partial(tail_kernel, rank, states, chunk, seq),
+        grid=(pairs + 3 + 2 * phases,),
+        in_specs=[
+            whole(d_pre_low), whole(select), whole(d_pair), whole(step_weight), whole(normed), whole(upstream),
+            whole(inputs), whole(scale), whole(ids), whole(gain), first, first, whole(select_weight), tile(some),
+            whole(d_rate), whole(d_bias), whole(d_skip), tile(rows), tile(rows), tile(rows), tile(rows),
+            high(select_weight.shape[1]), tile(conv_weight.shape[0]), tile(width),
+            pl.BlockSpec((width, tall), lambda i: (0, at(i) + pairs)), tile(rows), tile(rows), high(width), hbm,
+        ],
+        out_specs=[fixed, fixed, hbm, hbm, hbm, hbm, hbm, hbm],
+        out_shape=[
+            jax.ShapeDtypeStruct((rows, width), BF16),
+            jax.ShapeDtypeStruct((rows, width), F32),
+            jax.ShapeDtypeStruct((width, inner), BF16),
+            jax.ShapeDtypeStruct((width, rest), BF16),
+            jax.ShapeDtypeStruct((rest, width), BF16),
+            jax.ShapeDtypeStruct((vocab, width), BF16),
+            jax.ShapeDtypeStruct((chunk, LANES), BF16),
+            jax.ShapeDtypeStruct((chunk, LANES), BF16),
+        ],
+        scratch_shapes=[
+            pltpu.VMEM(select.shape, BF16),
+            pltpu.VMEM((SUB, inner), F32), pltpu.VMEM((SUB, inner), F32),
+            pltpu.VMEM((rows + some, tall), F32), pltpu.VMEM((rows + some, tall), F32),
+            pltpu.VMEM((width // LANES, rows, LANES), F32), pltpu.VMEM((width // LANES, rows, LANES), F32),
+            pltpu.VMEM((16, inner), F32), pltpu.VMEM((1, width), F32),
+        ]
+        + scratch(count, chunk, count, seq)
+        + [
+            pltpu.SemaphoreType.DMA((count,)), pltpu.SemaphoreType.DMA((count,)),
+            pltpu.SemaphoreType.DMA, pltpu.SemaphoreType.DMA,
+        ],
+        compiler_params=pltpu.CompilerParams(
+            collective_id=2, has_side_effects=True, vmem_limit_bytes=62 << 20
+        ),
+        name="span_tail",
+    )(
+        d_pre_low, select, d_pair, step_weight, normed, upstream, inputs, scale, ids, gain, d_active, mixed,
+        select_weight, halo, d_rate, d_bias, d_skip, d_active, mixed, front, active, select_weight, conv_weight,
+        input_weight, input_weight, d_gate, gated, output_weight, handed,
+    )
 
 
 def on_device(
@@ -710,8 +984,8 @@
     ).astype(BF16)
     last = front[rows - halo * SUB :].reshape(halo, SUB, inner)
     tail = passed_along(last[:, SUB - 1], "seq", 1)
-    earlier = jnp.concatenate([tail[:, None], last[:, : SUB - 1]], axis=1)
-    extended = jnp.concatenate([earlier.reshape(halo * SUB, inner), front], axis=0).astype(F32)
+    earlier = jnp.concatenate([tail[:, None], last[:, : SUB - 1]], axis=1).reshape(halo * SUB, inner)
+    extended = jnp.concatenate([earlier, front], axis=0).astype(F32)
     mixed = conv_bias + conv_weight[0] * extended[:rows]
     for place in range(1, kernel):
         mixed = mixed + conv_weight[place] * extended[place * SUB : place * SUB + rows]
@@ -721,91 +995,40 @@
     pre = jnp.dot(lowrank, step_weight, preferred_element_type=F32) + step_bias
     upstream = to_spans(cotangent.reshape(rows, width))
     graded = contract_cols(upstream, output_projection_weight)
+    seq = lax.axis_size("seq")
+    turned = normed_input.T
     (
-        gated, d_gate, d_pre_low, d_active, d_decay_log, d_step_bias, d_skip_gain, d_pair,
-        gate_sum, out_sum, gate_part, out_part,
+        gated, d_gate, d_pre_low, d_active, d_rate, d_bias, d_skip, d_pair, gate_sum, out_sum, handed
     ) = run_scan(
-        pre, active, gate, graded, select, decay_log, skip_gain.reshape(1, inner),
-        normed_input.T, upstream, rank, lax.axis_size("seq"),
+        pre, active, gate, graded, select, decay_log, skip_gain.reshape(1, inner), turned, upstream, rank, seq
     )
-
-    result = block_inputs + jnp.dot(gated, output_projection_weight, preferred_element_type=F32)
-    output = from_spans(result.astype(BF16)).reshape(count, stretch, width)
-    d_step_weight = contract_rows(lowrank, d_pre_low)
-    d_lowrank = contract_cols(d_pre_low, step_weight)
-    d_select = jnp.concatenate([d_lowrank, d_pair], axis=1).astype(BF16)
-    d_select_weight = contract_rows(active, d_select)
-    d_mixed = (d_active + contract_cols(d_select, select_weight)) * silu_slope(mixed)
-    d_conv_bias = jnp.sum(d_mixed, axis=0)
-    d_conv_weight = jnp.stack(
-        [
-            jnp.sum(d_mixed * extended[place * SUB : place * SUB + rows], axis=0)
-            for place in range(kernel)
-        ]
+    output, d_inputs, front_sum, gate_rest, out_rest, embedding_sum, wide_sum, mixed_sum = run_tail(
+        d_pre_low, select, d_pair, step_weight, turned, upstream, block_inputs, scale, ids, norm_gain.reshape(1, width),
+        d_active, mixed, select_weight, earlier, d_rate, d_bias, d_skip, front, active, conv_weight,
+        input_projection_weight, d_gate, gated, output_projection_weight, handed, vocab, seq,
     )
-    first = d_mixed[: halo * SUB].reshape(halo, SUB, inner)
-    after = passed_along(first[:, 0], "seq", -1)
-    later = jnp.concatenate([first[:, 1:], after[:, None]], axis=1)
-    spread = jnp.concatenate([d_mixed, later.reshape(halo * SUB, inner)], axis=0)
-    d_front = conv_weight[halo] * spread[:rows]
-    for place in range(1, kernel):
-        d_front = d_front + conv_weight[halo - place] * spread[place * SUB : place * SUB + rows]
-    d_front = d_front.astype(BF16)
-    d_both = jnp.concatenate([d_front, d_gate], axis=1)
-    d_front_weight = contract_rows(normed_input, d_front)
-    d_normed = contract_cols(d_both, input_projection_weight)
-    d_norm_gain = jnp.sum(d_normed * block_inputs * scale, axis=0)
-    scaled = norm_gain * d_normed
-    cubed = scale * scale * scale
-    d_inputs = (
-        upstream.astype(F32)
-        + scale * scaled
-        - block_inputs * cubed * jnp.mean(scaled * block_inputs, axis=1, keepdims=True)
-    )
-    high = d_inputs.astype(BF16)
-    low = (d_inputs - high.astype(F32)).astype(BF16)
-    hot = one_hot.astype(BF16)
-    d_embedding = contract_rows(hot, high) + contract_rows(hot, low)
-    small = (
-        d_norm_gain,
-        d_conv_weight,
-        d_conv_bias,
-        d_select_weight,
-        d_step_weight,
-        d_step_bias,
-        d_decay_log,
-        d_skip_gain,
-    )
-    flat = jnp.concatenate([part.astype(BF16).reshape(-1) for part in small])
-    unit = 2048 * LANES
-    flat = jnp.pad(flat, (0, -flat.size % unit)).reshape(-1, LANES)
-    front_sum, gate_rest, out_rest, embedding_sum, flat = sum_everywhere(
-        [d_front_weight.astype(BF16), gate_part, out_part, d_embedding.astype(BF16), flat], lax.axis_size("seq")
-    )
-    d_input_sum = jnp.concatenate([front_sum, gate_sum, gate_rest], axis=1).astype(F32)
-    d_output_sum = jnp.concatenate([out_sum, out_rest], axis=0).astype(F32)
-    d_embedding_sum = embedding_sum.astype(F32)
-    flat = flat.astype(F32)
-    flat = flat.reshape(-1)
-    sums, at = [], 0
-    shapes = [norm_gain, conv_weight, conv_bias, select_weight, step_weight, step_bias, decay_log, skip_gain]
-    for like in shapes:
-        sums.append(flat[at : at + like.size].reshape(like.shape))
-        at += like.size
+    tiles = inner // LANES
+
+    def unpacked(first, height, blocks):
+        part = mixed_sum[first : first + height * blocks].astype(F32).reshape(blocks, height, LANES)
+        return part.swapaxes(0, 1).reshape(height, blocks * LANES)
+
+    at = (rank + states) * tiles
+    misc = unpacked(at, 16, tiles)
     return (
-        output,
-        from_spans(d_inputs).reshape(count, stretch, width),
-        d_embedding_sum,
-        sums[0],
-        d_input_sum,
-        sums[1],
-        sums[2],
-        sums[3],
-        sums[4],
-        sums[5],
-        sums[6],
-        sums[7],
-        d_output_sum,
+        output.reshape(count, stretch, width),
+        d_inputs.reshape(count, stretch, width),
+        embedding_sum.astype(F32),
+        unpacked(at + 16 * tiles, 16, width // LANES)[0],
+        jnp.concatenate([front_sum, gate_sum, gate_rest], axis=1).astype(F32),
+        misc[:kernel],
+        misc[kernel],
+        wide_sum[:, : select_weight.shape[1]].astype(F32),
+        unpacked(0, rank, tiles),
+        misc[kernel + 1],
+        unpacked(rank * tiles, states, tiles),
+        misc[kernel + 2],
+        jnp.concatenate([out_sum, out_rest], axis=0).astype(F32),
     )
 
 

time: 382 us -> 317 us (0.83); the launches traced: 376 us -> 317 us
  matrix products: 49.5 us -> 19.4 us
  other arithmetic: 40.4 us -> 25.7 us
  local copies, waits for them, and re-layouts: 30.2 us -> 17.1 us
    pallas_call x1, Pallas kernels: 91.8 us -> 114 us  [run_tail(): pl.pallas_call(functools.partial(tail_kernel, rank, states, chunk, seq),...]
    pallas_call x1, Pallas kernels: 158 us -> 137 us  [run_scan(): pl.pallas_call(functools.partial(scan_kernel, rank, states, chunk, rounds...]
    dot_general x6 -> x0, matrix products: 16.2 us -> none  [the longest x5 10.6 us: contract_rows(): lax.dot_general(left, right, (((0,), (0,)), ((), ())), preferred_element_...]
    dot_general x4 -> x1, matrix products: 20.5 us -> 4.52 us  [contract_cols(): lax.dot_general(left, right, (((1,), (1,)), ((), ())), preferred_element_...]
    reduce_sum x1 -> x0, other arithmetic: 14.1 us -> none  [on_device(): jnp.sum(d_mixed * extended[place * SUB:place * SUB + rows], axis=0)]
    reshape x7 -> x1, local copies, waits for them, and re-layouts: 5.95 us -> 0.83 us  [to_spans(): return array.reshape(SUB, rows // SUB, -1).swapaxes(0, 1).reshape(rows, -1)]
    transpose x2 -> x0, local copies, waits for them, and re-layouts: 4.08 us -> none  [from_spans(): return array.reshape(rows // SUB, SUB, -1).swapaxes(0, 1).reshape(rows, -1)]
    unnamed x106 -> x52, local copies, waits for them, and re-layouts: 10.2 us -> 6.46 us
  transfers between devices with their start and end apart: 2 -> 1, of which waited for: 0 -> 0; matrix products, arithmetic and copies ran while one was open for 4% -> 5% of each run, Pallas kernels for 0% -> 0%
where the time goes in v1:
time: 317 us
  Pallas kernels  251 us (79%)
  other arithmetic  25.7 us (8%)
  matrix products  19.4 us (6%)
  local copies, waits for them, and re-layouts  17.1 us (5%)
    pallas_call x1, Pallas kernels, run_scan(): pl.pallas_call(functools.partial(scan_kernel, rank, states, chunk, rounds...  137 us
    pallas_call x1, Pallas kernels, run_tail(): pl.pallas_call(functools.partial(tail_kernel, rank, states, chunk, seq),...  114 us
    convert_element_type x1, other arithmetic, on_device(): jnp.concatenate([out_sum, out_rest], axis=0).astype(F32)  6.92 us
    unnamed x52, local copies, waits for them, and re-layouts  6.46 us
    convert_element_type x1, other arithmetic, on_device(): jnp.concatenate([front_sum, gate_sum, gate_rest], axis=1).astype(F32)  6.44 us
  transfers between devices with their start and end apart: 1, of which 0 were waited for; matrix products, arithmetic and copies ran while one was open for 5% of the time, Pallas kernels for 0%

profile of v1, /device:TPU:0, one launch (start us, length us, event | category | flops | bytes accessed | tf_op | source)
XLA Modules:
  0.0 317.0 jit_solution(10556524802201393622)
XLA Ops:
  0.6 0.0 copy-start
  0.7 0.0 copy-start.20
  0.7 0.5 broadcast.35
  1.2 1.3 reduce.3
  2.5 0.1 reshape_reshape.6
  2.6 0.1 copy.37
  2.7 0.1 eq.15
  2.8 0.6 multiply_reduce_fusion
  3.4 2.0 copy.38
  5.4 5.5 %fusion.8.front_ref = bf16[512,2048]{1,0:T(8,128)(2,1)S(1)} fusion(bf16[1024,4096]{1,0:T(8,128)(2,1)} %gate_weight_ref.1, f32[512,1024]{0,1:T(8,128)} %copy.38, f32[1024]{0:T(1024)S(1)} %copy-done.20, f32[512]{0:T(512)S(1)} %add_rsqrt_fusion), kind=kOutput, calls=%fused_computation.16 | convolution fusion | flops 2150105088 | bytes 8394752 | tf_op jit(solution)/shard_map/dot_general | solution.py:979
  10.9 0.0 copy-start.19
  11.0 0.0 copy-start.8
  11.0 0.0 copy-start.15
  11.0 2.8 collective-permute-start
  13.8 5.4 %fusion.11.gate_ref = bf16[512,2048]{1,0:T(8,128)(2,1)} fusion(bf16[1024,4096]{1,0:T(8,128)(2,1)S(1)} %copy-done.2, f32[512,1024]{0,1:T(8,128)} %copy.38, f32[1024]{0:T(1024)S(1)} %copy-done.20, f32[512]{0:T(512)S(1)} %add_rsqrt_fusion), kind=kOutput, calls=%fused_computation.17 | convolution fusion | flops 2150105088 | bytes 8394752 | tf_op jit(solution)/shard_map/dot_general | solution.py:982
  19.3 0.0 copy-start.7
  19.3 4.5 %fusion.17.graded_ref = f32[512,2048]{1,0:T(8,128)} fusion(bf16[2048,1024]{1,0:T(8,128)(2,1)S(1)} %copy-done.8, bf16[8,64,1024]{2,1,0:T(8,128)(2,1)S(1)} %bitcast.73), kind=kOutput, calls=%fused_computation.39 | convolution fusion | flops 2147483648 | bytes 9437184 | tf_op jit(solution)/shard_map/dot_general | solution.py:39
  23.8 1.2 fusion.29.normed_ref
  25.0 0.8 reshape.139.ids_ref
  25.8 2.8 copy.60
  28.6 1.0 copy.45.select_weight_ref.select_tile_ref
  29.6 0.9 copy.43.scale_ref
  30.5 0.1 maximum_bitcast_fusion.halo_ref
  30.6 0.6 maximum_convert_fusion.2
  31.2 0.0 copy-start.14
  31.2 0.0 copy-start.22
  31.2 3.8 %multiply_convert_fusion = (bf16[512,2048]{1,0:T(8,128)(2,1)S(1)}, f32[512,2048]{1,0:T(8,128)}) fusion(f32[536,2048]{1,0:T(8,128)S(1)} %maximum_convert_fusion.2, f32[2048]{0:T(1024)S(1)} %bitcast.84, f32[2048]{0:T(1024)S(1)} %bitcast.82, f32[2048]{0:T(1024)S(1)} %bitcast.83, f32[2048]{0:T(1024)S(1)} %bitcast.81, f32[2048]{0:T(1024)S(1)} %copy-done.21), kind=kLoop, calls=%fused_computation.12 | loop fusion | flops 13631488 | bytes 23109632 | tf_op jit(solution)/shard_map/convert_element_type | solution.py:992
  35.0 1.3 copy-done.4
  36.4 0.7 convolution_convert_fusion.select_ref
  37.1 2.7 convolution_add_fusion.pre_ref
  39.8 137.3 %span_scan.1 = (bf16[512,2048]{1,0:T(8,128)(2,1)}, bf16[512,2048]{1,0:T(8,128)(2,1)}, bf16[512,2048]{1,0:T(8,128)(2,1)}, f32[512,2048]{1,0:T(8,128)}, f32[16,204...) custom-call(f32[512,2048]{1,0:T(8,128)} %convolution_add_fusion.pre_, ...), custom_call_target="tpu_custom_call" | custom-call | tf_op jit(solution)/shard_map/span_scan/pallas_call | solution.py:417
  177.1 113.8 %span_tail.1 = (bf16[512,1024]{1,0:T(8,128)(2,1)}, f32[512,1024]{1,0:T(8,128)}, bf16[1024,2048]{1,0:T(8,128)(2,1)}, bf16[1024,1024]{1,0:T(8,128)(2,1)}, bf16[102...) custom-call(bf16[512,2048]{1,0:T(8,128)(2,1)} %get-tuple-element.32.dprel, ...), custom_call_target="tpu_custom_call" | custom-call | tf_op jit(solution)/shard_map/span_tail/pallas_call | solution.py:908
  290.9 0.8 slice.94
  291.6 0.9 fusion.19
  292.5 1.0 slice.101
  293.5 0.6 fusion.20
  294.1 0.6 slice_bitcast_fusion.1
  294.8 0.6 slice_convert_fusion.1
  295.4 0.7 copy_bitcast_fusion.2
  296.0 0.8 copy_bitcast_fusion.1
  296.9 2.1 convert_element_type.46
  299.0 1.1 slice_convert_fusion
  300.1 1.2 copy.50
  301.3 6.9 %maximum_convert_fusion.1 = f32[2048,1024]{1,0:T(8,128)} fusion(bf16[1024,1024]{1,0:T(8,128)(2,1)} %get-tuple-element.50, bf16[1024,1024]{1,0:T(8,128)(2,1)} %get-tuple-element.49), kind=kLoop, calls=%fused_computation.9 | loop fusion | flops 8388608 | bytes 12582912 | tf_op jit(solution)/shard_map/convert_element_type | solution.py:1031
  308.3 0.0 copy-start.1
  308.3 6.4 %maximum_convert_fusion = f32[1024,4096]{1,0:T(8,128)} fusion(bf16[1024,1024]{1,0:T(8,128)(2,1)S(1)} %copy-done.11, bf16[1024,1024]{1,0:T(8,128)(2,1)S(1)} %copy-done.10, bf16[1024,2048]{1,0:T(8,128)(2,1)S(1)} %copy-done.9), kind=kLoop, calls=%fused_computation | loop fusion | flops 25165824 | bytes 25165824 | tf_op jit(solution)/shard_map/convert_element_type | solution.py:1023
  314.7 1.0 copy.64
  315.7 1.3 copy.65
  (44 shorter events, 0.2 us)
Async XLA Ops:
  0.6 2.1 copy-start
  0.7 4.7 %copy-start.20 = (f32[1024]{0:T(1024)S(1)}, f32[1024]{0:T(1024)}, u32[]{:S(2)}) copy-start(f32[1024]{0:T(1024)} %param.16) | copy-start | bytes 12292
  3.4 7.5 %copy-start.3 = (f32[512,1024]{1,0:T(8,128)}, f32[512,1024]{1,0:T(8,128)S(1)}, u32[]{:S(2)}) copy-start(f32[512,1024]{1,0:T(8,128)S(1)} %get-tuple-element.89.inputs_ref) | copy-start | bytes 6291460
  5.4 8.4 %copy-start.2 = (bf16[1024,4096]{1,0:T(8,128)(2,1)S(1)}, bf16[1024,4096]{1,0:T(8,128)(2,1)}, u32[]{:S(2)}) copy-start(bf16[1024,4096]{1,0:T(8,128)(2,1)} %gate_weight_ref.1) | copy-start | bytes 25165828
  10.9 8.3 %copy-start.5 = (bf16[512,2048]{1,0:T(8,128)(2,1)}, bf16[512,2048]{1,0:T(8,128)(2,1)S(1)}, u32[]{:S(2)}) copy-start(bf16[512,2048]{1,0:T(8,128)(2,1)S(1)} %fusion.8.front_ref) | copy-start | bytes 6291460
  10.9 8.3 %copy-start.19 = (f32[4,2048]{1,0:T(4,128)S(1)}, f32[4,2048]{1,0:T(4,128)}, u32[]{:S(2)}) copy-start(f32[4,2048]{1,0:T(4,128)} %conv_ref.1) | copy-start | bytes 98308
  11.0 8.3 %copy-start.8 = (bf16[2048,1024]{1,0:T(8,128)(2,1)S(1)}, bf16[2048,1024]{1,0:T(8,128)(2,1)}, u32[]{:S(2)}) copy-start(bf16[2048,1024]{1,0:T(8,128)(2,1)} %out_weight_ref.1) | copy-start | bytes 12582916
  11.0 8.3 %copy-start.15 = (bf16[1,512,1024]{2,1,0:T(8,128)(2,1)S(1)}, bf16[1,512,1024]{2,1,0:T(8,128)(2,1)}, u32[]{:S(2)}) copy-start(bf16[1,512,1024]{2,1,0:T(8,128)(2,1)} %param.15) | copy-start | bytes 3145732
  11.0 19.5 %collective-permute-start = (bf16[3,2048]{1,0:T(4,128)(2,1)S(1)}, bf16[3,2048]{1,0:T(4,128)(2,1)S(1)}, u32[]{:S(2)}, u32[]{:S(2)}) collective-permute-start(bf16[3,2048]{1,0:T(4,128)(2,1)S(1)} %bitcast.87), channel_id=1, source_target_pairs={{0,1},{1,2},{2,3},{3,4},{4,5},{5,6},{6,7},{8,9},{9,10},{10,11},{11... | collective-permute-start | bytes 36872 | tf_op jit(solution)/shard_map/ppermute | solution.py:24
  19.3 4.5 %copy-start.7 = (f32[512,1024]{0,1:T(8,128)S(1)}, f32[512,1024]{0,1:T(8,128)}, u32[]{:S(2)}) copy-start(f32[512,1024]{0,1:T(8,128)} %copy.38) | copy-start | bytes 6291460
  23.8 4.8 %copy-start.18 = (bf16[2048,96]{0,1:T(8,128)(2,1)S(1)}, bf16[2048,96]{0,1:T(8,128)(2,1)}, u32[]{:S(2)}) copy-start(bf16[2048,96]{0,1:T(8,128)(2,1)} %param.20) | copy-start | bytes 1179652
  23.8 6.8 %copy-start.6 = (bf16[512,2048]{1,0:T(8,128)(2,1)S(1)}, bf16[512,2048]{1,0:T(8,128)(2,1)}, u32[]{:S(2)}) copy-start(bf16[512,2048]{1,0:T(8,128)(2,1)} %copy-done.5) | copy-start | bytes 6291460
  28.6 2.5 copy-start.21
  30.6 4.4 %copy-start.17 = (bf16[24,2048]{1,0:T(8,128)(2,1)}, bf16[24,2048]{1,0:T(8,128)(2,1)S(1)}, u32[]{:S(2)}) copy-start(bf16[24,2048]{1,0:T(8,128)(2,1)S(1)} %maximum_bitcast_fusion.halo_ref) | copy-start | bytes 294916
  31.2 5.9 %copy-start.14 = (bf16[64,2048]{1,0:T(8,128)(2,1)S(1)}, bf16[64,2048]{1,0:T(8,128)(2,1)}, u32[]{:S(2)}) copy-start(bf16[64,2048]{1,0:T(8,128)(2,1)} %step_weight_ref.1) | copy-start | bytes 786436
  31.2 5.9 %copy-start.22 = (f32[2048]{0:T(1024)S(1)}, f32[2048]{0:T(1024)}, u32[]{:S(2)}) copy-start(f32[2048]{0:T(1024)} %param.22) | copy-start | bytes 24580
  35.0 1.3 copy-start.4
  37.1 2.7 copy-start.13
  301.3 6.9 %copy-start.9 = (bf16[1024,2048]{1,0:T(8,128)(2,1)S(1)}, bf16[1024,2048]{1,0:T(8,128)(2,1)}, u32[]{:S(2)}) copy-start(bf16[1024,2048]{1,0:T(8,128)(2,1)} %get-tuple-element.45) | copy-start | bytes 12582916
  301.3 6.9 %copy-start.10 = (bf16[1024,1024]{1,0:T(8,128)(2,1)S(1)}, bf16[1024,1024]{1,0:T(8,128)(2,1)}, u32[]{:S(2)}) copy-start(bf16[1024,1024]{1,0:T(8,128)(2,1)} %get-tuple-element.46) | copy-start | bytes 6291460
  301.3 6.9 %copy-start.11 = (bf16[1024,1024]{1,0:T(8,128)(2,1)S(1)}, bf16[1024,1024]{1,0:T(8,128)(2,1)}, u32[]{:S(2)}) copy-start(bf16[1024,1024]{1,0:T(8,128)(2,1)} %get-tuple-element.47) | copy-start | bytes 6291460
  308.2 6.5 %copy-start.16 = (bf16[512,1024]{1,0:T(8,128)(2,1)S(1)}, bf16[512,1024]{1,0:T(8,128)(2,1)}, u32[]{:S(2)}) copy-start(bf16[512,1024]{1,0:T(8,128)(2,1)} %get-tuple-element.41) | copy-start | bytes 3145732
  308.3 7.4 %copy-start.12 = (f32[512,1024]{1,0:T(8,128)S(1)}, f32[512,1024]{1,0:T(8,128)}, u32[]{:S(2)}) copy-start(f32[512,1024]{1,0:T(8,128)} %get-tuple-element.42) | copy-start | bytes 6291460
  308.3 8.7 %copy-start.1 = (bf16[256,1024]{1,0:T(8,128)(2,1)S(1)}, bf16[256,1024]{1,0:T(8,128)(2,1)}, u32[]{:S(2)}) copy-start(bf16[256,1024]{1,0:T(8,128)(2,1)} %param.14) | copy-start | bytes 1572868

commit v2 on v1

--- a/solution.py
+++ b/solution.py
@@ -81,19 +81,19 @@
 
 
 def slot_of(k, p):
-    return 3 * k + 5 + 2 * p
+    return 2 * k + 3 + 2 * p
 
 
 def turns(phases, place):
-    return [(p, (place - 5 - 2 * p) // 3) for p in range(phases, -1, -1) if (place - 5 - 2 * p) % 3 == 0]
+    return [(p, (place - 3 - 2 * p) // 2) for p in range(phases, -1, -1) if (place - 3 - 2 * p) % 2 == 0]
 
 
 def done_early(tiles, phases):
-    return sum(slot_of(k, phases) < 3 * tiles for k in range(tiles))
+    return sum(slot_of(k, phases) < 2 * tiles for k in range(tiles))
 
 
 def next_phase(k, tiles):
-    return next(p for p in range(1000) if slot_of(k, p) >= 3 * tiles)
+    return next(p for p in range(1000) if slot_of(k, p) >= 2 * tiles)
 
 
 class Prefix:
@@ -144,11 +144,12 @@
 
 def scan_kernel(
     rank, states, chunk, rounds, seq,
-    pre_ref, active_ref, gate_ref, graded_ref, select_ref, decay_ref, skip_ref, normed_ref, upstream_ref,
+    pre_now, active_now, gate_now, graded_now, pre_ref, active_ref, gate_ref, graded_ref,
+    select_ref, decay_ref, skip_ref, normed_ref, upstream_ref,
     gated_ref, dgate_ref, dprelow_ref, dactive_ref, drate_ref, dbias_ref, dskip_ref, dselect_ref,
     gate_sum, out_sum, handed,
     inject_scr, readout_scr, dread_scr, dinject_scr, state_scr, factor_scr,
-    rates_scr, rate_scr, delta_scr, drive_scr, grad_scr, scan_scr, weight_scr,
+    rates_scr, rate_scr, delta_scr, drive_scr, grad_scr, sigma_scr, scan_scr, weight_scr,
     ahead_scr, behind_scr, sums_scr, gated_scr, dgated_scr,
     totals, totals_in, start_scr, incoming_scr, gaps_scr, prefix_send, prefix_recv,
     acc, out, landing, extra, send_sem, recv_sem, store_sem,
@@ -156,10 +157,9 @@
     rows = pre_ref.shape[0]
     steps = rows // SUB
     step = pl.program_id(0)
-    tiles = pl.num_programs(0) // 2
-    count = 2 * rates_scr.shape[0] // 2
+    count = rates_scr.shape[0]
+    lag = rounds + 1
     width = upstream_ref.shape[1]
-    tile = lax.rem(step, tiles)
     prefix = Prefix(
         totals, totals_in, start_scr, incoming_scr, gaps_scr, rates_scr, prefix_send, prefix_recv, rounds
     )
@@ -180,7 +180,7 @@
             store_rows(out.at[k], out_sum, pair, store_sem.at[k])
 
     def take_turns(place):
-        c = step - tiles
+        c = step - lag
         for p, shift in turns(ex.phases, place):
             k = c + shift
 
@@ -193,9 +193,10 @@
     @pl.when(step == 0)
     def _():
         for first, scr in ((rank, inject_scr), (rank + states, readout_scr)):
-            wide = expand_columns(select_ref[...], first, states)
-            for n in range(states):
-                scr[:, n] = wide[:, n * LANES : (n + 1) * LANES].reshape(steps, SUB, LANES)
+            for n in range(0, states, 2):
+                wide = expand_columns(select_ref[...], first + n, 2)
+                for side in range(2):
+                    scr[:, n + side] = wide[:, side * LANES : (side + 1) * LANES].reshape(steps, SUB, LANES)
         dread_scr[...] = jnp.zeros_like(dread_scr)
         dinject_scr[...] = jnp.zeros_like(dinject_scr)
         start_scr[...] = jnp.zeros_like(start_scr)
@@ -205,21 +206,25 @@
             rates_scr[e] = -jnp.exp(decay_ref[:, e * LANES : (e + 1) * LANES]) * LOG2E
         ex.greet()
 
-    rates = rates_scr[tile]
-    for n in range(states):
-        rate_scr[n] = jnp.broadcast_to(rates[n : n + 1], (SUB, LANES))
     flat = lambda value: value.reshape(steps, SUB, LANES)
-    active = active_ref[...].astype(F32)
-    delta = jax.nn.softplus(pre_ref[...])
-    delta_scr[...] = flat(delta)
-    drive_scr[...] = flat(delta * active)
-    gate = gate_ref[...].astype(F32)
-    sigma = jax.nn.sigmoid(gate)
-    grad_scr[...] = flat(graded_ref[...] * (gate * sigma))
     zero = jnp.zeros((half, SUB, LANES), F32)
 
-    @pl.when(step < tiles)
+    def prepare(tile, pre_ref, active_ref, gate_ref, graded_ref):
+        rates = rates_scr[tile]
+        for n in range(states):
+            rate_scr[n] = jnp.broadcast_to(rates[n : n + 1], (SUB, LANES))
+        delta = jax.nn.softplus(pre_ref[...])
+        delta_scr[...] = flat(delta)
+        drive_scr[...] = flat(delta * active_ref[...].astype(F32))
+        gate = gate_ref[...].astype(F32)
+        sigma = jax.nn.sigmoid(gate)
+        sigma_scr[...] = flat(sigma)
+        grad_scr[...] = flat(graded_ref[...] * (gate * sigma))
+
+    @pl.when(step < count)
     def _():
+        tile = step
+        prepare(tile, pre_now, active_now, gate_now, graded_now)
         total = jnp.sum(delta_scr[...], axis=0)
         sums_scr[tile] = total
         whole = jnp.sum(total, axis=0, keepdims=True)
@@ -254,9 +259,11 @@
             [jnp.broadcast_to(table[n : n + 1], (1, SUB, LANES)) for n in range(states)], axis=0
         )
 
-    @pl.when(step >= tiles)
+    @pl.when(step >= lag)
     def _():
-        c = step - tiles
+        c = step - lag
+        tile = c
+        prepare(tile, pre_ref, active_ref, gate_ref, graded_ref)
         total = sums_scr[tile]
         before, after = total, total
         for by in (1, 2, 4):
@@ -281,7 +288,7 @@
         active = active_ref[...].astype(F32)
         skip = skip_ref[...]
         gate = gate_ref[...].astype(F32)
-        sigma = jax.nn.sigmoid(gate)
+        sigma = sigma_scr[...].reshape(rows, LANES)
         graded = graded_ref[...]
         scanned = scan_scr[...].reshape(rows, LANES) + skip * active
         gated = (scanned * (gate * sigma)).astype(BF16)
@@ -327,8 +334,6 @@
                 drate_ref[at : at + 1, :] = (
                     jnp.sum(total[n], axis=0, keepdims=True) * rate_scr[at, 0:1] * LN2
                 )
-            if h == 0:
-                take_turns(1)
         weight = weight_scr[...].reshape(rows, LANES)
         delta = delta_scr[...].reshape(rows, LANES)
         active = active_ref[...].astype(F32)
@@ -352,32 +357,35 @@
                     at = (2 * b + side) * 2 * LANES
                     acc[2 * pair + 1, at : at + 2 * LANES, :] = part[:, side * LANES : (side + 1) * LANES]
 
-        take_turns(2)
+        take_turns(1)
 
     for r in range(rounds, -1, -1):
-        e = step - 2 * r
-
-        @pl.when((e >= 0) & (e < tiles))
+        e = step - r
+
+        @pl.when((e >= 0) & (e < count))
         def _():
             prefix.advance(e, r)
 
-    @pl.when(step == 2 * tiles - 1)
+    @pl.when(step == count + lag - 1)
     def _():
-        ones = jnp.ones((LANES, LANES), BF16)
+        shape = (2 * LANES, 2 * states)
+        from_lane = lax.broadcasted_iota(jnp.int32, shape, 0) // LANES
+        to_column = lax.broadcasted_iota(jnp.int32, shape, 1)
+        whole = jnp.zeros((rows, 2 * states), F32)
         for first, scr in ((0, dinject_scr), (states, dread_scr)):
-            for n in range(states):
-                value = scr[:, n].reshape(rows, LANES)
+            for n in range(0, states, 2):
+                ones = (from_lane + (first + n) == to_column).astype(F32).astype(BF16)
+                value = jnp.concatenate([scr[:, n + side].reshape(rows, LANES) for side in range(2)], axis=1)
                 high = value.astype(BF16)
                 low = (value - high.astype(F32)).astype(BF16)
-                part = jnp.dot(high, ones, preferred_element_type=F32) + jnp.dot(
-                    low, ones, preferred_element_type=F32
-                )
-                dselect_ref[:, first + n : first + n + 1] = part[:, first + n : first + n + 1]
-
-        slots = 3 * count
+                whole = whole + jnp.dot(high, ones, preferred_element_type=F32)
+                whole = whole + jnp.dot(low, ones, preferred_element_type=F32)
+        dselect_ref[...] = whole
+
+        slots = 2 * count
         for k in range(count):
             for p in range(ex.phases):
-                if slots - 2 <= slot_of(k, p) < slots:
+                if slot_of(k, p) in (slots - 1, slots - 2):
                     ex.finish(k, p)
         sizes = []
         for k in range(early, count):
@@ -399,12 +407,13 @@
     chunk = 2 * width
     tiles, steps = inner // LANES, rows // SUB
     rounds = seq.bit_length() - 1
-    phases = 10 + max(rounds - 3, 0)
+    phases = 8 + max(rounds - 3, 0)
     early = done_early(tiles, phases)
-    first = early * LANES
-    tall = pl.BlockSpec((rows, LANES), lambda i: (0, lax.rem(i, tiles)))
-    line = pl.BlockSpec((1, LANES), lambda i: (0, lax.rem(i, tiles)))
-    late = lambda shape: pl.BlockSpec(shape, lambda i: (0, lax.max(i - tiles, 0)))
+    gates, outs = (early + 1) // 2 * 2 * LANES, early // 2 * 2 * LANES
+    lag = rounds + 1
+    now = pl.BlockSpec((rows, LANES), lambda i: (0, lax.min(i, tiles - 1)))
+    late = lambda shape: pl.BlockSpec(shape, lambda i: (0, lax.max(i - lag, 0)))
+    tall, line = late((rows, LANES)), late((1, LANES))
     whole = lambda a: pl.BlockSpec(a.shape, lambda i: (0, 0), pipeline_mode=pl.Buffered(1))
     hbm = pl.BlockSpec(memory_space=pltpu.HBM)
     wide = pltpu.VMEM((steps, states, SUB, LANES), F32)
@@ -412,13 +421,13 @@
     cube = pltpu.VMEM((tiles, states, SUB, LANES), F32)
     small = pltpu.VMEM((tiles, states, LANES), F32)
     pair = pltpu.VMEM((rows, 2 * LANES), BF16)
-    buffers = scratch(tiles, chunk, 3 * tiles // 4, seq)
+    buffers = scratch(tiles, chunk, tiles // 2, seq)
     buffers[1] = pltpu.VMEM((3 * tiles // 4, chunk, LANES), BF16)
     return pl.pallas_call(
         functools.partial(scan_kernel, rank, states, chunk, rounds, seq),
-        grid=(2 * tiles,),
+        grid=(tiles + lag,),
         in_specs=[
-            tall, tall, tall, tall, whole(select), whole(decay_log), line, whole(normed), whole(upstream),
+            now, now, now, now, tall, tall, tall, tall, whole(select), whole(decay_log), line, whole(normed), whole(upstream),
         ],
         out_specs=[
             late((rows, LANES)), late((rows, LANES)), late((rows, LANES)), late((rows, LANES)),
@@ -434,14 +443,14 @@
             jax.ShapeDtypeStruct((1, inner), F32),
             jax.ShapeDtypeStruct((1, inner), F32),
             jax.ShapeDtypeStruct((rows, 2 * states), F32),
-            jax.ShapeDtypeStruct((width, first), BF16),
-            jax.ShapeDtypeStruct((first, width), BF16),
+            jax.ShapeDtypeStruct((width, gates), BF16),
+            jax.ShapeDtypeStruct((outs, width), BF16),
             jax.ShapeDtypeStruct((tiles - early, chunk, LANES), BF16),
         ],
         scratch_shapes=[
             wide, wide, wide, wide,
             pltpu.VMEM((steps + 1, states, SUB, LANES), F32), wide,
-            small, pltpu.VMEM((states, SUB, LANES), F32), thin, thin, thin, thin, thin,
+            small, pltpu.VMEM((states, SUB, LANES), F32), thin, thin, thin, thin, thin, thin,
             cube, cube, pltpu.VMEM((tiles, SUB, LANES), F32), pair, pair,
             pltpu.VMEM((tiles, 2 * states + SUB, LANES), F32),
             pltpu.VMEM((tiles, rounds, 2 * states + SUB, LANES), F32),
@@ -454,7 +463,7 @@
             collective_id=1, has_side_effects=True, vmem_limit_bytes=62 << 20
         ),
         name="span_scan",
-    )(pre, active, gate, graded, select, decay_log, skip, normed, upstream)
+    )(pre, active, gate, graded, pre, active, gate, graded, select, decay_log, skip, normed, upstream)
 
 
 def bit_of(index, step):
@@ -467,7 +476,7 @@
         return (place, lax.axis_index("seq"))
     return (lax.axis_index("dp"), place)
 
-CORE, X, Y, Z, ZZ = ("seq", 1), ("dp", 1), ("dp", 2), ("seq", 2), ("seq", 4)
+CORE, X, Y = ("seq", 1), ("dp", 1), ("dp", 2)
 
 def wait_rows(rows, sem):
     pltpu.make_async_copy(rows, rows, sem).wait()
@@ -490,29 +499,34 @@
 
 
 class Exchange:
+    levels = 4
+
     def __init__(self, acc, out, landing, extra, send_sem, recv_sem, rows, window, seq):
         self.acc, self.out, self.landing, self.extra = acc, out, landing, extra
         self.send_sem, self.recv_sem = send_sem, recv_sem
         self.rows, self.window = rows, window
-        self.more = [("seq", step) for step in (8 << i for i in range(12)) if step < seq]
-        self.orders = ((CORE, X, Y, Z, ZZ), (CORE, Y, X, Z, ZZ))
-        self.halvings = 5
-        self.phases = 2 * self.halvings + len(self.more)
-        quarter = rows // 4
-        core = bit_of(lax.axis_index("seq"), 1)
-        self.core_base = core * (rows // 2)
+        self.more = [("seq", 8 << i) for i in range(12) if (8 << i) < seq]
+        self.orders = ((CORE, X, Y), (CORE, Y, X))
+        self.back = self.levels + len(self.more)
+        self.phases = self.back + self.levels
+        place = lax.axis_index("seq")
+        self.quarter = (place // 2) % 4
+        self.core_base = bit_of(place, 1) * (rows // 2)
         self.kept = []
         for s, order in enumerate(self.orders):
-            base, size = core * (rows // 2) + s * quarter, quarter
+            base, size = self.core_base + s * (rows // 4), rows // 4
             spans = [(base, size)]
             for axis, step in order[1:]:
                 size = size // 2
                 base = base + bit_of(lax.axis_index(axis), step) * size
                 spans.append((base, size))
+            size = size // 4
+            spans.append((base + self.quarter * size, size))
             self.kept.append(spans)
 
     def partners(self):
-        return [other(*link) for link in (CORE, X, Y, Z, ZZ)] + [other(*link) for link in self.more]
+        links = [CORE, X, Y] + self.more
+        return [other(*link) for link in links] + [self.along(i) for i in range(1, 4)]
 
     def greet(self):
         barrier = pltpu.get_barrier_semaphore()
@@ -521,80 +535,101 @@
             pl.semaphore_signal(barrier, inc=1, device_id=device, device_id_type=MESH)
         pl.semaphore_wait(barrier, len(partners))
 
-    def sent(self, s, level):
-        base, size = self.kept[s][level]
-        axis, step = self.orders[s][level]
-        before = self.kept[s][level - 1][0]
-        mine = bit_of(lax.axis_index(axis), step)
-        return before + (1 - mine) * size, size
+    def along(self, i):
+        place = lax.axis_index("seq")
+        return (lax.axis_index("dp"), place + 2 * (lax.rem(self.quarter + i, 4) - self.quarter))
 
     def span(self, ref, k, base, size):
         return ref.at[k, pl.ds(pl.multiple_of(base, 16), size), :]
 
+    def land(self, p):
+        rows = self.rows
+        return [0, rows // 2, rows // 2 + rows // 4, rows // 2 + rows // 4 + rows // 8][p]
+
+    def rows_of(self, p):
+        rows, last = self.rows, self.phases - 1
+        if self.levels <= p < self.back:
+            return rows // 32
+        return [rows // 2, rows // 4, rows // 8, 6 * rows // 64][min(p, last - p)]
+
     def copies(self, k, p):
         w = lax.rem(k, self.window)
-        rows, levels, more = self.rows, self.halvings, len(self.more)
-        out = []
-        def copy(s, src, dst, link):
-            return pltpu.make_async_remote_copy(
-                src_ref=src, dst_ref=dst, send_sem=self.send_sem.at[w, p, s], recv_sem=self.recv_sem.at[w, p, s],
-                device_id=other(*link), device_id_type=MESH)
+        rows = self.rows
         if p == 0:
-            src = self.span(self.acc, k, rows // 2 - self.core_base, rows // 2)
-            return [copy(0, src, self.landing.at[w, pl.ds(0, rows // 2), :], CORE)]
-        if p == levels * 2 + more - 1:
+            return [(self.span(self.acc, k, rows // 2 - self.core_base, rows // 2),
+                     self.landing.at[w, pl.ds(0, rows // 2), :], other(*CORE))]
+        if p == self.phases - 1:
             half = self.span(self.out, k, self.core_base, rows // 2)
-            return [copy(0, half, half, CORE)]
+            return [(half, half, other(*CORE))]
+        found = []
         for s in range(2):
-            if p < levels:
-                base, size = self.sent(s, p)
-                dst = self.landing.at[w, pl.ds(self.land(p, s), size), :]
-                out.append(copy(s, self.span(self.acc, k, base, size), dst, self.orders[s][p]))
-            elif p < levels + more:
+            if p < self.levels - 1:
+                size = self.kept[s][p][1]
+                axis, step = self.orders[s][p]
+                base = self.kept[s][p - 1][0] + (1 - bit_of(lax.axis_index(axis), step)) * size
+                target = self.landing.at[w, pl.ds(self.land(p) + s * size, size), :]
+                found.append((self.span(self.acc, k, base, size), target, other(axis, step)))
+            elif p == self.levels - 1:
+                first, size = self.kept[s][p - 1][0], self.kept[s][p][1]
+                for i in range(1, 4):
+                    base = first + lax.rem(self.quarter + i, 4) * size
+                    target = self.landing.at[w, pl.ds(self.land(p) + (3 * s + i - 1) * size, size), :]
+                    found.append((self.span(self.acc, k, base, size), target, self.along(i)))
+            elif p < self.back:
                 base, size = self.kept[s][-1]
-                dst = self.extra.at[w, p - levels, pl.ds(s * size, size), :]
-                out.append(copy(s, self.span(self.acc, k, base, size), dst, self.more[p - levels]))
+                target = self.extra.at[w, p - self.levels, pl.ds(s * size, size), :]
+                found.append((self.span(self.acc, k, base, size), target, other(*self.more[p - self.levels])))
             else:
-                level = 2 * levels + more - 1 - p
+                level = self.phases - 1 - p
                 piece = self.span(self.out, k, *self.kept[s][level])
-                out.append(copy(s, piece, piece, self.orders[s][level]))
-        return out
-
-    def land(self, p, s):
-        size = self.rows // 4 >> p
-        start = self.rows // 2 + sum(2 * (self.rows // 4 >> q) for q in range(1, p))
-        return start + s * size
-
-    def add(self, k, base, source, first, size, target):
-        step = math.gcd(size, 128)
-        w = lax.rem(k, self.window)
+                devices = [self.along(i) for i in range(1, 4)] if level == 3 else [other(*self.orders[s][level])]
+                found += [(piece, piece, device) for device in devices]
+        return found
+
+    def add(self, k, base, size, sources, target):
+        step = min(size, 256)
+
         def body(i, _):
             here = pl.ds(pl.multiple_of(base + i * step, 16), step)
-            there = pl.ds(pl.multiple_of(first + i * step, 16), step)
-            target[k, here, :] = (self.acc[k, here, :].astype(F32) + source(w, there).astype(F32)).astype(BF16)
+            total = self.acc[k, here, :].astype(F32)
+            for ref, index, first in sources:
+                there = pl.ds(pl.multiple_of(first + i * step, 16), step)
+                total = total + ref[index + (there,)].astype(F32)
+            target[k, here, :] = total.astype(BF16)
             return 0
+
         lax.fori_loop(0, size // step, body, 0)
 
     def finish(self, k, p):
-        for copy in self.copies(k, p):
-            copy.wait()
-        levels, more = self.halvings, len(self.more)
-        target = self.out if p == levels + more - 1 else self.acc
-        landed = lambda w, there: self.landing[w, there, :]
+        w = lax.rem(k, self.window)
+        rows = self.acc.at[k, pl.ds(0, self.rows_of(p)), :]
+        copy = pltpu.make_async_remote_copy(
+            src_ref=rows, dst_ref=rows, send_sem=self.send_sem.at[w, p], recv_sem=self.recv_sem.at[w, p],
+            device_id=other(*CORE), device_id_type=MESH,
+        )
+        copy.wait_send()
+        copy.wait_recv()
+        target = self.out if p == self.back - 1 else self.acc
         if p == 0:
-            self.add(k, self.core_base, landed, 0, self.rows // 2, self.acc)
-        elif p < levels:
+            self.add(k, self.core_base, self.rows // 2, [(self.landing, (w,), 0)], target)
+        elif p < self.back:
             for s in range(2):
-                base, size = self.kept[s][p]
-                self.add(k, base, landed, self.land(p, s), size, target)
-        elif p < levels + more:
-            for s in range(2):
-                base, size = self.kept[s][-1]
-                self.add(k, base, lambda w, there: self.extra[w, p - levels, there, :], s * size, size, target)
+                base, size = self.kept[s][min(p, self.levels - 1)]
+                if p < self.levels - 1:
+                    sources = [(self.landing, (w,), self.land(p) + s * size)]
+                elif p < self.levels:
+                    sources = [(self.landing, (w,), self.land(p) + (3 * s + i) * size) for i in range(3)]
+                else:
+                    sources = [(self.extra, (w, p - self.levels), s * size)]
+                self.add(k, base, size, sources, target)
 
     def start(self, k, p):
-        for copy in self.copies(k, p):
-            copy.start()
+        w = lax.rem(k, self.window)
+        for source, target, device in self.copies(k, p):
+            pltpu.make_async_remote_copy(
+                src_ref=source, dst_ref=target, send_sem=self.send_sem.at[w, p], recv_sem=self.recv_sem.at[w, p],
+                device_id=device, device_id_type=MESH,
+            ).start()
 
     def advance(self, k, p):
         if p > 0:
@@ -603,27 +638,27 @@
             self.start(k, p)
 
     def state(self, k, p):
-        levels, more, rows = self.halvings, len(self.more), self.rows
+        rows = self.rows
         if p == 0:
             return [(self.acc, 0, rows)]
         if p == self.phases:
             return [(self.out, 0, rows)]
-        sending = p < levels + more
-        level = min(p - 1, levels - 1) if sending else 2 * levels + more - 1 - p
+        level = min(p - 1, self.levels - 1) if p < self.back else self.phases - 1 - p
         spans = [(self.core_base, rows // 2)] if level == 0 else [self.kept[s][level] for s in range(2)]
-        return [(self.acc if sending else self.out, base, size) for base, size in spans]
+        return [(self.acc if p < self.back else self.out, base, size) for base, size in spans]
+
 
 def scratch(chunks, rows, window, seq):
     more = len([1 for i in range(12) if (8 << i) < seq])
-    phases = 10 + more
     return [
         pltpu.VMEM((chunks, rows, LANES), BF16),
         pltpu.VMEM((chunks, rows, LANES), BF16),
         pltpu.VMEM((window, rows, LANES), BF16),
         pltpu.VMEM((window, max(more, 1), rows // 32, LANES), BF16),
-        pltpu.SemaphoreType.DMA((window, phases, 2)),
-        pltpu.SemaphoreType.DMA((window, phases, 2)),
+        pltpu.SemaphoreType.DMA((window, 8 + more)),
+        pltpu.SemaphoreType.DMA((window, 8 + more)),
     ]
+
 
 def tail_kernel(
     rank, states, chunk, seq,
@@ -688,7 +723,7 @@
 
         @pl.when((k < old) & (lax.rem(k + early, 2) == 0))
         def _():
-            store_lanes(out.at[k], gate_rest, pair - early // 2, store_sem.at[k])
+            store_lanes(out.at[k], gate_rest, pair - (early + 1) // 2, store_sem.at[k])
 
         @pl.when((k < old) & (lax.rem(k + early, 2) == 1))
         def _():
@@ -713,28 +748,27 @@
         def _():
             pltpu.make_async_copy(out.at[k], mixed_sum, store_sem.at[k]).start()
 
-    def old_turns():
-        for spot in range(3):
-            slot = 3 * (tiles + step) + spot
-            for p, shift in turns(ex.phases, spot):
-                k = tiles + step + shift - early
-
-                @pl.when((k >= 0) & (k < old))
-                def _():
-                    if p > 0:
-
-                        @pl.when(slot >= 3 * tiles + 2)
-                        def _():
-                            ex.finish(k, p - 1)
-
-                    if p < ex.phases:
-                        ex.start(k, p)
-                    else:
-                        store(k)
-
-    def new_turns():
+    def old_turns(spot):
+        slot = 2 * (tiles + step) + spot
+        for p, shift in turns(ex.phases, spot):
+            k = tiles + step + shift - early
+
+            @pl.when((k >= 0) & (k < old))
+            def _():
+                if p > 0:
+
+                    @pl.when(slot > 2 * tiles + 1)
+                    def _():
+                        ex.finish(k, p - 1)
+
+                if p < ex.phases:
+                    ex.start(k, p)
+                else:
+                    store(k)
+
+    def new_turns(turn):
         for p in range(ex.phases, -1, -1):
-            k = old + step - 2 * p
+            k = old + turn - 2 * p
 
             @pl.when((k >= old) & (k < count))
             def _():
@@ -754,7 +788,7 @@
         greet()
         dlow = contract_cols(dprelow_ref[...], step_weight_ref[...])
         dselect_scr[...] = jnp.concatenate([dlow, dpair_ref[...]], axis=1).astype(BF16)
-        some = contract_cols(dselect_scr[: halo * SUB], select_weight_ref[...])
+        some = jnp.dot(dselect_scr[: halo * SUB], select_weight_ref[...], preferred_element_type=F32)
         some = (dactive_first_ref[...] + some) * silu_slope(mixed_first_ref[...])
         for i in range(halo):
             first_scr[i : i + 1, :] = some[i * SUB : i * SUB + 1, :]
@@ -777,7 +811,7 @@
         for k in range(old):
             wait_rows(acc.at[k, pl.ds(0, sizes[k]), :], load_sem.at[k])
 
-    old_turns()
+    old_turns(0)
 
     @pl.when(step < pairs)
     def _():
@@ -785,7 +819,7 @@
         add(dnormed_scr, contract_cols(dgate_ref[...], gate_weight_ref[...]))
         lanes = pl.ds(pl.multiple_of(step * tall, tall), tall)
         mixed = mixed_ref[...]
-        back = contract_cols(dselect_scr[...], select_tile_ref[...])
+        back = jnp.dot(dselect_scr[...], select_tile_ref[...], preferred_element_type=F32)
         dmixed = (dactive_ref[...] + back) * silu_slope(mixed)
         spread_scr[:rows] = dmixed
         extended_scr[: halo * SUB] = halo_ref[...].astype(F32)
@@ -795,8 +829,11 @@
             misc_scr[i : i + 1, lanes] = jnp.sum(
                 dmixed * extended_scr[i * SUB : i * SUB + rows], axis=0, keepdims=True
             )
-        wide = contract_rows(active_ref[...], dselect_scr[...]).astype(BF16)
-        acc[wide_at, pl.ds(pl.multiple_of(step * tall, tall), tall), : wide.shape[1]] = wide
+        wide = contract_rows(dselect_scr[...], active_ref[...]).astype(BF16)
+        columns = wide.shape[0]
+        for side in range(2):
+            at = pl.ds(pl.multiple_of((2 * step + side) * columns, columns), columns)
+            acc[wide_at, at, :] = wide[:, side * LANES : (side + 1) * LANES]
         part = contract_rows(select_ref[:, :rank], dprelow_ref[:, lanes]).astype(BF16)
         for side in range(2):
             at = pl.ds(pl.multiple_of((2 * step + side) * rank, rank), rank)
@@ -876,10 +913,16 @@
                 dinputs_ref[i * span : (i + 1) * span, lanes] = dnormed_scr[b, every, :]
                 output_ref[i * span : (i + 1) * span, lanes] = result_scr[b, every, :].astype(BF16)
 
-    new_turns()
+    old_turns(1)
+    new_turns(step)
 
     @pl.when(step == pl.num_programs(0) - 1)
     def _():
+        def rest(turn, _):
+            new_turns(turn)
+            return 0
+
+        lax.fori_loop(pairs + 3, pairs + 3 + 2 * ex.phases, rest, 0)
         for k in range(count):
             wait_rows(out.at[k], store_sem.at[k])
 
@@ -893,7 +936,7 @@
     rank, states = step_weight.shape[0], d_rate.shape[0]
     chunk = 2 * width
     tiles, pairs, tall = inner // LANES, inner // (2 * LANES), 2 * LANES
-    phases = 10 + max(seq.bit_length() - 4, 0)
+    phases = 8 + max(seq.bit_length() - 4, 0)
     early = done_early(tiles, phases)
     count = tiles - early + pairs + 3
     some = halo.shape[0]
@@ -904,15 +947,15 @@
     high = lambda wide: pl.BlockSpec((tall, wide), lambda i: (at(i), 0))
     hbm = pl.BlockSpec(memory_space=pltpu.HBM)
     fixed = pl.BlockSpec((rows, width), lambda i: (0, 0))
-    rest = (tiles - early) * LANES
+    gates, outs = inner - (early + 1) // 2 * tall, inner - early // 2 * tall
     return pl.pallas_call(
         functools.partial(tail_kernel, rank, states, chunk, seq),
-        grid=(pairs + 3 + 2 * phases,),
+        grid=(pairs + 3,),
         in_specs=[
             whole(d_pre_low), whole(select), whole(d_pair), whole(step_weight), whole(normed), whole(upstream),
             whole(inputs), whole(scale), whole(ids), whole(gain), first, first, whole(select_weight), tile(some),
             whole(d_rate), whole(d_bias), whole(d_skip), tile(rows), tile(rows), tile(rows), tile(rows),
-            high(select_weight.shape[1]), tile(conv_weight.shape[0]), tile(width),
+            tile(select_weight.shape[0]), tile(conv_weight.shape[0]), tile(width),
             pl.BlockSpec((width, tall), lambda i: (0, at(i) + pairs)), tile(rows), tile(rows), high(width), hbm,
         ],
         out_specs=[fixed, fixed, hbm, hbm, hbm, hbm, hbm, hbm],
@@ -920,8 +963,8 @@
             jax.ShapeDtypeStruct((rows, width), BF16),
             jax.ShapeDtypeStruct((rows, width), F32),
             jax.ShapeDtypeStruct((width, inner), BF16),
-            jax.ShapeDtypeStruct((width, rest), BF16),
-            jax.ShapeDtypeStruct((rest, width), BF16),
+            jax.ShapeDtypeStruct((width, gates), BF16),
+            jax.ShapeDtypeStruct((outs, width), BF16),
             jax.ShapeDtypeStruct((vocab, width), BF16),
             jax.ShapeDtypeStruct((chunk, LANES), BF16),
             jax.ShapeDtypeStruct((chunk, LANES), BF16),
@@ -933,7 +976,7 @@
             pltpu.VMEM((width // LANES, rows, LANES), F32), pltpu.VMEM((width // LANES, rows, LANES), F32),
             pltpu.VMEM((16, inner), F32), pltpu.VMEM((1, width), F32),
         ]
-        + scratch(count, chunk, count, seq)
+        + scratch(count, chunk, 8, seq)
         + [
             pltpu.SemaphoreType.DMA((count,)), pltpu.SemaphoreType.DMA((count,)),
             pltpu.SemaphoreType.DMA, pltpu.SemaphoreType.DMA,
@@ -947,6 +990,77 @@
         select_weight, halo, d_rate, d_bias, d_skip, d_active, mixed, front, active, select_weight, conv_weight,
         input_weight, input_weight, d_gate, gated, output_weight, handed,
     )
+
+
+def widen_kernel(
+    rank, states, columns, outs,
+    front_ref, gate_ref, gate_rest_ref, out_ref, out_rest_ref, embedding_ref, wide_ref, mixed_ref,
+    input_to, output_to, embedding_to, select_to, step_to, decay_to, conv_to, gain_to, *line_to,
+):
+    step = pl.program_id(0)
+    inner, gates = front_ref.shape[1], gate_ref.shape[1]
+    input_to[:, :inner] = front_ref[...].astype(F32)
+    input_to[:, inner : inner + gates] = gate_ref[...].astype(F32)
+    input_to[:, inner + gates :] = gate_rest_ref[...].astype(F32)
+
+    @pl.when(step < outs)
+    def _():
+        output_to[...] = out_ref[...].astype(F32)
+
+    @pl.when(step >= outs)
+    def _():
+        output_to[...] = out_rest_ref[...].astype(F32)
+
+    embedding_to[...] = embedding_ref[...].astype(F32)
+
+    @pl.when(step == 0)
+    def _():
+        for source, whole in (
+            (wide_ref, ((select_to, columns),)),
+            (mixed_ref, ((step_to, rank), (decay_to, states), (conv_to, 16), (gain_to, 16))),
+        ):
+            at = 0
+            for to, height in whole:
+                for b in range(to.shape[1] // LANES):
+                    part = source[at : at + height, :].astype(F32)
+                    lanes = slice(b * LANES, (b + 1) * LANES)
+                    to[:, lanes] = part[: to.shape[0]]
+                    if to is conv_to:
+                        for i, line in enumerate(line_to):
+                            line[:, lanes] = part[to.shape[0] + i : to.shape[0] + i + 1]
+                    at += height
+
+
+def run_widen(front, gate, gate_rest, out, out_rest, embedding, wide, mixed, rank, states, columns, kernel):
+    width, inner = front.shape
+    tall = 2 * LANES
+    tiles, outs = inner // tall, out.shape[0] // tall
+    vocab = embedding.shape[0]
+    lines = lambda a: pl.BlockSpec((width // tiles, a.shape[1]), lambda i: (i, 0))
+    thin = pl.BlockSpec((vocab // tiles, width), lambda i: (i, 0))
+    fixed = lambda shape: pl.BlockSpec(shape, lambda i: (0, 0))
+    shapes = [
+        (width, 2 * inner), (inner, width), (vocab, width), (columns, inner), (rank, inner), (states, inner), (kernel, inner),
+        (1, width), (1, inner), (1, inner), (1, inner),
+    ]
+    return pl.pallas_call(
+        functools.partial(widen_kernel, rank, states, columns, outs),
+        grid=(tiles,),
+        in_specs=[
+            lines(front), lines(gate), lines(gate_rest),
+            pl.BlockSpec((tall, width), lambda i: (lax.min(i, outs - 1), 0)),
+            pl.BlockSpec((tall, width), lambda i: (lax.max(i - outs, 0), 0)),
+            thin, fixed(wide.shape), fixed(mixed.shape),
+        ],
+        out_specs=[
+            pl.BlockSpec((width // tiles, 2 * inner), lambda i: (i, 0)),
+            pl.BlockSpec((tall, width), lambda i: (i, 0)), thin,
+        ]
+        + [fixed(shape) for shape in shapes[3:]],
+        out_shape=[jax.ShapeDtypeStruct(shape, F32) for shape in shapes],
+        compiler_params=pltpu.CompilerParams(vmem_limit_bytes=62 << 20),
+        name="sums_to_float32",
+    )(front, gate, gate_rest, out, out_rest, embedding, wide, mixed)
 
 
 def on_device(
@@ -1004,31 +1118,30 @@
     )
     output, d_inputs, front_sum, gate_rest, out_rest, embedding_sum, wide_sum, mixed_sum = run_tail(
         d_pre_low, select, d_pair, step_weight, turned, upstream, block_inputs, scale, ids, norm_gain.reshape(1, width),
-        d_active, mixed, select_weight, earlier, d_rate, d_bias, d_skip, front, active, conv_weight,
+        d_active, mixed, select_weight.T, earlier, d_rate, d_bias, d_skip, front, active, conv_weight,
         input_projection_weight, d_gate, gated, output_projection_weight, handed, vocab, seq,
     )
-    tiles = inner // LANES
-
-    def unpacked(first, height, blocks):
-        part = mixed_sum[first : first + height * blocks].astype(F32).reshape(blocks, height, LANES)
-        return part.swapaxes(0, 1).reshape(height, blocks * LANES)
-
-    at = (rank + states) * tiles
-    misc = unpacked(at, 16, tiles)
+    (
+        d_input_weight, d_output_weight, d_embedding, d_select_weight, d_step_weight, d_decay_log, d_conv_weight,
+        d_norm_gain, d_conv_bias, d_step_bias, d_skip_gain,
+    ) = run_widen(
+        front_sum, gate_sum, gate_rest, out_sum, out_rest, embedding_sum, wide_sum, mixed_sum, rank, states,
+        select_weight.shape[1], kernel,
+    )
     return (
         output.reshape(count, stretch, width),
         d_inputs.reshape(count, stretch, width),
-        embedding_sum.astype(F32),
-        unpacked(at + 16 * tiles, 16, width // LANES)[0],
-        jnp.concatenate([front_sum, gate_sum, gate_rest], axis=1).astype(F32),
-        misc[:kernel],
-        misc[kernel],
-        wide_sum[:, : select_weight.shape[1]].astype(F32),
-        unpacked(0, rank, tiles),
-        misc[kernel + 1],
-        unpacked(rank * tiles, states, tiles),
-        misc[kernel + 2],
-        jnp.concatenate([out_sum, out_rest], axis=0).astype(F32),
+        d_embedding,
+        d_norm_gain[0],
+        d_input_weight,
+        d_conv_weight,
+        d_conv_bias[0],
+        d_select_weight.T,
+        d_step_weight,
+        d_step_bias[0],
+        d_decay_log,
+        d_skip_gain[0],
+        d_output_weight,
     )
 
 

time: 317 us -> 277 us (0.87)
  other arithmetic: 25.7 us -> 7.02 us
  Pallas kernels: 251 us -> 233 us
  local copies, waits for them, and re-layouts: 17.1 us -> 12.9 us
    pallas_call x1, Pallas kernels: 114 us -> 88.8 us  [run_tail(): pl.pallas_call(functools.partial(tail_kernel, rank, states, chunk, seq),...]
    convert_element_type x4 -> x0, other arithmetic: 16.6 us -> none  [the longest x1 6.92 us: on_device(): jnp.concatenate([out_sum, out_rest], axis=0).astype(F32)]
    pallas_call x0 -> x1, Pallas kernels: none -> 15.7 us  [run_widen(): pl.pallas_call(functools.partial(widen_kernel, rank, states, columns, out...]
    pallas_call x1, Pallas kernels: 137 us -> 129 us  [run_scan(): pl.pallas_call(functools.partial(scan_kernel, rank, states, chunk, rounds...]
    slice x5 -> x0, local copies, waits for them, and re-layouts: 3.85 us -> none  [the longest x3 2.61 us: unpacked(): mixed_sum[first:first + height * blocks].astype(F32)]
    unnamed x52 -> x42, local copies, waits for them, and re-layouts: 6.46 us -> 6.08 us
  transfers between devices with their start and end apart: 1 -> 1, of which waited for: 0 -> 0; matrix products, arithmetic and copies ran while one was open for 5% -> 6% of each run, Pallas kernels for 0% -> 0%
where the time goes in v2:
time: 277 us; the launch traced here: 276 us
  Pallas kernels  233 us (84%)
  matrix products  19.4 us (7%)
  local copies, waits for them, and re-layouts  12.9 us (5%)
  other arithmetic  7.02 us (3%)
    pallas_call x1, Pallas kernels, run_scan(): pl.pallas_call(functools.partial(scan_kernel, rank, states, chunk, rounds...  129 us
    pallas_call x1, Pallas kernels, run_tail(): pl.pallas_call(functools.partial(tail_kernel, rank, states, chunk, seq),...  88.8 us
    pallas_call x1, Pallas kernels, run_widen(): pl.pallas_call(functools.partial(widen_kernel, rank, states, columns, out...  15.7 us
    unnamed x42, local copies, waits for them, and re-layouts  6.08 us
  transfers between devices with their start and end apart: 1, of which 0 were waited for; matrix products, arithmetic and copies ran while one was open for 6% of the time, Pallas kernels for 0%

profile of v2, /device:TPU:0, one launch (start us, length us, event | category | flops | bytes accessed | tf_op | source)
XLA Modules:
  0.0 276.5 jit_solution(677217714890477126)
XLA Ops:
  0.6 0.0 copy-start
  0.7 0.0 copy-start.16
  0.7 0.5 broadcast.35
  1.2 1.3 reduce.3
  2.5 0.1 reshape_reshape.6
  2.6 0.1 copy.31
  2.7 0.1 eq.15
  2.8 0.6 multiply_reduce_fusion
  3.4 2.0 copy.32
  5.4 0.0 copy-done.16
  5.4 5.5 %fusion.8.front_ref = bf16[512,2048]{1,0:T(8,128)(2,1)S(1)} fusion(bf16[1024,4096]{1,0:T(8,128)(2,1)} %gate_weight_ref.1, f32[512,1024]{0,1:T(8,128)} %copy.32, f32[1024]{0:T(1024)S(1)} %copy-done.16, f32[512]{0:T(512)S(1)} %add_rsqrt_fusion), kind=kOutput, calls=%fused_computation.14 | convolution fusion | flops 2150105088 | bytes 8394752 | tf_op jit(solution)/shard_map/dot_general | solution.py:1093
  10.8 0.0 copy-done.4
  10.9 0.0 copy-start.5
  10.9 0.0 copy-start.15
  11.0 0.0 copy-start.8
  11.0 0.0 copy-start.12
  11.0 2.8 collective-permute-start
  13.7 0.0 copy-done.3
  13.7 5.4 %fusion.11.gate_now.gate_ref = bf16[512,2048]{1,0:T(8,128)(2,1)} fusion(bf16[1024,4096]{1,0:T(8,128)(2,1)S(1)} %copy-done.3, f32[512,1024]{0,1:T(8,128)} %copy.32, f32[1024]{0:T(1024)S(1)} %copy-done.16, f32[512]{0:T(512)S(1)} %add_rsqrt_fusion), kind=kOutput, calls=%fused_computation.15 | convolution fusion | flops 2150105088 | bytes 8394752 | tf_op jit(solution)/shard_map/dot_general | solution.py:1096
  19.2 0.0 copy-done.5
  19.2 0.0 copy-done.8
  19.2 0.0 copy-done.12
  19.2 0.0 copy-start.7
  19.2 4.6 %fusion.17.graded_now.graded_ref = f32[512,2048]{1,0:T(8,128)} fusion(bf16[2048,1024]{1,0:T(8,128)(2,1)S(1)} %copy-done.8, bf16[8,64,1024]{2,1,0:T(8,128)(2,1)S(1)} %bitcast.51), kind=kOutput, calls=%fused_computation.29 | convolution fusion | flops 2147483648 | bytes 9437184 | tf_op jit(solution)/shard_map/dot_general | solution.py:39
  23.8 0.0 copy-done.7
  23.8 1.2 fusion.27.normed_ref
  25.0 0.8 reshape.80.ids_ref
  25.9 2.8 %copy.44 = bf16[8,64,1024]{2,0,1:T(8,128)(2,1)} copy(bf16[8,64,1024]{2,1,0:T(8,128)(2,1)} %bitcast.50) | data formatting | bytes 2097152 | tf_op jit(solution)/shard_map/reshape;reshape | solution.py:46
  28.7 0.9 copy.37.scale_ref
  29.5 0.0 collective-permute-done
  29.5 0.1 maximum_bitcast_fusion.halo_ref
  29.6 0.6 maximum_convert_fusion
  30.2 0.0 copy-start.9
  30.2 0.0 copy-start.11
  30.2 0.0 copy-start.18
  30.2 3.8 %multiply_convert_fusion = (bf16[512,2048]{1,0:T(8,128)(2,1)S(1)}, f32[512,2048]{1,0:T(8,128)}) fusion(f32[536,2048]{1,0:T(8,128)S(1)} %maximum_convert_fusion, f32[2048]{0:T(1024)S(1)} %bitcast.59, f32[2048]{0:T(1024)S(1)} %bitcast.57, f32[2048]{0:T(1024)S(1)} %bitcast.58, f32[2048]{0:T(1024)S(1)} %bitcast.56, f32[2048]{0:T(1024)S(1)} %copy-done.17), kind=kLoop, calls=%fused_computation.10 | loop fusion | flops 13631488 | bytes 23109632 | tf_op jit(solution)/shard_map/convert_element_type | solution.py:1106
  34.1 0.0 copy-done.14
  34.1 1.3 copy-done.2
  35.4 0.7 convolution_convert_fusion.select_ref
  36.1 0.0 copy-start.10
  36.1 2.7 convolution_add_fusion.pre_now.pre_ref
  38.8 0.0 copy-done.10
  38.8 128.9 %span_scan.1 = (bf16[512,2048]{1,0:T(8,128)(2,1)}, bf16[512,2048]{1,0:T(8,128)(2,1)}, bf16[512,2048]{1,0:T(8,128)(2,1)}, f32[512,2048]{1,0:T(8,128)}, f32[16,204...) custom-call(f32[512,2048]{1,0:T(8,128)} %convolution_add_fusion.pre_, ...), custom_call_target="tpu_custom_call" | custom-call | tf_op jit(solution)/shard_map/span_scan/pallas_call | solution.py:426
  167.8 88.8 %span_tail.1 = (bf16[512,1024]{1,0:T(8,128)(2,1)}, f32[512,1024]{1,0:T(8,128)}, bf16[1024,2048]{1,0:T(8,128)(2,1)}, bf16[1024,1024]{1,0:T(8,128)(2,1)}, bf16[128...) custom-call(bf16[512,2048]{1,0:T(8,128)(2,1)} %get-tuple-element.43.dprel, ...), custom_call_target="tpu_custom_call" | custom-call | tf_op jit(solution)/shard_map/span_tail/pallas_call | solution.py:951
  256.6 0.0 copy-start.1
  256.7 15.7 %sums_to_float32.1 = (f32[1024,4096]{1,0:T(8,128)}, f32[2048,1024]{1,0:T(8,128)}, f32[256,1024]{1,0:T(8,128)}, f32[96,2048]{1,0:T(8,128)}, f32[64,2048]{1,0:T(8,...) custom-call(bf16[1024,2048]{1,0:T(8,128)(2,1)} %get-tuple-element.54, ...), custom_call_target="tpu_custom_call" | custom-call | tf_op jit(solution)/shard_map/sums_to_float32/pallas_call | solution.py:1046
  272.4 1.0 copy.48
  273.3 3.2 %copy.49 = f32[1,512,1024]{2,1,0:T(8,128)} copy(f32[1,512,1024]{2,1,0:T(8,128)} %bitcast.47) | data formatting | bytes 4194304
  (22 shorter events, 0.1 us)
Async XLA Ops:
  0.6 2.1 copy-start
  0.7 4.7 %copy-start.16 = (f32[1024]{0:T(1024)S(1)}, f32[1024]{0:T(1024)}, u32[]{:S(2)}) copy-start(f32[1024]{0:T(1024)} %param.16) | copy-start | bytes 12292
  3.4 7.5 %copy-start.4 = (f32[512,1024]{1,0:T(8,128)}, f32[512,1024]{1,0:T(8,128)S(1)}, u32[]{:S(2)}) copy-start(f32[512,1024]{1,0:T(8,128)S(1)} %get-tuple-element.80.inputs_ref) | copy-start | bytes 6291460
  5.4 8.4 %copy-start.3 = (bf16[1024,4096]{1,0:T(8,128)(2,1)S(1)}, bf16[1024,4096]{1,0:T(8,128)(2,1)}, u32[]{:S(2)}) copy-start(bf16[1024,4096]{1,0:T(8,128)(2,1)} %gate_weight_ref.1) | copy-start | bytes 25165828
  10.9 8.3 %copy-start.5 = (bf16[512,2048]{1,0:T(8,128)(2,1)}, bf16[512,2048]{1,0:T(8,128)(2,1)S(1)}, u32[]{:S(2)}) copy-start(bf16[512,2048]{1,0:T(8,128)(2,1)S(1)} %fusion.8.front_ref) | copy-start | bytes 6291460
  10.9 8.2 %copy-start.15 = (f32[4,2048]{1,0:T(4,128)S(1)}, f32[4,2048]{1,0:T(4,128)}, u32[]{:S(2)}) copy-start(f32[4,2048]{1,0:T(4,128)} %conv_ref.1) | copy-start | bytes 98308
  11.0 8.2 %copy-start.8 = (bf16[2048,1024]{1,0:T(8,128)(2,1)S(1)}, bf16[2048,1024]{1,0:T(8,128)(2,1)}, u32[]{:S(2)}) copy-start(bf16[2048,1024]{1,0:T(8,128)(2,1)} %out_weight_ref.1) | copy-start | bytes 12582916
  11.0 8.2 %copy-start.12 = (bf16[1,512,1024]{2,1,0:T(8,128)(2,1)S(1)}, bf16[1,512,1024]{2,1,0:T(8,128)(2,1)}, u32[]{:S(2)}) copy-start(bf16[1,512,1024]{2,1,0:T(8,128)(2,1)} %param.15) | copy-start | bytes 3145732
  11.0 18.5 %collective-permute-start = (bf16[3,2048]{1,0:T(4,128)(2,1)S(1)}, bf16[3,2048]{1,0:T(4,128)(2,1)S(1)}, u32[]{:S(2)}, u32[]{:S(2)}) collective-permute-start(bf16[3,2048]{1,0:T(4,128)(2,1)S(1)} %bitcast.62), channel_id=1, source_target_pairs={{0,1},{1,2},{2,3},{3,4},{4,5},{5,6},{6,7},{8,9},{9,10},{10,11},{11... | collective-permute-start | bytes 36872 | tf_op jit(solution)/shard_map/ppermute | solution.py:24
  19.2 4.6 %copy-start.7 = (f32[512,1024]{0,1:T(8,128)S(1)}, f32[512,1024]{0,1:T(8,128)}, u32[]{:S(2)}) copy-start(f32[512,1024]{0,1:T(8,128)} %copy.32) | copy-start | bytes 6291460
  23.8 5.8 %copy-start.6 = (bf16[512,2048]{1,0:T(8,128)(2,1)S(1)}, bf16[512,2048]{1,0:T(8,128)(2,1)}, u32[]{:S(2)}) copy-start(bf16[512,2048]{1,0:T(8,128)(2,1)} %copy-done.5) | copy-start | bytes 6291460
  25.9 4.3 %copy-start.17 = (f32[2048]{0:T(1024)S(1)}, f32[2048]{0:T(1024)}, u32[]{:S(2)}) copy-start(f32[2048]{0:T(1024)} %param.19) | copy-start | bytes 24580
  29.6 4.5 %copy-start.14 = (bf16[24,2048]{1,0:T(8,128)(2,1)}, bf16[24,2048]{1,0:T(8,128)(2,1)S(1)}, u32[]{:S(2)}) copy-start(bf16[24,2048]{1,0:T(8,128)(2,1)S(1)} %maximum_bitcast_fusion.halo_ref) | copy-start | bytes 294916
  30.2 5.2 %copy-start.9 = (bf16[2048,96]{0,1:T(8,128)(2,1)S(1)}, bf16[2048,96]{0,1:T(8,128)(2,1)}, u32[]{:S(2)}) copy-start(bf16[2048,96]{0,1:T(8,128)(2,1)} %param.20) | copy-start | bytes 1179652
  30.2 5.9 %copy-start.11 = (bf16[64,2048]{1,0:T(8,128)(2,1)S(1)}, bf16[64,2048]{1,0:T(8,128)(2,1)}, u32[]{:S(2)}) copy-start(bf16[64,2048]{1,0:T(8,128)(2,1)} %step_weight_ref.1) | copy-start | bytes 786436
  30.2 5.9 %copy-start.18 = (f32[2048]{0:T(1024)S(1)}, f32[2048]{0:T(1024)}, u32[]{:S(2)}) copy-start(f32[2048]{0:T(1024)} %param.22) | copy-start | bytes 24580
  34.1 1.3 copy-start.2
  36.1 2.7 copy-start.10
  256.6 15.7 %copy-start.13 = (bf16[512,1024]{1,0:T(8,128)(2,1)S(1)}, bf16[512,1024]{1,0:T(8,128)(2,1)}, u32[]{:S(2)}) copy-start(bf16[512,1024]{1,0:T(8,128)(2,1)} %get-tuple-element.52) | copy-start | bytes 3145732
  256.6 19.8 %copy-start.1 = (bf16[256,1024]{1,0:T(8,128)(2,1)S(1)}, bf16[256,1024]{1,0:T(8,128)(2,1)}, u32[]{:S(2)}) copy-start(bf16[256,1024]{1,0:T(8,128)(2,1)} %param.14) | copy-start | bytes 1572868

commit v3 on v2

--- a/solution.py
+++ b/solution.py
@@ -18,12 +18,6 @@
 MESH = pl.DeviceIdType.MESH
 
 
-def passed_along(value, axis, by):
-    peers = lax.axis_size(axis)
-    pairs = [(i, i + by) for i in range(peers) if 0 <= i + by < peers]
-    return lax.ppermute(value, axis, pairs)
-
-
 def silu_slope(value):
     sigma = jax.nn.sigmoid(value)
     return sigma * (1.0 + value * (1.0 - sigma))
@@ -39,16 +33,6 @@
     return lax.dot_general(
         left, right, (((1,), (1,)), ((), ())), preferred_element_type=F32
     )
-
-
-def to_spans(array):
-    rows = array.shape[0]
-    return array.reshape(SUB, rows // SUB, -1).swapaxes(0, 1).reshape(rows, -1)
-
-
-def from_spans(array):
-    rows = array.shape[0]
-    return array.reshape(rows // SUB, SUB, -1).swapaxes(0, 1).reshape(rows, -1)
 
 
 def sublane(shape):
@@ -80,16 +64,160 @@
     return value[0]
 
 
+def front_kernel(
+    seq,
+    ids_ref, embedding_ref, cotangent_ref, gain_ref, front_weight_ref, gate_weight_ref, out_weight_ref, conv_ref,
+    conv_bias_ref, select_weight_ref,
+    inputs_ref, scale_ref, normed_ref, turned_ref, upstream_ref, hot_ref, front_ref, halo_ref, mixed_ref, active_ref,
+    gate_ref, graded_ref, select_ref,
+    last_scr, extended_scr, total_scr, send_sem, recv_sem,
+):
+    step = pl.program_id(0)
+    rows, width = upstream_ref.shape
+    span = rows // SUB
+    vocab = embedding_ref.shape[0]
+    kernel = conv_ref.shape[0]
+    halo = kernel - 1
+    place = lax.axis_index("seq")
+
+    def there(by):
+        return (lax.axis_index("dp"), place + by)
+
+    def copy():
+        return pltpu.make_async_remote_copy(
+            src_ref=ids_ref.at[:, pl.ds(rows - LANES, LANES)], dst_ref=last_scr, send_sem=send_sem, recv_sem=recv_sem,
+            device_id=there(1), device_id_type=MESH,
+        )
+
+    def norm(inputs):
+        scale = lax.rsqrt(jnp.sum(inputs * inputs, axis=1, keepdims=True) * (1.0 / width) + EPS)
+        return scale, (inputs * scale * gain_ref[...]).astype(BF16)
+
+    def hot_of(ids):
+        shape = (vocab, ids.shape[1])
+        return (lax.broadcasted_iota(jnp.int32, shape, 0) == ids).astype(F32).astype(BF16)
+
+    @pl.when(step == 0)
+    def _():
+        barrier = pltpu.get_barrier_semaphore()
+
+        @pl.when(place > 0)
+        def _():
+            pl.semaphore_signal(barrier, inc=1, device_id=there(-1), device_id_type=MESH)
+
+        @pl.when(place == 0)
+        def _():
+            last_scr[...] = jnp.full(last_scr.shape, -1, jnp.int32)
+
+        row = lax.broadcasted_iota(jnp.int32, (rows, rows), 0)
+        position = lax.broadcasted_iota(jnp.int32, (rows, rows), 1)
+        order = (lax.rem(row, SUB) * span + row // SUB == position).astype(F32).astype(BF16)
+        upstream_ref[...] = jnp.dot(order, cotangent_ref[...], preferred_element_type=F32).astype(BF16)
+
+        @pl.when(place < seq - 1)
+        def _():
+            pl.semaphore_wait(barrier, 1)
+            copy().start()
+
+        hot = contract_cols(hot_of(ids_ref[...]), order).astype(BF16)
+        hot_ref[...] = hot
+        inputs = contract_rows(hot, embedding_ref[...])
+        inputs_ref[...] = inputs
+        scale, normed = norm(inputs)
+        scale_ref[...] = scale
+        normed_ref[:rows] = normed
+        turned_ref[...] = normed.T
+
+        @pl.when(place < seq - 1)
+        def _():
+            copy().wait_send()
+
+        @pl.when(place > 0)
+        def _():
+            copy().wait_recv()
+
+        last = contract_rows(hot_of(last_scr[...]), embedding_ref[...])[LANES - 16 :]
+        normed_ref[rows:] = norm(last)[1]
+        total_scr[...] = jnp.zeros_like(total_scr)
+
+    both = jnp.dot(normed_ref[...], front_weight_ref[...], preferred_element_type=F32).astype(BF16)
+    front_ref[...] = both[:rows]
+    both = both.astype(F32)
+    extended_scr[halo * SUB :] = both[:rows]
+    sub = lax.broadcasted_iota(jnp.int32, (SUB, both.shape[1]), 0)
+    for i in range(halo):
+        own = pltpu.roll(both[rows - (halo - i) * SUB : rows - (halo - i - 1) * SUB], 1, 0)
+        before = both[rows + 16 - halo + i : rows + 16 - halo + i + 1]
+        extended_scr[i * SUB : (i + 1) * SUB] = jnp.where(sub > 0, own, before)
+    halo_ref[...] = extended_scr[: halo * SUB].astype(BF16)
+    mixed = conv_bias_ref[...] + conv_ref[0:1] * extended_scr[:rows]
+    for i in range(1, kernel):
+        mixed = mixed + conv_ref[i : i + 1] * extended_scr[i * SUB : i * SUB + rows]
+    mixed_ref[...] = mixed
+    active = jax.nn.silu(mixed).astype(BF16)
+    active_ref[...] = active
+    gate_ref[...] = jnp.dot(normed_ref[:rows], gate_weight_ref[...], preferred_element_type=F32).astype(BF16)
+    graded_ref[...] = contract_cols(upstream_ref[...], out_weight_ref[...])
+    total_scr[...] += contract_cols(active, select_weight_ref[...])
+
+    @pl.when(step == pl.num_programs(0) - 1)
+    def _():
+        select_ref[...] = total_scr[...].astype(BF16)
+
+
+def run_front(
+    ids, embedding, cotangent, gain, input_weight, output_weight, conv_weight, conv_bias, select_weight, seq
+):
+    rows, width = cotangent.shape
+    inner = output_weight.shape[0]
+    vocab, kernel, columns = embedding.shape[0], conv_weight.shape[0], select_weight.shape[0]
+    halo = (kernel - 1) * SUB
+    tall = 2 * LANES
+    pairs = inner // tall
+    whole = lambda a: pl.BlockSpec(a.shape, lambda i: (0, 0), pipeline_mode=pl.Buffered(1))
+    tile = lambda height: pl.BlockSpec((height, tall), lambda i: (0, i))
+    fixed = lambda shape: pl.BlockSpec(shape, lambda i: (0, 0))
+    outs = [
+        ((rows, width), F32, None), ((rows, 1), F32, None), ((rows + 16, width), BF16, None),
+        ((width, rows), BF16, None), ((rows, width), BF16, None), ((vocab, rows), BF16, None),
+        ((rows, inner), BF16, rows), ((halo, inner), BF16, halo), ((rows, inner), F32, rows), ((rows, inner), BF16, rows),
+        ((rows, inner), BF16, rows), ((rows, inner), F32, rows), ((rows, columns), BF16, None),
+    ]
+    return pl.pallas_call(
+        functools.partial(front_kernel, seq),
+        grid=(pairs,),
+        in_specs=[
+            whole(ids), whole(embedding), whole(cotangent), whole(gain), tile(width),
+            pl.BlockSpec((width, tall), lambda i: (0, i + pairs)), pl.BlockSpec((tall, width), lambda i: (i, 0)),
+            tile(kernel), tile(1), tile(columns),
+        ],
+        out_specs=[fixed(shape) if height is None else tile(height) for shape, kind, height in outs],
+        out_shape=[jax.ShapeDtypeStruct(shape, kind) for shape, kind, height in outs],
+        scratch_shapes=[
+            pltpu.VMEM((1, LANES), jnp.int32), pltpu.VMEM((rows + halo, tall), F32), pltpu.VMEM((rows, columns), F32),
+            pltpu.SemaphoreType.DMA, pltpu.SemaphoreType.DMA,
+        ],
+        compiler_params=pltpu.CompilerParams(
+            collective_id=3, has_side_effects=True, vmem_limit_bytes=62 << 20
+        ),
+        name="span_front",
+    )(
+        ids, embedding, cotangent, gain, input_weight, input_weight, output_weight, conv_weight, conv_bias, select_weight
+    )
+
+
 def slot_of(k, p):
-    return 2 * k + 3 + 2 * p
-
-
-def turns(phases, place):
-    return [(p, (place - 3 - 2 * p) // 2) for p in range(phases, -1, -1) if (place - 3 - 2 * p) % 2 == 0]
-
-
-def done_early(tiles, phases):
-    return sum(slot_of(k, phases) < 2 * tiles for k in range(tiles))
+    return 2 * k + 3 - k % 2 + 2 * p
+
+
+def turns(phases, tile, place):
+    for p in range(phases, -1, -1):
+        k = tile - 1 - p
+        yield k, p, (k >= 0) & (lax.rem(k + 2 * phases, 2) == 1 - place)
+
+
+def begun(tiles, p):
+    return sum(slot_of(k, p) < 2 * tiles for k in range(tiles))
 
 
 def next_phase(k, tiles):
@@ -144,27 +272,27 @@
 
 def scan_kernel(
     rank, states, chunk, rounds, seq,
-    pre_now, active_now, gate_now, graded_now, pre_ref, active_ref, gate_ref, graded_ref,
-    select_ref, decay_ref, skip_ref, normed_ref, upstream_ref,
-    gated_ref, dgate_ref, dprelow_ref, dactive_ref, drate_ref, dbias_ref, dskip_ref, dselect_ref,
+    active_now, gate_now, graded_now, select_ref, step_weight_ref, step_bias_ref, decay_ref, skip_ref, normed_ref, upstream_ref,
+    gated_ref, dgate_ref, dprelow_ref, dactive_ref, lines_ref, dselect_ref,
     gate_sum, out_sum, handed,
     inject_scr, readout_scr, dread_scr, dinject_scr, state_scr, factor_scr,
-    rates_scr, rate_scr, delta_scr, drive_scr, grad_scr, sigma_scr, scan_scr, weight_scr,
+    rates_scr, rate_scr, delta_ring, drive_ring, grad_ring, silu_ring, sway_ring, active_ring, slope_ring, scan_scr, weight_scr,
     ahead_scr, behind_scr, sums_scr, gated_scr, dgated_scr,
     totals, totals_in, start_scr, incoming_scr, gaps_scr, prefix_send, prefix_recv,
     acc, out, landing, extra, send_sem, recv_sem, store_sem,
 ):
-    rows = pre_ref.shape[0]
+    rows = active_now.shape[0]
     steps = rows // SUB
     step = pl.program_id(0)
     count = rates_scr.shape[0]
-    lag = rounds + 1
+    lag = delta_ring.shape[0]
+    per = -(-rounds // (lag - 1))
     width = upstream_ref.shape[1]
     prefix = Prefix(
         totals, totals_in, start_scr, incoming_scr, gaps_scr, rates_scr, prefix_send, prefix_recv, rounds
     )
     ex = Exchange(acc, out, landing, extra, send_sem, recv_sem, chunk, landing.shape[0], seq)
-    early = done_early(count, ex.phases)
+    early = begun(count, ex.phases)
     half, unroll = states // 2, 8
     halves = [pl.ds(0, half), pl.ds(half, half)]
 
@@ -180,11 +308,9 @@
             store_rows(out.at[k], out_sum, pair, store_sem.at[k])
 
     def take_turns(place):
-        c = step - lag
-        for p, shift in turns(ex.phases, place):
-            k = c + shift
-
-            @pl.when(k >= 0)
+        for k, p, now in turns(ex.phases, step - lag, place):
+
+            @pl.when(now)
             def _():
                 ex.advance(k, p)
                 if p == ex.phases:
@@ -209,50 +335,10 @@
     flat = lambda value: value.reshape(steps, SUB, LANES)
     zero = jnp.zeros((half, SUB, LANES), F32)
 
-    def prepare(tile, pre_ref, active_ref, gate_ref, graded_ref):
+    def spread_rates(tile):
         rates = rates_scr[tile]
         for n in range(states):
             rate_scr[n] = jnp.broadcast_to(rates[n : n + 1], (SUB, LANES))
-        delta = jax.nn.softplus(pre_ref[...])
-        delta_scr[...] = flat(delta)
-        drive_scr[...] = flat(delta * active_ref[...].astype(F32))
-        gate = gate_ref[...].astype(F32)
-        sigma = jax.nn.sigmoid(gate)
-        sigma_scr[...] = flat(sigma)
-        grad_scr[...] = flat(graded_ref[...] * (gate * sigma))
-
-    @pl.when(step < count)
-    def _():
-        tile = step
-        prepare(tile, pre_now, active_now, gate_now, graded_now)
-        total = jnp.sum(delta_scr[...], axis=0)
-        sums_scr[tile] = total
-        whole = jnp.sum(total, axis=0, keepdims=True)
-        totals[tile, 2 * states :] = jnp.broadcast_to(whole, (SUB, LANES))
-        for h, part in enumerate(halves):
-
-            def ends(i, carry):
-                state, message, decay = carry
-                for u in range(unroll):
-                    j = i * unroll + u
-                    factor = jnp.exp2(delta_scr[j][None] * rate_scr[part])
-                    state = factor * state + drive_scr[j][None] * inject_scr[j, part]
-                    decay = decay * factor
-                    message = message + decay * (grad_scr[j][None] * readout_scr[j, part])
-                return state, message, decay
-
-            state, message, decay = lax.fori_loop(0, steps // unroll, ends, (zero, zero, zero + 1.0))
-            for value, kept, at, reverse in (
-                (state, ahead_scr, h * half, False), (message, behind_scr, states + h * half, True)
-            ):
-                factor = decay
-                for by in (1, 2, 4):
-                    value = value + factor * shift_up(value, by, 0.0, reverse)
-                    factor = factor * shift_up(factor, by, 1.0, reverse)
-                kept[tile, part] = shift_up(value, 1, 0.0, reverse)
-                last = 0 if reverse else SUB - 1
-                for n in range(half):
-                    totals[tile, at + n : at + n + 1] = value[n, last : last + 1]
 
     def spread(table):
         return jnp.concatenate(
@@ -263,7 +349,9 @@
     def _():
         c = step - lag
         tile = c
-        prepare(tile, pre_ref, active_ref, gate_ref, graded_ref)
+        spread_rates(tile)
+        slot = lax.rem(c, lag)
+        delta_scr, drive_scr, grad_scr = delta_ring.at[slot], drive_ring.at[slot], grad_ring.at[slot]
         total = sums_scr[tile]
         before, after = total, total
         for by in (1, 2, 4):
@@ -285,17 +373,17 @@
 
         lax.fori_loop(0, steps // (unroll // 2), forward, state_scr[0])
         take_turns(0)
-        active = active_ref[...].astype(F32)
-        skip = skip_ref[...]
-        gate = gate_ref[...].astype(F32)
-        sigma = sigma_scr[...].reshape(rows, LANES)
-        graded = graded_ref[...]
+        lanes = pl.ds(pl.multiple_of(c * LANES, LANES), LANES)
+        skip = skip_ref[:, lanes]
+        active = active_ring[slot].reshape(rows, LANES)
         scanned = scan_scr[...].reshape(rows, LANES) + skip * active
-        gated = (scanned * (gate * sigma)).astype(BF16)
+        gated = (scanned * silu_ring[slot].reshape(rows, LANES)).astype(BF16)
         gated_ref[...] = gated
-        dgate = (graded * scanned * (sigma * (1.0 + gate * (1.0 - sigma)))).astype(BF16)
+        dgate = (scanned * sway_ring[slot].reshape(rows, LANES)).astype(BF16)
         dgate_ref[...] = dgate
-        dskip_ref[...] = jnp.sum(graded * (gate * sigma) * active, axis=0, keepdims=True)
+        lines_ref[states + 1 : states + 2, :] = jnp.sum(
+            grad_scr[...].reshape(rows, LANES) * active, axis=0, keepdims=True
+        )
         odd = lax.rem(c, 2)
 
         @pl.when(odd == 0)
@@ -331,16 +419,16 @@
             unused, total = lax.fori_loop(0, steps // unroll, backward, (state_scr[steps, part], zero))
             for n in range(half):
                 at = h * half + n
-                drate_ref[at : at + 1, :] = (
+                lines_ref[at : at + 1, :] = (
                     jnp.sum(total[n], axis=0, keepdims=True) * rate_scr[at, 0:1] * LN2
                 )
         weight = weight_scr[...].reshape(rows, LANES)
         delta = delta_scr[...].reshape(rows, LANES)
-        active = active_ref[...].astype(F32)
-        dactive_ref[...] = delta * weight + skip_ref[...] * grad_scr[...].reshape(rows, LANES)
-        dpre = (scan_scr[...].reshape(rows, LANES) * LN2 + active * weight) * jax.nn.sigmoid(pre_ref[...])
+        active = active_ring[slot].reshape(rows, LANES)
+        dactive_ref[...] = delta * weight + skip_ref[:, lanes] * grad_scr[...].reshape(rows, LANES)
+        dpre = (scan_scr[...].reshape(rows, LANES) * LN2 + active * weight) * slope_ring[slot].reshape(rows, LANES)
         dprelow_ref[...] = dpre.astype(BF16)
-        dbias_ref[...] = jnp.sum(dpre, axis=0, keepdims=True)
+        lines_ref[states : states + 1, :] = jnp.sum(dpre, axis=0, keepdims=True)
 
         @pl.when(odd == 1)
         def _():
@@ -359,33 +447,89 @@
 
         take_turns(1)
 
-    for r in range(rounds, -1, -1):
+    @pl.when(step < count)
+    def _():
+        tile = step
+        spread_rates(tile)
+        slot = lax.rem(step, lag)
+        delta_scr, drive_scr, grad_scr = delta_ring.at[slot], drive_ring.at[slot], grad_ring.at[slot]
+        lanes = pl.ds(pl.multiple_of(tile * LANES, LANES), LANES)
+        pre = jnp.dot(select_ref[:, :rank], step_weight_ref[:, lanes], preferred_element_type=F32)
+        pre = pre + step_bias_ref[:, lanes]
+        small = jnp.exp(-jnp.abs(pre))
+        delta = jnp.maximum(pre, 0.0) + jnp.log1p(small)
+        slope_ring[slot] = flat(jnp.where(pre >= 0.0, 1.0, small) / (1.0 + small))
+        delta_scr[...] = flat(delta)
+        active = active_now[...].astype(F32)
+        active_ring[slot] = flat(active)
+        drive_scr[...] = flat(delta * active)
+        gate = gate_now[...].astype(F32)
+        sigma = jax.nn.sigmoid(gate)
+        silu = gate * sigma
+        silu_ring[slot] = flat(silu)
+        graded = graded_now[...]
+        grad_scr[...] = flat(graded * silu)
+        sway_ring[slot] = flat(graded * (sigma * (1.0 + gate * (1.0 - sigma))))
+        total = jnp.sum(delta_scr[...], axis=0)
+        sums_scr[tile] = total
+        whole = jnp.sum(total, axis=0, keepdims=True)
+        totals[tile, 2 * states :] = jnp.broadcast_to(whole, (SUB, LANES))
+        for h, part in enumerate(halves):
+
+            def ends(i, carry):
+                state, message, decay = carry
+                for u in range(unroll):
+                    j = i * unroll + u
+                    factor = jnp.exp2(delta_scr[j][None] * rate_scr[part])
+                    state = factor * state + drive_scr[j][None] * inject_scr[j, part]
+                    decay = decay * factor
+                    message = message + decay * (grad_scr[j][None] * readout_scr[j, part])
+                return state, message, decay
+
+            state, message, decay = lax.fori_loop(0, steps // unroll, ends, (zero, zero, zero + 1.0))
+            for value, kept, at, reverse in (
+                (state, ahead_scr, h * half, False), (message, behind_scr, states + h * half, True)
+            ):
+                factor = decay
+                for by in (1, 2, 4):
+                    value = value + factor * shift_up(value, by, 0.0, reverse)
+                    factor = factor * shift_up(factor, by, 1.0, reverse)
+                kept[tile, part] = shift_up(value, 1, 0.0, reverse)
+                last = 0 if reverse else SUB - 1
+                for n in range(half):
+                    totals[tile, at + n : at + n + 1] = value[n, last : last + 1]
+
+    for r in range(lag - 1, -1, -1):
         e = step - r
 
         @pl.when((e >= 0) & (e < count))
         def _():
-            prefix.advance(e, r)
+            if r == 0:
+                prefix.copy(e, 0).start()
+            for done in range((r - 1) * per, min(r * per, rounds)) if r > 0 else ():
+                prefix.advance(e, done + 1)
 
     @pl.when(step == count + lag - 1)
     def _():
-        shape = (2 * LANES, 2 * states)
+        group = 4
+        shape = (group * LANES, 2 * states)
         from_lane = lax.broadcasted_iota(jnp.int32, shape, 0) // LANES
         to_column = lax.broadcasted_iota(jnp.int32, shape, 1)
         whole = jnp.zeros((rows, 2 * states), F32)
         for first, scr in ((0, dinject_scr), (states, dread_scr)):
-            for n in range(0, states, 2):
+            for n in range(0, states, group):
                 ones = (from_lane + (first + n) == to_column).astype(F32).astype(BF16)
-                value = jnp.concatenate([scr[:, n + side].reshape(rows, LANES) for side in range(2)], axis=1)
-                high = value.astype(BF16)
-                low = (value - high.astype(F32)).astype(BF16)
-                whole = whole + jnp.dot(high, ones, preferred_element_type=F32)
-                whole = whole + jnp.dot(low, ones, preferred_element_type=F32)
+                values = [scr[:, n + i].reshape(rows, LANES) for i in range(group)]
+                highs = [value.astype(BF16) for value in values]
+                lows = [(value - high.astype(F32)).astype(BF16) for value, high in zip(values, highs)]
+                for parts in (highs, lows):
+                    whole = whole + jnp.dot(jnp.concatenate(parts, axis=1), ones, preferred_element_type=F32)
         dselect_ref[...] = whole
 
         slots = 2 * count
         for k in range(count):
             for p in range(ex.phases):
-                if slot_of(k, p) in (slots - 1, slots - 2):
+                if slots - 2 <= slot_of(k, p) < slots:
                     ex.finish(k, p)
         sizes = []
         for k in range(early, count):
@@ -400,20 +544,20 @@
             wait_rows(acc.at[k, pl.ds(0, sizes[k - early]), :], store_sem.at[k])
 
 
-def run_scan(pre, active, gate, graded, select, decay_log, skip, normed, upstream, rank, seq):
-    rows, inner = pre.shape
+def run_scan(active, gate, graded, select, step_weight, step_bias, decay_log, skip, normed, upstream, seq):
+    rows, inner = active.shape
+    rank = step_weight.shape[0]
     states = decay_log.shape[0]
     width = upstream.shape[1]
     chunk = 2 * width
     tiles, steps = inner // LANES, rows // SUB
     rounds = seq.bit_length() - 1
     phases = 8 + max(rounds - 3, 0)
-    early = done_early(tiles, phases)
+    early = begun(tiles, phases)
     gates, outs = (early + 1) // 2 * 2 * LANES, early // 2 * 2 * LANES
-    lag = rounds + 1
+    lag = min(rounds, 3) + 1
     now = pl.BlockSpec((rows, LANES), lambda i: (0, lax.min(i, tiles - 1)))
     late = lambda shape: pl.BlockSpec(shape, lambda i: (0, lax.max(i - lag, 0)))
-    tall, line = late((rows, LANES)), late((1, LANES))
     whole = lambda a: pl.BlockSpec(a.shape, lambda i: (0, 0), pipeline_mode=pl.Buffered(1))
     hbm = pl.BlockSpec(memory_space=pltpu.HBM)
     wide = pltpu.VMEM((steps, states, SUB, LANES), F32)
@@ -422,26 +566,25 @@
     small = pltpu.VMEM((tiles, states, LANES), F32)
     pair = pltpu.VMEM((rows, 2 * LANES), BF16)
     buffers = scratch(tiles, chunk, tiles // 2, seq)
-    buffers[1] = pltpu.VMEM((3 * tiles // 4, chunk, LANES), BF16)
+    buffers[1] = pltpu.VMEM((begun(tiles, phases - 5), chunk, LANES), BF16)
+    ring = pltpu.VMEM((lag, steps, SUB, LANES), F32)
     return pl.pallas_call(
         functools.partial(scan_kernel, rank, states, chunk, rounds, seq),
         grid=(tiles + lag,),
         in_specs=[
-            now, now, now, now, tall, tall, tall, tall, whole(select), whole(decay_log), line, whole(normed), whole(upstream),
+            now, now, now, whole(select), whole(step_weight), whole(step_bias), whole(decay_log), whole(skip),
+            whole(normed), whole(upstream),
         ],
         out_specs=[
             late((rows, LANES)), late((rows, LANES)), late((rows, LANES)), late((rows, LANES)),
-            late((states, LANES)), late((1, LANES)), late((1, LANES)),
-            pl.BlockSpec((rows, 2 * states), lambda i: (0, 0)), hbm, hbm, hbm,
+            late((states + SUB, LANES)), pl.BlockSpec((rows, 2 * states), lambda i: (0, 0)), hbm, hbm, hbm,
         ],
         out_shape=[
             jax.ShapeDtypeStruct((rows, inner), BF16),
             jax.ShapeDtypeStruct((rows, inner), BF16),
             jax.ShapeDtypeStruct((rows, inner), BF16),
             jax.ShapeDtypeStruct((rows, inner), F32),
-            jax.ShapeDtypeStruct((states, inner), F32),
-            jax.ShapeDtypeStruct((1, inner), F32),
-            jax.ShapeDtypeStruct((1, inner), F32),
+            jax.ShapeDtypeStruct((states + SUB, inner), F32),
             jax.ShapeDtypeStruct((rows, 2 * states), F32),
             jax.ShapeDtypeStruct((width, gates), BF16),
             jax.ShapeDtypeStruct((outs, width), BF16),
@@ -450,7 +593,7 @@
         scratch_shapes=[
             wide, wide, wide, wide,
             pltpu.VMEM((steps + 1, states, SUB, LANES), F32), wide,
-            small, pltpu.VMEM((states, SUB, LANES), F32), thin, thin, thin, thin, thin, thin,
+            small, pltpu.VMEM((states, SUB, LANES), F32), ring, ring, ring, ring, ring, ring, ring, thin, thin,
             cube, cube, pltpu.VMEM((tiles, SUB, LANES), F32), pair, pair,
             pltpu.VMEM((tiles, 2 * states + SUB, LANES), F32),
             pltpu.VMEM((tiles, rounds, 2 * states + SUB, LANES), F32),
@@ -463,7 +606,9 @@
             collective_id=1, has_side_effects=True, vmem_limit_bytes=62 << 20
         ),
         name="span_scan",
-    )(pre, active, gate, graded, pre, active, gate, graded, select, decay_log, skip, normed, upstream)
+    )(
+        active, gate, graded, select, step_weight, step_bias, decay_log, skip, normed, upstream
+    )
 
 
 def bit_of(index, step):
@@ -662,8 +807,8 @@
 
 def tail_kernel(
     rank, states, chunk, seq,
-    dprelow_ref, select_ref, dpair_ref, step_weight_ref, normed_ref, upstream_ref, inputs_ref, scale_ref, ids_ref,
-    gain_ref, dactive_first_ref, mixed_first_ref, select_weight_ref, halo_ref, drate_ref, dbias_ref, dskip_ref,
+    dprelow_ref, select_ref, dpair_ref, step_weight_ref, normed_ref, upstream_ref, inputs_ref, scale_ref, hot_ref,
+    gain_ref, dactive_first_ref, mixed_first_ref, select_weight_ref, halo_ref, lines_ref,
     dactive_ref, mixed_ref, front_ref, active_ref, select_tile_ref, conv_ref, front_weight_ref, gate_weight_ref,
     dgate_ref, gated_ref, out_weight_ref, handed,
     output_ref, dinputs_ref, front_sum, gate_rest, out_rest, embedding_sum, wide_sum, mixed_sum,
@@ -680,7 +825,7 @@
     halo = kernel - 1
     vocab = embedding_sum.shape[0]
     ex = Exchange(acc, out, landing, extra, send_sem, recv_sem, chunk, landing.shape[0], seq)
-    early = done_early(tiles, ex.phases)
+    early = begun(tiles, ex.phases)
     old = tiles - early
     embedding_at, wide_at, mixed_at = (old + pairs + i for i in range(3))
     count = old + pairs + 3
@@ -749,15 +894,14 @@
             pltpu.make_async_copy(out.at[k], mixed_sum, store_sem.at[k]).start()
 
     def old_turns(spot):
-        slot = 2 * (tiles + step) + spot
-        for p, shift in turns(ex.phases, spot):
-            k = tiles + step + shift - early
-
-            @pl.when((k >= 0) & (k < old))
+        for k, p, now in turns(ex.phases, tiles + step, spot):
+            k = k - early
+
+            @pl.when(now & (k >= 0) & (k < old))
             def _():
                 if p > 0:
 
-                    @pl.when(slot > 2 * tiles + 1)
+                    @pl.when(step > 0)
                     def _():
                         ex.finish(k, p - 1)
 
@@ -801,13 +945,12 @@
         dnormed_scr[...] = jnp.zeros_like(dnormed_scr)
         result_scr[...] = jnp.zeros_like(result_scr)
         misc_scr[...] = jnp.zeros_like(misc_scr)
-        misc_scr[kernel + 1 : kernel + 2, :] = dbias_ref[...]
-        misc_scr[kernel + 2 : kernel + 3, :] = dskip_ref[...]
+        misc_scr[kernel + 1 : kernel + 3, :] = lines_ref[states : states + 2, :]
         acc[wide_at] = jnp.zeros_like(acc[wide_at])
         acc[mixed_at] = jnp.zeros_like(acc[mixed_at])
         for b in range(tiles):
             at = rank * tiles + b * states
-            acc[mixed_at, at : at + states, :] = drate_ref[:, b * LANES : (b + 1) * LANES].astype(BF16)
+            acc[mixed_at, at : at + states, :] = lines_ref[:states, b * LANES : (b + 1) * LANES].astype(BF16)
         for k in range(old):
             wait_rows(acc.at[k, pl.ds(0, sizes[k]), :], load_sem.at[k])
 
@@ -817,6 +960,11 @@
     def _():
         add(result_scr, jnp.dot(gated_ref[...], out_weight_ref[...], preferred_element_type=F32))
         add(dnormed_scr, contract_cols(dgate_ref[...], gate_weight_ref[...]))
+
+    old_turns(1)
+
+    @pl.when(step < pairs)
+    def _():
         lanes = pl.ds(pl.multiple_of(step * tall, tall), tall)
         mixed = mixed_ref[...]
         back = jnp.dot(dselect_scr[...], select_tile_ref[...], preferred_element_type=F32)
@@ -886,12 +1034,12 @@
 
         total = lax.fori_loop(0, SUB, norms, jnp.zeros((SUB, width), F32))
         gain_scr[...] = jnp.sum(total, axis=0, keepdims=True)
-        hot = (ids_ref[...] == lax.broadcasted_iota(jnp.int32, (rows, vocab), 1)).astype(F32).astype(BF16)
         for b in range(width // tall):
             value = jnp.concatenate([dnormed_scr[2 * b], dnormed_scr[2 * b + 1]], axis=1)
             high = value.astype(BF16)
             low = (value - high.astype(F32)).astype(BF16)
-            whole = (contract_rows(hot, high) + contract_rows(hot, low)).astype(BF16)
+            whole = jnp.dot(hot_ref[...], high, preferred_element_type=F32)
+            whole = (whole + jnp.dot(hot_ref[...], low, preferred_element_type=F32)).astype(BF16)
             for side in range(2):
                 at = (2 * b + side) * vocab
                 acc[embedding_at, at : at + vocab, :] = whole[:, side * LANES : (side + 1) * LANES]
@@ -913,7 +1061,6 @@
                 dinputs_ref[i * span : (i + 1) * span, lanes] = dnormed_scr[b, every, :]
                 output_ref[i * span : (i + 1) * span, lanes] = result_scr[b, every, :].astype(BF16)
 
-    old_turns(1)
     new_turns(step)
 
     @pl.when(step == pl.num_programs(0) - 1)
@@ -929,15 +1076,15 @@
 
 def run_tail(
     d_pre_low, select, d_pair, step_weight, normed, upstream, inputs, scale, ids, gain, d_active, mixed, select_weight,
-    halo, d_rate, d_bias, d_skip, front, active, conv_weight, input_weight, d_gate, gated, output_weight, handed, vocab, seq,
+    halo, lines, front, active, conv_weight, input_weight, d_gate, gated, output_weight, handed, vocab, seq,
 ):
     rows, inner = front.shape
     width = inputs.shape[1]
-    rank, states = step_weight.shape[0], d_rate.shape[0]
+    rank, states = step_weight.shape[0], lines.shape[0] - SUB
     chunk = 2 * width
     tiles, pairs, tall = inner // LANES, inner // (2 * LANES), 2 * LANES
     phases = 8 + max(seq.bit_length() - 4, 0)
-    early = done_early(tiles, phases)
+    early = begun(tiles, phases)
     count = tiles - early + pairs + 3
     some = halo.shape[0]
     at = lambda i: lax.min(i, pairs - 1)
@@ -954,7 +1101,7 @@
         in_specs=[
             whole(d_pre_low), whole(select), whole(d_pair), whole(step_weight), whole(normed), whole(upstream),
             whole(inputs), whole(scale), whole(ids), whole(gain), first, first, whole(select_weight), tile(some),
-            whole(d_rate), whole(d_bias), whole(d_skip), tile(rows), tile(rows), tile(rows), tile(rows),
+            whole(lines), tile(rows), tile(rows), tile(rows), tile(rows),
             tile(select_weight.shape[0]), tile(conv_weight.shape[0]), tile(width),
             pl.BlockSpec((width, tall), lambda i: (0, at(i) + pairs)), tile(rows), tile(rows), high(width), hbm,
         ],
@@ -987,7 +1134,7 @@
         name="span_tail",
     )(
         d_pre_low, select, d_pair, step_weight, normed, upstream, inputs, scale, ids, gain, d_active, mixed,
-        select_weight, halo, d_rate, d_bias, d_skip, d_active, mixed, front, active, select_weight, conv_weight,
+        select_weight, halo, lines, d_active, mixed, front, active, select_weight, conv_weight,
         input_weight, input_weight, d_gate, gated, output_weight, handed,
     )
 
@@ -1084,41 +1231,23 @@
     states = decay_log.shape[0]
     rank = step_weight.shape[0]
     rows = count * stretch
-    halo = kernel - 1
-    ids = to_spans(byte_ids.reshape(rows, 1))
-    one_hot = ids == jnp.arange(vocab, dtype=jnp.int32)[None, :]
-    block_inputs = jnp.dot(one_hot.astype(BF16), embedding, preferred_element_type=F32)
-    scale = lax.rsqrt(jnp.mean(block_inputs * block_inputs, axis=1, keepdims=True) + EPS)
-    normed_input = (block_inputs * scale * norm_gain).astype(BF16)
-    front = jnp.dot(
-        normed_input, input_projection_weight[:, :inner], preferred_element_type=F32
-    ).astype(BF16)
-    gate = jnp.dot(
-        normed_input, input_projection_weight[:, inner:], preferred_element_type=F32
-    ).astype(BF16)
-    last = front[rows - halo * SUB :].reshape(halo, SUB, inner)
-    tail = passed_along(last[:, SUB - 1], "seq", 1)
-    earlier = jnp.concatenate([tail[:, None], last[:, : SUB - 1]], axis=1).reshape(halo * SUB, inner)
-    extended = jnp.concatenate([earlier, front], axis=0).astype(F32)
-    mixed = conv_bias + conv_weight[0] * extended[:rows]
-    for place in range(1, kernel):
-        mixed = mixed + conv_weight[place] * extended[place * SUB : place * SUB + rows]
-    active = jax.nn.silu(mixed).astype(BF16)
-    select = jnp.dot(active, select_weight, preferred_element_type=F32).astype(BF16)
-    lowrank = select[:, :rank]
-    pre = jnp.dot(lowrank, step_weight, preferred_element_type=F32) + step_bias
-    upstream = to_spans(cotangent.reshape(rows, width))
-    graded = contract_cols(upstream, output_projection_weight)
     seq = lax.axis_size("seq")
-    turned = normed_input.T
+    gain, turned_select = norm_gain.reshape(1, width), select_weight.T
     (
-        gated, d_gate, d_pre_low, d_active, d_rate, d_bias, d_skip, d_pair, gate_sum, out_sum, handed
+        block_inputs, scale, unused, turned, upstream, hot, front, earlier, mixed, active, gate, graded, select
+    ) = run_front(
+        byte_ids.reshape(1, rows), embedding, cotangent.reshape(rows, width), gain, input_projection_weight,
+        output_projection_weight, conv_weight, conv_bias.reshape(1, inner), turned_select, seq,
+    )
+    (
+        gated, d_gate, d_pre_low, d_active, lines, d_pair, gate_sum, out_sum, handed
     ) = run_scan(
-        pre, active, gate, graded, select, decay_log, skip_gain.reshape(1, inner), turned, upstream, rank, seq
+        active, gate, graded, select, step_weight, step_bias.reshape(1, inner), decay_log, skip_gain.reshape(1, inner),
+        turned, upstream, seq,
     )
     output, d_inputs, front_sum, gate_rest, out_rest, embedding_sum, wide_sum, mixed_sum = run_tail(
-        d_pre_low, select, d_pair, step_weight, turned, upstream, block_inputs, scale, ids, norm_gain.reshape(1, width),
-        d_active, mixed, select_weight.T, earlier, d_rate, d_bias, d_skip, front, active, conv_weight,
+        d_pre_low, select, d_pair, step_weight, turned, upstream, block_inputs, scale, hot, gain,
+        d_active, mixed, turned_select, earlier, lines, front, active, conv_weight,
         input_projection_weight, d_gate, gated, output_projection_weight, handed, vocab, seq,
     )
     (

time: 277 us -> 257 us (0.928)
  Pallas kernels: 233 us -> 253 us
  matrix products: 19.4 us -> 0 us
  local copies, waits for them, and re-layouts: 12.9 us -> 3.27 us
  other arithmetic: 7.02 us -> 0 us
    pallas_call x0 -> x1, Pallas kernels: none -> 19.9 us  [run_front(): pl.pallas_call(functools.partial(front_kernel, seq), grid=(pairs,), in_sp...]
    dot_general x6 -> x0, matrix products: 19.4 us -> none  [the longest x1 5.47 us: on_device(): jnp.dot(normed_input, input_projection_weight[:, :inner], preferred_eleme...]
    convert_element_type x3 -> x0, other arithmetic: 5.61 us -> none  [the longest x1 3.84 us: on_device(): active = jax.nn.silu(mixed).astype(BF16)]
    another operation x3 -> x0, local copies, waits for them, and re-layouts: 2.95 us -> none  [to_spans(): return array.reshape(SUB, rows // SUB, -1).swapaxes(0, 1).reshape(rows, -1)]
    unnamed x42 -> x6, local copies, waits for them, and re-layouts: 6.08 us -> 3.27 us
  transfers between devices with their start and end apart: 1 -> 0, of which waited for: 0 -> 0; matrix products, arithmetic and copies ran while one was open for 6% -> 0% of each run, Pallas kernels for 0% -> 0%
where the time goes in v3:
time: 257 us
  Pallas kernels  253 us (98%)
  local copies, waits for them, and re-layouts  3.27 us (1%)
    pallas_call x1, Pallas kernels, run_scan(): pl.pallas_call(functools.partial(scan_kernel, rank, states, chunk, rounds...  128 us
    pallas_call x1, Pallas kernels, run_tail(): pl.pallas_call(functools.partial(tail_kernel, rank, states, chunk, seq),...  89 us
    pallas_call x1, Pallas kernels, run_front(): pl.pallas_call(functools.partial(front_kernel, seq), grid=(pairs,), in_sp...  19.9 us
    pallas_call x1, Pallas kernels, run_widen(): pl.pallas_call(functools.partial(widen_kernel, rank, states, columns, out...  15.7 us

profile of v3, /device:TPU:0, one launch (start us, length us, event | category | flops | bytes accessed | tf_op | source)
XLA Modules:
  0.0 256.7 jit_solution(12221426345405948951)
XLA Ops:
  0.6 19.9 %span_front.1 = (f32[512,1024]{1,0:T(8,128)}, f32[512,1]{1,0:T(8,128)}, bf16[528,1024]{1,0:T(8,128)(2,1)}, bf16[1024,512]{1,0:T(8,128)(2,1)}, bf16[512,1024]{1,0...) custom-call(s32[1,512]{1,0:T(1,128)} %ids_ref.1, ...), custom_call_target="tpu_custom_call" | custom-call | tf_op jit(solution)/shard_map/span_front/pallas_call | solution.py:186
  20.5 128.2 %span_scan.1 = (bf16[512,2048]{1,0:T(8,128)(2,1)}, bf16[512,2048]{1,0:T(8,128)(2,1)}, bf16[512,2048]{1,0:T(8,128)(2,1)}, f32[512,2048]{1,0:T(8,128)}, f32[24,204...) custom-call(bf16[512,2048]{1,0:T(8,128)(2,1)} %get-tuple-element.53., ...), custom_call_target="tpu_custom_call" | custom-call | tf_op jit(solution)/shard_map/span_scan/pallas_call | solution.py:571
  148.8 89.0 %span_tail.1 = (bf16[512,1024]{1,0:T(8,128)(2,1)}, f32[512,1024]{1,0:T(8,128)}, bf16[1024,2048]{1,0:T(8,128)(2,1)}, bf16[1024,1024]{1,0:T(8,128)(2,1)}, bf16[128...) custom-call(bf16[512,2048]{1,0:T(8,128)(2,1)} %get-tuple-element.59.dprel, ...), custom_call_target="tpu_custom_call" | custom-call | tf_op jit(solution)/shard_map/span_tail/pallas_call | solution.py:1098
  237.7 0.0 copy-start.1
  237.8 15.7 %sums_to_float32.1 = (f32[1024,4096]{1,0:T(8,128)}, f32[2048,1024]{1,0:T(8,128)}, f32[256,1024]{1,0:T(8,128)}, f32[96,2048]{1,0:T(8,128)}, f32[64,2048]{1,0:T(8,...) custom-call(bf16[1024,2048]{1,0:T(8,128)(2,1)} %get-tuple-element.74, ...), custom_call_target="tpu_custom_call" | custom-call | tf_op jit(solution)/shard_map/sums_to_float32/pallas_call | solution.py:1193
  253.4 0.0 copy-start
  253.4 0.0 copy-done.1
  253.4 1.0 copy.28
  254.4 1.0 copy-done
  255.4 1.3 copy.29
Async XLA Ops:
  237.7 15.7 %copy-start.1 = (bf16[512,1024]{1,0:T(8,128)(2,1)S(1)}, bf16[512,1024]{1,0:T(8,128)(2,1)}, u32[]{:S(2)}) copy-start(bf16[512,1024]{1,0:T(8,128)(2,1)} %get-tuple-element.72) | copy-start | bytes 3145732
  253.4 2.0 copy-start

commit v4 on v3

--- a/solution.py
+++ b/solution.py
@@ -272,13 +272,14 @@
 
 def scan_kernel(
     rank, states, chunk, rounds, seq,
-    active_now, gate_now, graded_now, select_ref, step_weight_ref, step_bias_ref, decay_ref, skip_ref, normed_ref, upstream_ref,
+    active_now, gate_now, graded_now, select_ref, step_weight_ref, step_bias_ref, decay_ref, skip_ref, normed_hbm, upstream_hbm,
     gated_ref, dgate_ref, dprelow_ref, dactive_ref, lines_ref, dselect_ref,
     gate_sum, out_sum, handed,
     inject_scr, readout_scr, dread_scr, dinject_scr, state_scr, factor_scr,
     rates_scr, rate_scr, delta_ring, drive_ring, grad_ring, silu_ring, sway_ring, active_ring, slope_ring, scan_scr, weight_scr,
     ahead_scr, behind_scr, sums_scr, gated_scr, dgated_scr,
     totals, totals_in, start_scr, incoming_scr, gaps_scr, prefix_send, prefix_recv,
+    normed_ref, upstream_ref, late_sem,
     acc, out, landing, extra, send_sem, recv_sem, store_sem,
 ):
     rows = active_now.shape[0]
@@ -316,8 +317,16 @@
                 if p == ex.phases:
                     store(k)
 
+    late_loads = [
+        pltpu.make_async_copy(source, target, late_sem.at[i])
+        for i, (source, target) in enumerate(((normed_hbm, normed_ref), (upstream_hbm, upstream_ref)))
+    ]
+
     @pl.when(step == 0)
     def _():
+        ex.greet()
+        for copy in late_loads:
+            copy.start()
         for first, scr in ((rank, inject_scr), (rank + states, readout_scr)):
             for n in range(0, states, 2):
                 wide = expand_columns(select_ref[...], first + n, 2)
@@ -330,7 +339,9 @@
         gaps_scr[...] = jnp.zeros_like(gaps_scr)
         for e in range(count):
             rates_scr[e] = -jnp.exp(decay_ref[:, e * LANES : (e + 1) * LANES]) * LOG2E
-        ex.greet()
+        for copy in late_loads:
+            copy.wait()
+        ex.welcome()
 
     flat = lambda value: value.reshape(steps, SUB, LANES)
     zero = jnp.zeros((half, SUB, LANES), F32)
@@ -573,7 +584,7 @@
         grid=(tiles + lag,),
         in_specs=[
             now, now, now, whole(select), whole(step_weight), whole(step_bias), whole(decay_log), whole(skip),
-            whole(normed), whole(upstream),
+            hbm, hbm,
         ],
         out_specs=[
             late((rows, LANES)), late((rows, LANES)), late((rows, LANES)), late((rows, LANES)),
@@ -599,6 +610,7 @@
             pltpu.VMEM((tiles, rounds, 2 * states + SUB, LANES), F32),
             small, small, pltpu.VMEM((tiles, SUB, LANES), F32),
             pltpu.SemaphoreType.DMA((tiles, rounds)), pltpu.SemaphoreType.DMA((tiles, rounds)),
+            pltpu.VMEM(normed.shape, BF16), pltpu.VMEM(upstream.shape, BF16), pltpu.SemaphoreType.DMA((2,)),
         ]
         + buffers
         + [pltpu.SemaphoreType.DMA((tiles,))],
@@ -674,11 +686,11 @@
         return [other(*link) for link in links] + [self.along(i) for i in range(1, 4)]
 
     def greet(self):
-        barrier = pltpu.get_barrier_semaphore()
-        partners = self.partners()
-        for device in partners:
-            pl.semaphore_signal(barrier, inc=1, device_id=device, device_id_type=MESH)
-        pl.semaphore_wait(barrier, len(partners))
+        for device in self.partners():
+            pl.semaphore_signal(pltpu.get_barrier_semaphore(), inc=1, device_id=device, device_id_type=MESH)
+
+    def welcome(self):
+        pl.semaphore_wait(pltpu.get_barrier_semaphore(), len(self.partners()))
 
     def along(self, i):
         place = lax.axis_index("seq")
@@ -807,12 +819,12 @@
 
 def tail_kernel(
     rank, states, chunk, seq,
-    dprelow_ref, select_ref, dpair_ref, step_weight_ref, normed_ref, upstream_ref, inputs_ref, scale_ref, hot_ref,
+    dprelow_ref, select_ref, dpair_ref, step_weight_ref, normed_ref, upstream_hbm, inputs_hbm, scale_ref, hot_hbm,
     gain_ref, dactive_first_ref, mixed_first_ref, select_weight_ref, halo_ref, lines_ref,
     dactive_ref, mixed_ref, front_ref, active_ref, select_tile_ref, conv_ref, front_weight_ref, gate_weight_ref,
     dgate_ref, gated_ref, out_weight_ref, handed,
     output_ref, dinputs_ref, front_sum, gate_rest, out_rest, embedding_sum, wide_sum, mixed_sum,
-    dselect_scr, first_scr, after_scr, spread_scr, extended_scr, dnormed_scr, result_scr, misc_scr, gain_scr,
+    upstream_ref, inputs_ref, hot_ref, late_sem, dselect_scr, first_scr, after_scr, spread_scr, extended_scr, dnormed_scr, result_scr, misc_scr, gain_scr,
     acc, out, landing, extra, send_sem, recv_sem, load_sem, store_sem, first_send, first_recv,
 ):
     step = pl.program_id(0)
@@ -849,19 +861,26 @@
             device_id=(here_dp, lax.rem(place + seq - 1, seq)), device_id_type=MESH,
         )
 
+    late_loads = [
+        pltpu.make_async_copy(source, target, late_sem.at[i])
+        for i, (source, target) in enumerate(
+            ((upstream_hbm, upstream_ref), (inputs_hbm, inputs_ref), (hot_hbm, hot_ref))
+        )
+    ]
+
     def greet():
         barrier = pltpu.get_barrier_semaphore()
-        partners = ex.partners()
-        for device in partners:
-            pl.semaphore_signal(barrier, inc=1, device_id=device, device_id_type=MESH)
+        ex.greet()
         for there, by in ((place > 0, -1), (place < seq - 1, 1)):
 
             @pl.when(there)
             def _():
                 pl.semaphore_signal(barrier, inc=1, device_id=(here_dp, place + by), device_id_type=MESH)
 
+    def welcome():
+        barrier = pltpu.get_barrier_semaphore()
         neighbours = 2 - (place == 0).astype(jnp.int32) - (place == seq - 1).astype(jnp.int32)
-        pl.semaphore_wait(barrier, len(partners) + neighbours)
+        pl.semaphore_wait(barrier, len(ex.partners()) + neighbours)
 
     def store(k):
         pair = (k + early) // 2
@@ -922,6 +941,7 @@
 
     @pl.when(step == 0)
     def _():
+        greet()
         sizes = []
         for k in range(old):
             sizes.append(0)
@@ -929,7 +949,8 @@
                 here = pl.ds(pl.multiple_of(base, 16), size)
                 sizes[-1] += size
                 pltpu.make_async_copy(handed.at[k, here, :], ref.at[k, here, :], load_sem.at[k]).start()
-        greet()
+        for copy in late_loads:
+            copy.start()
         dlow = contract_cols(dprelow_ref[...], step_weight_ref[...])
         dselect_scr[...] = jnp.concatenate([dlow, dpair_ref[...]], axis=1).astype(BF16)
         some = jnp.dot(dselect_scr[: halo * SUB], select_weight_ref[...], preferred_element_type=F32)
@@ -937,6 +958,7 @@
         for i in range(halo):
             first_scr[i : i + 1, :] = some[i * SUB : i * SUB + 1, :]
         first_scr[halo:, :] = jnp.zeros((SUB - halo, inner), F32)
+        welcome()
 
         @pl.when(place > 0)
         def _():
@@ -1018,6 +1040,8 @@
 
     @pl.when(step == pairs)
     def _():
+        for copy in late_loads:
+            copy.wait()
         part = rows // SUB
 
         def norms(i, total):
@@ -1075,7 +1099,7 @@
 
 
 def run_tail(
-    d_pre_low, select, d_pair, step_weight, normed, upstream, inputs, scale, ids, gain, d_active, mixed, select_weight,
+    d_pre_low, select, d_pair, step_weight, normed, upstream, inputs, scale, hot, gain, d_active, mixed, select_weight,
     halo, lines, front, active, conv_weight, input_weight, d_gate, gated, output_weight, handed, vocab, seq,
 ):
     rows, inner = front.shape
@@ -1099,8 +1123,8 @@
         functools.partial(tail_kernel, rank, states, chunk, seq),
         grid=(pairs + 3,),
         in_specs=[
-            whole(d_pre_low), whole(select), whole(d_pair), whole(step_weight), whole(normed), whole(upstream),
-            whole(inputs), whole(scale), whole(ids), whole(gain), first, first, whole(select_weight), tile(some),
+            whole(d_pre_low), whole(select), whole(d_pair), whole(step_weight), whole(normed), hbm,
+            hbm, whole(scale), hbm, whole(gain), first, first, whole(select_weight), tile(some),
             whole(lines), tile(rows), tile(rows), tile(rows), tile(rows),
             tile(select_weight.shape[0]), tile(conv_weight.shape[0]), tile(width),
             pl.BlockSpec((width, tall), lambda i: (0, at(i) + pairs)), tile(rows), tile(rows), high(width), hbm,
@@ -1117,6 +1141,8 @@
             jax.ShapeDtypeStruct((chunk, LANES), BF16),
         ],
         scratch_shapes=[
+            pltpu.VMEM(upstream.shape, BF16), pltpu.VMEM(inputs.shape, F32), pltpu.VMEM(hot.shape, BF16),
+            pltpu.SemaphoreType.DMA((3,)),
             pltpu.VMEM(select.shape, BF16),
             pltpu.VMEM((SUB, inner), F32), pltpu.VMEM((SUB, inner), F32),
             pltpu.VMEM((rows + some, tall), F32), pltpu.VMEM((rows + some, tall), F32),
@@ -1133,35 +1159,55 @@
         ),
         name="span_tail",
     )(
-        d_pre_low, select, d_pair, step_weight, normed, upstream, inputs, scale, ids, gain, d_active, mixed,
+        d_pre_low, select, d_pair, step_weight, normed, upstream, inputs, scale, hot, gain, d_active, mixed,
         select_weight, halo, lines, d_active, mixed, front, active, select_weight, conv_weight,
         input_weight, input_weight, d_gate, gated, output_weight, handed,
     )
 
 
 def widen_kernel(
-    rank, states, columns, outs,
-    front_ref, gate_ref, gate_rest_ref, out_ref, out_rest_ref, embedding_ref, wide_ref, mixed_ref,
-    input_to, output_to, embedding_to, select_to, step_to, decay_to, conv_to, gain_to, *line_to,
+    rank, states, columns, parts, slots,
+    front, gate, gate_rest, outs, outs_rest, output, dinputs, embedding, wide_sum, mixed_sum,
+    input_to, output_weight_to, output_to, dinputs_to, *rest,
 ):
-    step = pl.program_id(0)
-    inner, gates = front_ref.shape[1], gate_ref.shape[1]
-    input_to[:, :inner] = front_ref[...].astype(F32)
-    input_to[:, inner : inner + gates] = gate_ref[...].astype(F32)
-    input_to[:, inner + gates :] = gate_rest_ref[...].astype(F32)
-
-    @pl.when(step < outs)
-    def _():
-        output_to[...] = out_ref[...].astype(F32)
-
-    @pl.when(step >= outs)
-    def _():
-        output_to[...] = out_rest_ref[...].astype(F32)
-
-    embedding_to[...] = embedding_ref[...].astype(F32)
-
-    @pl.when(step == 0)
-    def _():
+    small_to, scratches = rest[:9], rest[9:]
+    (
+        input_scr, outs_scr, wide_input, wide_outs, output_scr, dinputs_scr, embedding_ref, wide_ref, mixed_ref,
+        load_sem, outs_load, store_sem, outs_store, pass_sem, small_load, small_store,
+    ) = scratches[:16]
+    small_scr = scratches[16:]
+    small = [
+        pltpu.make_async_copy(source, scr, small_load.at[i])
+        for i, (source, scr) in enumerate(((embedding, embedding_ref), (wide_sum, wide_ref), (mixed_sum, mixed_ref)))
+    ]
+    small_out = [
+        pltpu.make_async_copy(scr, to, small_store.at[i]) for i, (scr, to) in enumerate(zip(small_scr, small_to))
+    ]
+    passed = [
+        (pltpu.make_async_copy(source, scr, pass_sem.at[i]), pltpu.make_async_copy(scr, to, pass_sem.at[i]))
+        for i, (source, scr, to) in enumerate(((output, output_scr, output_to), (dinputs, dinputs_scr, dinputs_to)))
+    ]
+    thick, tall = input_scr.shape[0] // parts, outs_scr.shape[0] // parts
+    early = outs.shape[0] // tall
+    for i in range(parts):
+        here, lane = pl.ds(i * thick, thick), 0
+        for source in (front, gate, gate_rest):
+            lanes = pl.ds(lane, source.shape[1])
+            pltpu.make_async_copy(source.at[here, :], input_scr.at[here, lanes], load_sem.at[i]).start()
+            lane += source.shape[1]
+        source, at = (outs, i) if i < early else (outs_rest, i - early)
+        there = pl.ds(i * tall, tall)
+        pltpu.make_async_copy(source.at[pl.ds(at * tall, tall), :], outs_scr.at[there, :], outs_load.at[i]).start()
+    for copy, unused in passed:
+        copy.start()
+    for copy in small:
+        copy.start()
+
+    def unpack():
+        embedding_to, select_to, step_to, decay_to, conv_to, gain_to, *line_to = small_scr
+        for copy in small:
+            copy.wait()
+        embedding_to[...] = embedding_ref[...].astype(F32)
         for source, whole in (
             (wide_ref, ((select_to, columns),)),
             (mixed_ref, ((step_to, rank), (decay_to, states), (conv_to, 16), (gain_to, 16))),
@@ -1176,38 +1222,69 @@
                         for i, line in enumerate(line_to):
                             line[:, lanes] = part[to.shape[0] + i : to.shape[0] + i + 1]
                     at += height
-
-
-def run_widen(front, gate, gate_rest, out, out_rest, embedding, wide, mixed, rank, states, columns, kernel):
+        for copy in small_out:
+            copy.start()
+
+    for i in range(parts):
+        if i == parts // 2:
+            for first, second in passed:
+                first.wait()
+                second.start()
+            unpack()
+        slot = i % slots
+        for narrow, wide, to, size, load, store in (
+            (input_scr, wide_input, input_to, thick, load_sem, store_sem),
+            (outs_scr, wide_outs, output_weight_to, tall, outs_load, outs_store),
+        ):
+            here, half = pl.ds(i * size, size), size // 2
+            wait_rows(narrow.at[here, :], load.at[i])
+            if i >= slots:
+                wait_rows(wide.at[slot], store.at[slot])
+            wide[slot] = narrow[here, :].astype(F32)
+            for j in range(2):
+                pltpu.make_async_copy(
+                    wide.at[slot, pl.ds(j * half, half), :], to.at[pl.ds(i * size + j * half, half), :], store.at[slot]
+                ).start()
+    for slot in range(slots):
+        wait_rows(wide_input.at[slot], store_sem.at[slot])
+        wait_rows(wide_outs.at[slot], outs_store.at[slot])
+    for unused, copy in passed:
+        copy.wait()
+    for copy in small_out:
+        copy.wait()
+
+
+def run_widen(
+    front, gate, gate_rest, out, out_rest, output, d_inputs, embedding, wide, mixed, rank, states, columns, kernel
+):
     width, inner = front.shape
-    tall = 2 * LANES
-    tiles, outs = inner // tall, out.shape[0] // tall
     vocab = embedding.shape[0]
-    lines = lambda a: pl.BlockSpec((width // tiles, a.shape[1]), lambda i: (i, 0))
-    thin = pl.BlockSpec((vocab // tiles, width), lambda i: (i, 0))
-    fixed = lambda shape: pl.BlockSpec(shape, lambda i: (0, 0))
+    parts, slots = inner // (2 * LANES), 4
+    hbm = pl.BlockSpec(memory_space=pltpu.HBM)
     shapes = [
-        (width, 2 * inner), (inner, width), (vocab, width), (columns, inner), (rank, inner), (states, inner), (kernel, inner),
-        (1, width), (1, inner), (1, inner), (1, inner),
+        (width, 2 * inner), (inner, width), output.shape, d_inputs.shape, (vocab, width), (columns, inner), (rank, inner),
+        (states, inner), (kernel, inner), (1, width), (1, inner), (1, inner), (1, inner),
     ]
     return pl.pallas_call(
-        functools.partial(widen_kernel, rank, states, columns, outs),
-        grid=(tiles,),
-        in_specs=[
-            lines(front), lines(gate), lines(gate_rest),
-            pl.BlockSpec((tall, width), lambda i: (lax.min(i, outs - 1), 0)),
-            pl.BlockSpec((tall, width), lambda i: (lax.max(i - outs, 0), 0)),
-            thin, fixed(wide.shape), fixed(mixed.shape),
+        functools.partial(widen_kernel, rank, states, columns, parts, slots),
+        in_specs=[hbm] * 10,
+        out_specs=[hbm] * len(shapes),
+        out_shape=[
+            jax.ShapeDtypeStruct(shape, output.dtype if i == 2 else F32) for i, shape in enumerate(shapes)
         ],
-        out_specs=[
-            pl.BlockSpec((width // tiles, 2 * inner), lambda i: (i, 0)),
-            pl.BlockSpec((tall, width), lambda i: (i, 0)), thin,
+        scratch_shapes=[
+            pltpu.VMEM((width, 2 * inner), BF16), pltpu.VMEM((inner, width), BF16),
+            pltpu.VMEM((slots, width // parts, 2 * inner), F32), pltpu.VMEM((slots, inner // parts, width), F32),
+            pltpu.VMEM(output.shape, output.dtype), pltpu.VMEM(d_inputs.shape, F32),
+            pltpu.VMEM(embedding.shape, BF16), pltpu.VMEM(wide.shape, BF16), pltpu.VMEM(mixed.shape, BF16),
+            pltpu.SemaphoreType.DMA((parts,)), pltpu.SemaphoreType.DMA((parts,)),
+            pltpu.SemaphoreType.DMA((slots,)), pltpu.SemaphoreType.DMA((slots,)), pltpu.SemaphoreType.DMA((2,)),
+            pltpu.SemaphoreType.DMA((3,)), pltpu.SemaphoreType.DMA((len(shapes) - 4,)),
         ]
-        + [fixed(shape) for shape in shapes[3:]],
-        out_shape=[jax.ShapeDtypeStruct(shape, F32) for shape in shapes],
+        + [pltpu.VMEM(shape, F32) for shape in shapes[4:]],
         compiler_params=pltpu.CompilerParams(vmem_limit_bytes=62 << 20),
         name="sums_to_float32",
-    )(front, gate, gate_rest, out, out_rest, embedding, wide, mixed)
+    )(front, gate, gate_rest, out, out_rest, output, d_inputs, embedding, wide, mixed)
 
 
 def on_device(
@@ -1251,10 +1328,10 @@
         input_projection_weight, d_gate, gated, output_projection_weight, handed, vocab, seq,
     )
     (
-        d_input_weight, d_output_weight, d_embedding, d_select_weight, d_step_weight, d_decay_log, d_conv_weight,
+        d_input_weight, d_output_weight, output, d_inputs, d_embedding, d_select_weight, d_step_weight, d_decay_log, d_conv_weight,
         d_norm_gain, d_conv_bias, d_step_bias, d_skip_gain,
     ) = run_widen(
-        front_sum, gate_sum, gate_rest, out_sum, out_rest, embedding_sum, wide_sum, mixed_sum, rank, states,
+        front_sum, gate_sum, gate_rest, out_sum, out_rest, output, d_inputs, embedding_sum, wide_sum, mixed_sum, rank, states,
         select_weight.shape[1], kernel,
     )
     return (

time: 257 us -> 251 us (0.977)
  local copies, waits for them, and re-layouts: 3.27 us -> 0 us
  Pallas kernels: 253 us -> 250 us
    unnamed x6 -> x0, local copies, waits for them, and re-layouts: 3.27 us -> none
    pallas_call x1, Pallas kernels: 128 us -> 125 us  [run_scan(): pl.pallas_call(functools.partial(scan_kernel, rank, states, chunk, rounds...]
where the time goes in v4:
time: 251 us; the launch traced here: 250 us
  Pallas kernels  250 us (100%)
    pallas_call x1, Pallas kernels, run_scan(): pl.pallas_call(functools.partial(scan_kernel, rank, states, chunk, rounds...  125 us
    pallas_call x1, Pallas kernels, run_tail(): pl.pallas_call(functools.partial(tail_kernel, rank, states, chunk, seq),...  87.6 us
    pallas_call x1, Pallas kernels, run_front(): pl.pallas_call(functools.partial(front_kernel, seq), grid=(pairs,), in_sp...  19.8 us
    pallas_call x1, Pallas kernels, run_widen(): pl.pallas_call(functools.partial(widen_kernel, rank, states, columns, par...  16.9 us

profile of v4, /device:TPU:0, one launch (start us, length us, event | category | flops | bytes accessed | tf_op | source)
XLA Modules:
  0.0 250.5 jit_solution(14440265810911859702)
XLA Ops:
  0.6 19.8 %span_front.1 = (f32[512,1024]{1,0:T(8,128)}, f32[512,1]{1,0:T(8,128)}, bf16[528,1024]{1,0:T(8,128)(2,1)}, bf16[1024,512]{1,0:T(8,128)(2,1)}, bf16[512,1024]{1,0...) custom-call(s32[1,512]{1,0:T(1,128)} %ids_ref.1, ...), custom_call_target="tpu_custom_call" | custom-call | tf_op jit(solution)/shard_map/span_front/pallas_call | solution.py:186
  20.5 125.3 %span_scan.1 = (bf16[512,2048]{1,0:T(8,128)(2,1)}, bf16[512,2048]{1,0:T(8,128)(2,1)}, bf16[512,2048]{1,0:T(8,128)(2,1)}, f32[512,2048]{1,0:T(8,128)}, f32[24,204...) custom-call(bf16[512,2048]{1,0:T(8,128)(2,1)} %get-tuple-element.55., ...), custom_call_target="tpu_custom_call" | custom-call | tf_op jit(solution)/shard_map/span_scan/pallas_call | solution.py:582
  145.8 87.6 %span_tail.1 = (bf16[512,1024]{1,0:T(8,128)(2,1)}, f32[512,1024]{1,0:T(8,128)}, bf16[1024,2048]{1,0:T(8,128)(2,1)}, bf16[1024,1024]{1,0:T(8,128)(2,1)}, bf16[128...) custom-call(bf16[512,2048]{1,0:T(8,128)(2,1)} %get-tuple-element.61.dprel, ...), custom_call_target="tpu_custom_call" | custom-call | tf_op jit(solution)/shard_map/span_tail/pallas_call | solution.py:1122
  233.4 16.9 %sums_to_float32.1 = (f32[1024,4096]{1,0:T(8,128)}, f32[2048,1024]{1,0:T(8,128)}, bf16[512,1024]{1,0:T(8,128)(2,1)}, f32[512,1024]{1,0:T(8,128)}, f32[256,1024]{...) custom-call(bf16[1024,2048]{1,0:T(8,128)(2,1)} %get-tuple-element.74, ...), custom_call_target="tpu_custom_call" | custom-call | tf_op jit(solution)/shard_map/sums_to_float32/pallas_call | solution.py:1268

commit v5 on v4

--- a/solution.py
+++ b/solution.py
@@ -149,7 +149,7 @@
         own = pltpu.roll(both[rows - (halo - i) * SUB : rows - (halo - i - 1) * SUB], 1, 0)
         before = both[rows + 16 - halo + i : rows + 16 - halo + i + 1]
         extended_scr[i * SUB : (i + 1) * SUB] = jnp.where(sub > 0, own, before)
-    halo_ref[...] = extended_scr[: halo * SUB].astype(BF16)
+    halo_ref[...] = extended_scr[: halo * SUB]
     mixed = conv_bias_ref[...] + conv_ref[0:1] * extended_scr[:rows]
     for i in range(1, kernel):
         mixed = mixed + conv_ref[i : i + 1] * extended_scr[i * SUB : i * SUB + rows]
@@ -172,7 +172,7 @@
     inner = output_weight.shape[0]
     vocab, kernel, columns = embedding.shape[0], conv_weight.shape[0], select_weight.shape[0]
     halo = (kernel - 1) * SUB
-    tall = 2 * LANES
+    tall = 4 * LANES
     pairs = inner // tall
     whole = lambda a: pl.BlockSpec(a.shape, lambda i: (0, 0), pipeline_mode=pl.Buffered(1))
     tile = lambda height: pl.BlockSpec((height, tall), lambda i: (0, i))
@@ -180,7 +180,7 @@
     outs = [
         ((rows, width), F32, None), ((rows, 1), F32, None), ((rows + 16, width), BF16, None),
         ((width, rows), BF16, None), ((rows, width), BF16, None), ((vocab, rows), BF16, None),
-        ((rows, inner), BF16, rows), ((halo, inner), BF16, halo), ((rows, inner), F32, rows), ((rows, inner), BF16, rows),
+        ((rows, inner), BF16, rows), ((halo, inner), F32, halo), ((rows, inner), F32, rows), ((rows, inner), BF16, rows),
         ((rows, inner), BF16, rows), ((rows, inner), F32, rows), ((rows, columns), BF16, None),
     ]
     return pl.pallas_call(
@@ -294,7 +294,7 @@
     )
     ex = Exchange(acc, out, landing, extra, send_sem, recv_sem, chunk, landing.shape[0], seq)
     early = begun(count, ex.phases)
-    half, unroll = states // 2, 8
+    half, unroll = states // 2, 16
     halves = [pl.ds(0, half), pl.ds(half, half)]
 
     def store(k):
@@ -953,8 +953,8 @@
             copy.start()
         dlow = contract_cols(dprelow_ref[...], step_weight_ref[...])
         dselect_scr[...] = jnp.concatenate([dlow, dpair_ref[...]], axis=1).astype(BF16)
-        some = jnp.dot(dselect_scr[: halo * SUB], select_weight_ref[...], preferred_element_type=F32)
-        some = (dactive_first_ref[...] + some) * silu_slope(mixed_first_ref[...])
+        some = jnp.dot(dselect_scr[: (halo + 1) * SUB], select_weight_ref[...], preferred_element_type=F32)
+        some = (dactive_first_ref[...] + some[: halo * SUB]) * silu_slope(mixed_first_ref[...])
         for i in range(halo):
             first_scr[i : i + 1, :] = some[i * SUB : i * SUB + 1, :]
         first_scr[halo:, :] = jnp.zeros((SUB - halo, inner), F32)
@@ -992,7 +992,7 @@
         back = jnp.dot(dselect_scr[...], select_tile_ref[...], preferred_element_type=F32)
         dmixed = (dactive_ref[...] + back) * silu_slope(mixed)
         spread_scr[:rows] = dmixed
-        extended_scr[: halo * SUB] = halo_ref[...].astype(F32)
+        extended_scr[: halo * SUB] = halo_ref[...]
         extended_scr[halo * SUB :] = front_ref[...].astype(F32)
         misc_scr[kernel : kernel + 1, lanes] = jnp.sum(dmixed, axis=0, keepdims=True)
         for i in range(kernel):

time: 251 us -> 247 us (0.984)
  Pallas kernels: 250 us -> 246 us
where the time goes in v5:
time: 247 us
  Pallas kernels  246 us (100%)
    pallas_call x1, Pallas kernels, run_scan(): pl.pallas_call(functools.partial(scan_kernel, rank, states, chunk, rounds...  123 us
    pallas_call x1, Pallas kernels, run_tail(): pl.pallas_call(functools.partial(tail_kernel, rank, states, chunk, seq),...  87.1 us
    pallas_call x1, Pallas kernels, run_front(): pl.pallas_call(functools.partial(front_kernel, seq), grid=(pairs,), in_sp...  18.9 us
    pallas_call x1, Pallas kernels, run_widen(): pl.pallas_call(functools.partial(widen_kernel, rank, states, columns, par...  16.9 us

profile of v5, /device:TPU:0, one launch (start us, length us, event | category | flops | bytes accessed | tf_op | source)
XLA Modules:
  0.0 246.6 jit_solution(4350000832880907831)
XLA Ops:
  0.6 18.9 %span_front.1 = (f32[512,1024]{1,0:T(8,128)}, f32[512,1]{1,0:T(8,128)}, bf16[528,1024]{1,0:T(8,128)(2,1)}, bf16[1024,512]{1,0:T(8,128)(2,1)}, bf16[512,1024]{1,0...) custom-call(s32[1,512]{1,0:T(1,128)} %ids_ref.1, ...), custom_call_target="tpu_custom_call" | custom-call | tf_op jit(solution)/shard_map/span_front/pallas_call | solution.py:186
  19.6 122.9 %span_scan.1 = (bf16[512,2048]{1,0:T(8,128)(2,1)}, bf16[512,2048]{1,0:T(8,128)(2,1)}, bf16[512,2048]{1,0:T(8,128)(2,1)}, f32[512,2048]{1,0:T(8,128)}, f32[24,204...) custom-call(bf16[512,2048]{1,0:T(8,128)(2,1)} %get-tuple-element.55., ...), custom_call_target="tpu_custom_call" | custom-call | tf_op jit(solution)/shard_map/span_scan/pallas_call | solution.py:582
  142.5 87.1 %span_tail.1 = (bf16[512,1024]{1,0:T(8,128)(2,1)}, f32[512,1024]{1,0:T(8,128)}, bf16[1024,2048]{1,0:T(8,128)(2,1)}, bf16[1024,1024]{1,0:T(8,128)(2,1)}, bf16[128...) custom-call(bf16[512,2048]{1,0:T(8,128)(2,1)} %get-tuple-element.61.dprel, ...), custom_call_target="tpu_custom_call" | custom-call | tf_op jit(solution)/shard_map/span_tail/pallas_call | solution.py:1122
  229.6 16.9 %sums_to_float32.1 = (f32[1024,4096]{1,0:T(8,128)}, f32[2048,1024]{1,0:T(8,128)}, bf16[512,1024]{1,0:T(8,128)(2,1)}, f32[512,1024]{1,0:T(8,128)}, f32[256,1024]{...) custom-call(bf16[1024,2048]{1,0:T(8,128)(2,1)} %get-tuple-element.74, ...), custom_call_target="tpu_custom_call" | custom-call | tf_op jit(solution)/shard_map/sums_to_float32/pallas_call | solution.py:1268

commit v6 on v5

--- a/solution.py
+++ b/solution.py
@@ -372,8 +372,8 @@
         state_scr[0] = ahead_scr[tile] + jnp.exp2(before[None] * rate_scr[...]) * spread(start_scr[tile])
 
         def forward(i, state):
-            for u in range(unroll // 2):
-                j = i * (unroll // 2) + u
+            for u in range(unroll):
+                j = i * unroll + u
                 factor = jnp.exp2(delta_scr[j][None] * rate_scr[...])
                 factor_scr[j] = factor
                 state = factor * state + drive_scr[j][None] * inject_scr[j]
@@ -382,7 +382,7 @@
                 scan_scr[j] = tree_sum(readout_scr[j] * state)
             return state
 
-        lax.fori_loop(0, steps // (unroll // 2), forward, state_scr[0])
+        lax.fori_loop(0, steps // unroll, forward, state_scr[0])
         take_turns(0)
         lanes = pl.ds(pl.multiple_of(c * LANES, LANES), LANES)
         skip = skip_ref[:, lanes]
@@ -1259,7 +1259,7 @@
 ):
     width, inner = front.shape
     vocab = embedding.shape[0]
-    parts, slots = inner // (2 * LANES), 4
+    parts = slots = inner // (2 * LANES)
     hbm = pl.BlockSpec(memory_space=pltpu.HBM)
     shapes = [
         (width, 2 * inner), (inner, width), output.shape, d_inputs.shape, (vocab, width), (columns, inner), (rank, inner),

time: 247 us -> 246 us (level)
  no operation moved by 1% of the time
where the time goes in v6:
time: 246 us
  Pallas kernels  245 us (100%)
    pallas_call x1, Pallas kernels, run_scan(): pl.pallas_call(functools.partial(scan_kernel, rank, states, chunk, rounds...  122 us
    pallas_call x1, Pallas kernels, run_tail(): pl.pallas_call(functools.partial(tail_kernel, rank, states, chunk, seq),...  87 us
    pallas_call x1, Pallas kernels, run_front(): pl.pallas_call(functools.partial(front_kernel, seq), grid=(pairs,), in_sp...  18.9 us
    pallas_call x1, Pallas kernels, run_widen(): pl.pallas_call(functools.partial(widen_kernel, rank, states, columns, par...  17 us

profile of v6, /device:TPU:0, one launch (start us, length us, event | category | flops | bytes accessed | tf_op | source)
XLA Modules:
  0.0 246.1 jit_solution(9476145896488484869)
XLA Ops:
  0.6 18.9 %span_front.1 = (f32[512,1024]{1,0:T(8,128)}, f32[512,1]{1,0:T(8,128)}, bf16[528,1024]{1,0:T(8,128)(2,1)}, bf16[1024,512]{1,0:T(8,128)(2,1)}, bf16[512,1024]{1,0...) custom-call(s32[1,512]{1,0:T(1,128)} %ids_ref.1, ...), custom_call_target="tpu_custom_call" | custom-call | tf_op jit(solution)/shard_map/span_front/pallas_call | solution.py:186
  19.6 122.4 %span_scan.1 = (bf16[512,2048]{1,0:T(8,128)(2,1)}, bf16[512,2048]{1,0:T(8,128)(2,1)}, bf16[512,2048]{1,0:T(8,128)(2,1)}, f32[512,2048]{1,0:T(8,128)}, f32[24,204...) custom-call(bf16[512,2048]{1,0:T(8,128)(2,1)} %get-tuple-element.55., ...), custom_call_target="tpu_custom_call" | custom-call | tf_op jit(solution)/shard_map/span_scan/pallas_call | solution.py:582
  142.0 87.0 %span_tail.1 = (bf16[512,1024]{1,0:T(8,128)(2,1)}, f32[512,1024]{1,0:T(8,128)}, bf16[1024,2048]{1,0:T(8,128)(2,1)}, bf16[1024,1024]{1,0:T(8,128)(2,1)}, bf16[128...) custom-call(bf16[512,2048]{1,0:T(8,128)(2,1)} %get-tuple-element.61.dprel, ...), custom_call_target="tpu_custom_call" | custom-call | tf_op jit(solution)/shard_map/span_tail/pallas_call | solution.py:1122
  229.0 17.0 %sums_to_float32.1 = (f32[1024,4096]{1,0:T(8,128)}, f32[2048,1024]{1,0:T(8,128)}, bf16[512,1024]{1,0:T(8,128)(2,1)}, f32[512,1024]{1,0:T(8,128)}, f32[256,1024]{...) custom-call(bf16[1024,2048]{1,0:T(8,128)(2,1)} %get-tuple-element.74, ...), custom_call_target="tpu_custom_call" | custom-call | tf_op jit(solution)/shard_map/sums_to_float32/pallas_call | solution.py:1268
